TPU v7x, 32 devices: a whole 2x2x4 slice. The times are simulated.
32 devices in a mesh: wide: 8 (over y, x, core), narrow: 4 (over z).
Axes of the slice: x: 2, y: 2, z: 4, core: 2. Of those that a mesh axis runs over, the one named last changes fastest.
Arguments:
- corr_panel: float32 [4096, 512], P('wide', 'narrow'), may hold values from -24 to 24
- factor_prev: float32 [4096, 1024], P('wide', 'narrow'), may hold values from -400 to 400
- draws_prev: float32 [1024, 32], P('narrow'), may hold values from -6 to 6
- draws_panel: float32 [512, 32], P('narrow'), may hold values from -6 to 6
- diag_inverse: float32 [512, 512], P('narrow'), may hold values from -1 to 1, as said below
Outputs:
- panel_factor: float32 [4096, 512], P('wide', 'narrow')
- smoothed: float32 [32, 4096], P(('narrow', 'wide'))
Inputs may be any that keep to these rules, and one draw needn't show every extreme that they name: `diag_inverse`: lower triangular with a positive diagonal.
All inputs are finite; a program needn't handle non-finite values.
Results may differ from a plain program's by a relative error of at most 0.0003.
Values sent between devices are 32-bit elements; how exact they have to be, the bound alone decides.
No kernel may reach another device: no remote copies, remote signals or barrier semaphores. Data moves between devices by JAX's collectives and lax.ppermute only.
A program may use at most 64 MiB of HBM per device.

v0:
```python
import math

import jax
import jax.numpy as jnp
from jax import lax
from jax.sharding import PartitionSpec as P

PANEL = 512
ROWS_DEV = 512
WIN = 5
K = 1024


EXACT = lax.Precision.HIGHEST
HALF_ROOT = 1.0 / math.sqrt(2.0)


def broadcast(value, axis, source):
    kept = jnp.where(lax.axis_index(axis) == source, value, 0).astype(value.dtype)
    return lax.psum(kept, axis)


def contract(left_side, right_side, left_dim, right_dim):
    return lax.dot_general(
        left_side,
        right_side,
        (((left_dim,), (right_dim,)), ((), ())),
        precision=EXACT,
        preferred_element_type=jnp.float32,
    )


def smooth(uniforms):
    half_span = (WIN - 1) // 2
    feature_count = uniforms.shape[1]
    padded = jnp.pad(uniforms, ((0, 0), (half_span, half_span)))
    summed = jnp.zeros_like(uniforms)
    for offset in range(WIN):
        weight_tap = math.comb(WIN - 1, offset) / 2.0 ** (WIN - 1)
        summed = summed + weight_tap * padded[:, offset : offset + feature_count]
    return summed


def per_device(corr_panel, factor_prev, draws_prev, draws_panel, diag_inverse):
    row_count = factor_prev.shape[0]
    col_share = corr_panel.shape[1]
    narrow_place = lax.axis_index("narrow")
    pivot_block = broadcast(factor_prev, "wide", K // ROWS_DEV)
    update_part = contract(factor_prev, pivot_block, 1, 1)
    sample_part = contract(draws_prev, factor_prev, 0, 1)
    placed = lax.dynamic_update_slice_in_dim(
        jnp.zeros((row_count, PANEL), jnp.float32), corr_panel, narrow_place * col_share, 1
    )
    updated = lax.psum(placed - update_part, "narrow")
    sample_sum = lax.psum_scatter(sample_part, "narrow", scatter_dimension=0, tiled=True)
    panel_factor = contract(updated, diag_inverse, 1, 1)
    panel_part = contract(draws_panel, panel_factor, 0, 1)
    samples = sample_sum + lax.psum_scatter(panel_part, "narrow", scatter_dimension=0, tiled=True)
    own_squares = jnp.sum(factor_prev * factor_prev, axis=1) + jnp.sum(
        panel_factor * panel_factor, axis=1
    )
    variance = lax.psum(own_squares, "narrow")
    scaled = samples * lax.rsqrt(variance + 1e-06)[None, :]
    uniforms = 0.5 * (1.0 + lax.erf(scaled * HALF_ROOT))
    regrouped = lax.all_to_all(uniforms, "wide", split_axis=0, concat_axis=1, tiled=True)
    return (panel_factor, smooth(regrouped))


def solution(mesh):
    in_specs = (
        P("wide", "narrow"),
        P("wide", "narrow"),
        P("narrow", None),
        P("narrow", None),
        P("narrow", None),
    )
    out_specs = (P("wide", "narrow"), P(("narrow", "wide"), None))
    return jax.shard_map(
        per_device, mesh=mesh, in_specs=in_specs, out_specs=out_specs, check_vma=False
    )
```

profile of v0, /device:TPU:0, one launch (start us, length us, event | category | flops | bytes accessed | tf_op | source)
XLA Modules:
  0.0 170.7 jit_solution(10080647219116251030)
XLA Ops:
  7.2 0.0 all-reduce.4.cloned.1.call-start
  7.2 1.9 %multiply_reduce_fusion = (f32[512]{0:T(512)S(1)}, f32[512,256]{1,0:T(8,128)}) fusion(f32[512,256]{1,0:T(8,128)} %param.6, pred[]{:T(512)S(6)} %eq.3), kind=kLoop, calls=%fused_computation.4 | loop fusion | flops 392704 | bytes 1050625 | tf_op jit(solution)/shard_map/reduce_sum | solution.py:59
  9.1 0.0 all-reduce.4.cloned.1.call-update
  9.2 0.0 all-reduce.6.cloned.1.call-start
  9.2 0.1 broadcast_in_dim.8
  9.3 0.8 copy-done.2
  10.2 58.2 %all-reduce.4.cloned.1.call-done = f32[512,256]{1,0:T(8,128)} async-done(((f32[512,256]{1,0:T(8,128)}), f32[512,256]{1,0:T(8,128)}) %all-reduce.4.cloned.1.call-update) | async-done | bytes 524304 | tf_op jit(solution)/shard_map/psum | solution.py:20
  68.4 3.1 %fusion = f32[512,512]{1,0:T(8,128)} fusion(f32[512,512]{1,0:T(8,128)S(1)} %constant_dynamic-update-slice_fusion, f32[512,256]{1,0:T(8,128)} %all-reduce.4.cloned.1.call-done, f32[512,256]{1,0:T(8,128)S(1)} %copy-done.1), kind=kOutput, calls=%fused_computation.1 | convolution fusion | flops 805568512 | bytes 3145728 | tf_op jit(solution)/shard_map/dot_general | solution.py:24
  71.5 0.0 all-reduce.6.cloned.1.call-update
  71.5 0.0 reduce-scatter.2.cloned.1.call-start
  71.5 0.7 copy-done.3
  72.2 0.6 fusion.3
  72.8 50.0 %all-reduce.6.cloned.1.call-done = f32[512,512]{1,0:T(8,128)} async-done(((f32[512,512]{1,0:T(8,128)}), f32[512,512]{1,0:T(8,128)}) %all-reduce.6.cloned.1.call-update) | async-done | bytes 1048592 | tf_op jit(solution)/shard_map/psum | solution.py:54
  122.8 2.4 %multiply_reduce_fusion.1 = (f32[512]{0:T(512)S(1)}, f32[512,128]{0,1:T(8,128)S(1)}) fusion(f32[512,512]{1,0:T(8,128)} %all-reduce.6.cloned.1.call-done, f32[128,512]{1,0:T(8,128)S(1)} %copy-done), kind=kOutput, calls=%fused_computation.5 | convolution fusion | flops 402783744 | bytes 1574912 | tf_op jit(solution)/shard_map/dot_general | solution.py:24
  125.2 10.2 %psum.23 = f32[512]{0:T(512)S(1)} all-reduce(f32[512]{0:T(512)S(1)} %add.47), channel_id=1, replica_groups=mesh['wide'=8,'narrow'=4] {'narrow'}, use_global_device_ids=true, to_apply=%region_6.7 | all-reduce | flops 512 | bytes 4096 | tf_op jit(solution)/shard_map/psum | solution.py:62
  135.5 0.9 fusion.1
  136.4 0.0 reduce-scatter.2.cloned.1.call-update
  136.4 17.2 %reduce-scatter.2.cloned.1.call-done = f32[8,512]{1,0:T(8,128)} async-done(((f32[32,512]{1,0:T(8,128)}), f32[8,512]{1,0:T(8,128)}) %reduce-scatter.2.cloned.1.call-update) | async-done | bytes 16400 | tf_op jit(solution)/shard_map/reduce_scatter | solution.py:55
  153.6 0.7 multiply_bitcast_fusion
  154.3 0.6 copy.8
  154.9 3.7 %all-to-all-start = ((f32[8,1,512]{2,1,0:T(1,128)}), f32[8,1,512]{2,1,0:T(1,128)S(1)}, u32[]{:S(2)}, u32[]{:S(2)}) async-start(f32[8,1,512]{2,1,0:T(1,128)} %copy.8), calls=%async_computation | async-start | bytes 32768 | tf_op jit(solution)/shard_map/all_to_all | solution.py:65
  158.6 0.8 copy.9
  159.5 3.9 %all-to-all-done = f32[8,1,512]{2,1,0:T(1,128)S(1)} async-done(((f32[8,1,512]{2,1,0:T(1,128)}), f32[8,1,512]{2,1,0:T(1,128)S(1)}, u32[]{:S(2)}, u32[]{:S(2)}) %all-to-all-start) | async-done | bytes 16416 | tf_op jit(solution)/shard_map/all_to_all | solution.py:65
  163.4 0.8 multiply_add_fusion
  (11 shorter events, 0.1 us)
Async XLA Ops:
  7.2 115.6 %copy-start = (f32[128,512]{1,0:T(8,128)S(1)}, f32[128,512]{1,0:T(8,128)}, u32[]{:S(2)}) copy-start(f32[128,512]{1,0:T(8,128)} %param.9) | copy-start | bytes 786436
  7.2 61.2 %all-reduce.4.cloned.1.call-start = ((), (), s32[]{:S(2)}) async-start(), calls=%async_computation.2 | async-start | bytes 1048576 | tf_op jit(solution)/shard_map/psum | solution.py:20
  9.2 113.6 %all-reduce.6.cloned.1.call-start = ((), (), s32[]{:S(2)}) async-start(), calls=%async_computation.3 | async-start | bytes 2097152 | tf_op jit(solution)/shard_map/psum | solution.py:54
  9.2 1.0 copy-start.2
  10.2 58.2 %copy-start.1 = (f32[512,256]{1,0:T(8,128)S(1)}, f32[512,256]{1,0:T(8,128)}, u32[]{:S(2)}) copy-start(f32[512,256]{1,0:T(8,128)} %param.6) | copy-start | bytes 1572868
  71.5 0.8 copy-start.3
  71.5 82.1 %reduce-scatter.2.cloned.1.call-start = ((), (), s32[]{:S(2)}) async-start(), calls=%async_computation.4 | async-start | bytes 81920 | tf_op jit(solution)/shard_map/reduce_scatter | solution.py:55
  122.8 12.7 %copy-start.4 = (f32[128,32]{0,1:T(8,128)S(1)}, f32[128,32]{0,1:T(8,128)}, u32[]{:S(2)}) copy-start(f32[128,32]{0,1:T(8,128)} %param.8) | copy-start | bytes 49156
  154.9 8.5 %all-to-all-start = ((f32[8,1,512]{2,1,0:T(1,128)}), f32[8,1,512]{2,1,0:T(1,128)S(1)}, u32[]{:S(2)}, u32[]{:S(2)}) async-start(f32[8,1,512]{2,1,0:T(1,128)} %copy.8), calls=%async_computation | async-start | bytes 32768 | tf_op jit(solution)/shard_map/all_to_all | solution.py:65
Sparse Core Ops, SparseCore 0:
  11.1 57.2 all-reduce.3
  71.6 51.1 all-reduce.5
  136.5 17.0 reduce-scatter.1
where the time goes:
time: 171 us
  waiting for transfers between devices  129 us (75%)
  between operations  13.8 us (8%)
  blocking collectives  10.2 us (6%)
  matrix products  6.99 us (4%)
  starting transfers between devices  3.84 us (2%)
  other arithmetic  3.45 us (2%)
  local copies, waits for them, and re-layouts  3.12 us (2%)
    psum x1, waiting for transfers between devices, broadcast(): return lax.psum(kept, axis)  58.2 us
    psum x1, waiting for transfers between devices, per_device(): updated = lax.psum(placed - update_part, 'narrow')  50 us
    reduce_scatter x1, waiting for transfers between devices, per_device(): lax.psum_scatter(sample_part, 'narrow', scatter_dimension=0, tiled=True)  17.2 us
    psum x1, blocking collectives, per_device(): variance = lax.psum(own_squares, 'narrow')  10.2 us
    dot_general x4, matrix products, contract(): lax.dot_general(left_side, right_side, (((left_dim,), (right_dim,)), ((),...  6.99 us
    all_to_all x1, waiting for transfers between devices, per_device(): lax.all_to_all(uniforms, 'wide', split_axis=0, concat_axis=1, tiled=True)  3.92 us
    all_to_all x1, starting transfers between devices, per_device(): lax.all_to_all(uniforms, 'wide', split_axis=0, concat_axis=1, tiled=True)  3.72 us
  transfers between devices with their start and end apart: 4, of which 4 were waited for; matrix products, arithmetic and copies ran while one was open for 1% of the time, Pallas kernels for 0%

commit v1 on v0

v1 whole, which is shorter than its diff:
```python
import math

import jax
import jax.numpy as jnp
from jax import lax
from jax.sharding import PartitionSpec as P

WIN = 5
PRECISE = lax.Precision.HIGH
HALF_ROOT = 1.0 / math.sqrt(2.0)


def contract(left_side, right_side, left_dim, right_dim):
    return lax.dot_general(
        left_side,
        right_side,
        (((left_dim,), (right_dim,)), ((), ())),
        precision=PRECISE,
        preferred_element_type=jnp.float32,
    )


def broadcast(value, size, source):
    place = lax.axis_index("wide")
    holders = [source]
    held = jnp.where(place == source, value, 0.0)
    shift = 1
    while (1 << shift) < size:
        flips = [f << shift for f in (1, 2, 3) if (f << shift) < size]
        arrived = [lax.ppermute(held, "wide", [(h, h ^ f) for h in holders]) for f in flips]
        for block in arrived:
            held = held + block
        holders = holders + [h ^ f for h in holders for f in flips]
        shift += 2
    other = lax.ppermute(held, "wide", [(h, h ^ 1) for h in holders])
    return held + other


def smooth(uniforms):
    half_span = (WIN - 1) // 2
    feature_count = uniforms.shape[1]
    padded = jnp.pad(uniforms, ((0, 0), (half_span, half_span)))
    summed = jnp.zeros_like(uniforms)
    for offset in range(WIN):
        weight_tap = math.comb(WIN - 1, offset) / 2.0 ** (WIN - 1)
        summed = summed + weight_tap * padded[:, offset : offset + feature_count]
    return summed


def per_device(wide, narrow, corr_panel, factor_prev, draws_prev, draws_panel, diag_inverse):
    row_count, depth = factor_prev.shape
    col_share = corr_panel.shape[1]
    narrow_place = lax.axis_index("narrow")

    pivot = broadcast(factor_prev, wide, depth * narrow // row_count)
    diag = [diag_inverse] + [
        lax.ppermute(diag_inverse, "narrow", [(i, (i + k) % narrow) for i in range(narrow)])
        for k in range(1, narrow)
    ]

    parts = []
    for rows in diag:
        mixed = contract(rows, pivot, 1, 0)
        own_cols = lax.dynamic_slice_in_dim(rows, narrow_place * col_share, col_share, 1)
        parts.append(contract(corr_panel, own_cols, 1, 1) - contract(factor_prev, mixed, 1, 1))
    panel_factor = parts[0]
    for k in range(1, narrow):
        panel_factor = panel_factor + lax.ppermute(
            parts[k], "narrow", [(i, (i - k) % narrow) for i in range(narrow)]
        )

    samples = contract(draws_prev, factor_prev, 0, 1) + contract(draws_panel, panel_factor, 0, 1)
    squares = jnp.sum(factor_prev * factor_prev, axis=1) + jnp.sum(panel_factor * panel_factor, axis=1)
    outgoing = jnp.stack([samples, jnp.broadcast_to(squares[None, :], samples.shape)], axis=1)
    incoming = lax.all_to_all(outgoing, ("narrow", "wide"), split_axis=0, concat_axis=0, tiled=True)
    whole = jnp.sum(incoming.reshape(narrow, wide, 2, row_count), axis=0)
    scaled = whole[:, 0] * lax.rsqrt(whole[:, 1] + 1e-06)
    uniforms = 0.5 * (1.0 + lax.erf(scaled * HALF_ROOT))
    return (panel_factor, smooth(uniforms.reshape(1, wide * row_count)))


def solution(mesh):
    wide, narrow = mesh.shape["wide"], mesh.shape["narrow"]
    in_specs = (
        P("wide", "narrow"),
        P("wide", "narrow"),
        P("narrow", None),
        P("narrow", None),
        P("narrow", None),
    )
    out_specs = (P("wide", "narrow"), P(("narrow", "wide"), None))

    def body(*blocks):
        return per_device(wide, narrow, *blocks)

    return jax.shard_map(body, mesh=mesh, in_specs=in_specs, out_specs=out_specs, check_vma=False)
```

time: 171 us -> 78.2 us (0.46)
  waiting for transfers between devices: 129 us -> 31.4 us
  starting transfers between devices: 3.84 us -> 34.5 us
  between operations: 13.8 us -> 0.93 us
  blocking collectives: 10.2 us -> 0 us
    psum x2 -> x0, waiting for transfers between devices: 108 us -> none  [the longest x1 58.2 us: broadcast(): return lax.psum(kept, axis)]
    ppermute x0 -> x10, starting transfers between devices: none -> 24.2 us  [the longest x3 13.2 us: per_device(): lax.ppermute(parts[k], 'narrow', [(i, (i - k) % narrow) for i in range(na...]
    ppermute x0 -> x10, waiting for transfers between devices: none -> 24 us  [the longest x3 11.2 us: per_device(): lax.ppermute(diag_inverse, 'narrow', [(i, (i + k) % narrow) for i in rang...]
    reduce_scatter x1 -> x0, waiting for transfers between devices: 17.2 us -> none  [per_device(): lax.psum_scatter(sample_part, 'narrow', scatter_dimension=0, tiled=True)]
    psum x1 -> x0, blocking collectives: 10.2 us -> none  [per_device(): variance = lax.psum(own_squares, 'narrow')]
    all_to_all x1, starting transfers between devices: 3.72 us -> 10.4 us  [per_device(): lax.all_to_all(outgoing, ('narrow', 'wide'), split_axis=0, concat_axis=0,...]
    all_to_all x1, waiting for transfers between devices: 3.92 us -> 7.39 us  [per_device(): lax.all_to_all(outgoing, ('narrow', 'wide'), split_axis=0, concat_axis=0,...]
    dot_general x4 -> x14, matrix products: 6.99 us -> 5.81 us  [contract(): lax.dot_general(left_side, right_side, (((left_dim,), (right_dim,)), ((),...]
  transfers between devices with their start and end apart: 4 -> 11, of which waited for: 4 -> 5; matrix products, arithmetic and copies ran while one was open for 1% -> 8% of each run, Pallas kernels for 0% -> 0%
where the time goes in v1:
time: 78.2 us; the launch traced here: 77.8 us
  starting transfers between devices  34.5 us (44%)
  waiting for transfers between devices  31.4 us (40%)
  matrix products  5.81 us (7%)
  local copies, waits for them, and re-layouts  2.74 us (4%)
  other arithmetic  2.45 us (3%)
  between operations  0.93 us (1%)
    ppermute x3, starting transfers between devices, per_device(): lax.ppermute(parts[k], 'narrow', [(i, (i - k) % narrow) for i in range(na...  13.2 us
    ppermute x3, waiting for transfers between devices, per_device(): lax.ppermute(diag_inverse, 'narrow', [(i, (i + k) % narrow) for i in rang...  11.2 us
    all_to_all x1, starting transfers between devices, per_device(): lax.all_to_all(outgoing, ('narrow', 'wide'), split_axis=0, concat_axis=0,...  10.4 us
    ppermute x3, waiting for transfers between devices, broadcast(): lax.ppermute(held, 'wide', [(h, h ^ f) for h in holders])  8.67 us
    all_to_all x1, waiting for transfers between devices, per_device(): lax.all_to_all(outgoing, ('narrow', 'wide'), split_axis=0, concat_axis=0,...  7.39 us
    ppermute x3, starting transfers between devices, per_device(): lax.ppermute(diag_inverse, 'narrow', [(i, (i + k) % narrow) for i in rang...  6.72 us
    dot_general x14, matrix products, contract(): lax.dot_general(left_side, right_side, (((left_dim,), (right_dim,)), ((),...  5.81 us
    ppermute x3, waiting for transfers between devices, per_device(): lax.ppermute(parts[k], 'narrow', [(i, (i - k) % narrow) for i in range(na...  4.12 us
  transfers between devices with their start and end apart: 11, of which 5 were waited for; matrix products, arithmetic and copies ran while one was open for 8% of the time, Pallas kernels for 0%

profile of v1, /device:TPU:0, one launch (start us, length us, event | category | flops | bytes accessed | tf_op | source)
XLA Modules:
  0.0 77.8 jit_solution(15487883941354939779)
XLA Ops:
  0.7 1.2 %multiply_reduce_fusion = (f32[512]{0:T(512)S(1)}, f32[512,256]{1,0:T(8,128)S(1)}) fusion(f32[512,256]{1,0:T(8,128)} %param.6, pred[]{:T(512)S(6)} %eq.3), kind=kLoop, calls=%fused_computation.11 | loop fusion | flops 392704 | bytes 1050625 | tf_op jit(solution)/shard_map/reduce_sum | solution.py:73
  1.9 1.4 %collective-permute-start = (f32[512,256]{1,0:T(8,128)S(1)}, f32[512,256]{1,0:T(8,128)S(1)}, u32[]{:S(2)}, u32[]{:S(2)}) collective-permute-start(f32[512,256]{1,0:T(8,128)S(1)} %get-tuple-element.15), channel_id=1, source_target_pairs={{8,0},{9,1},{10,2},{11,3}} | collective-permute-start | bytes 1572872 | tf_op jit(solution)/shard_map/ppermute | solution.py:30
  3.3 0.7 collective-permute-start.1
  4.0 0.7 collective-permute-start.2
  4.7 8.7 %collective-permute-done = f32[512,256]{1,0:T(8,128)S(1)} collective-permute-done((f32[512,256]{1,0:T(8,128)S(1)}, f32[512,256]{1,0:T(8,128)S(1)}, u32[]{:S(2)}, u32[]{:S(2)}) %collective-permute-start) | collective-permute-done | bytes 524320 | tf_op jit(solution)/shard_map/ppermute | solution.py:30
  13.6 1.5 %collective-permute-start.3 = (f32[512,256]{1,0:T(8,128)S(1)}, f32[512,256]{1,0:T(8,128)S(1)}, u32[]{:S(2)}, u32[]{:S(2)}) collective-permute-start(f32[512,256]{1,0:T(8,128)S(1)} %add_add_fusion), channel_id=1, source_target_pairs={{8,12},{0,4},{24,28},{16,20},{9,13},{1,5},{25,29},{17,21},{10,14},... | collective-permute-start | bytes 1572872 | tf_op jit(solution)/shard_map/ppermute | solution.py:35
  15.0 2.8 %collective-permute-start.4 = (f32[128,512]{1,0:T(8,128)S(1)}, f32[128,512]{1,0:T(8,128)S(1)}, u32[]{:S(2)}, u32[]{:S(2)}) collective-permute-start(f32[128,512]{1,0:T(8,128)S(1)} %copy-done.2), channel_id=1, source_target_pairs={{0,1},{1,2},{2,3},{3,0},{4,5},{5,6},{6,7},{7,4},{8,9},{9,10},{10,1... | collective-permute-start | bytes 786440 | tf_op jit(solution)/shard_map/ppermute | solution.py:57
  17.8 2.6 %collective-permute-start.6 = (f32[128,512]{1,0:T(8,128)S(1)}, f32[128,512]{1,0:T(8,128)S(1)}, u32[]{:S(2)}, u32[]{:S(2)}) collective-permute-start(f32[128,512]{1,0:T(8,128)S(1)} %copy-done.2), channel_id=1, source_target_pairs={{0,2},{1,3},{2,0},{3,1},{4,6},{5,7},{6,4},{7,5},{8,10},{9,11},{10,... | collective-permute-start | bytes 786440 | tf_op jit(solution)/shard_map/ppermute | solution.py:57
  20.4 1.3 %collective-permute-start.8 = (f32[128,512]{1,0:T(8,128)S(1)}, f32[128,512]{1,0:T(8,128)S(1)}, u32[]{:S(2)}, u32[]{:S(2)}) collective-permute-start(f32[128,512]{1,0:T(8,128)S(1)} %copy-done.2), channel_id=1, source_target_pairs={{0,3},{1,0},{2,1},{3,2},{4,7},{5,4},{6,5},{7,6},{8,11},{9,8},{10,9... | collective-permute-start | bytes 786440 | tf_op jit(solution)/shard_map/ppermute | solution.py:57
  23.0 1.4 %collective-permute-done.4 = f32[128,512]{1,0:T(8,128)S(1)} collective-permute-done((f32[128,512]{1,0:T(8,128)S(1)}, f32[128,512]{1,0:T(8,128)S(1)}, u32[]{:S(2)}, u32[]{:S(2)}) %collective-permute-start.4) | collective-permute-done | bytes 262176 | tf_op jit(solution)/shard_map/ppermute | solution.py:57
  24.4 0.6 fusion.23
  25.7 2.9 %collective-permute-start.5 = (f32[512,128]{0,1:T(8,128)S(1)}, f32[512,128]{0,1:T(8,128)S(1)}, u32[]{:S(2)}, u32[]{:S(2)}) collective-permute-start(f32[512,128]{0,1:T(8,128)S(1)} %fusion.2), channel_id=1, source_target_pairs={{0,3},{1,0},{2,1},{3,2},{4,7},{5,4},{6,5},{7,6},{8,11},{9,8},{10,9... | collective-permute-start | bytes 786440 | tf_op jit(solution)/shard_map/ppermute | solution.py:68
  28.6 9.7 %collective-permute-done.6 = f32[128,512]{1,0:T(8,128)S(1)} collective-permute-done((f32[128,512]{1,0:T(8,128)S(1)}, f32[128,512]{1,0:T(8,128)S(1)}, u32[]{:S(2)}, u32[]{:S(2)}) %collective-permute-start.6) | collective-permute-done | bytes 262176 | tf_op jit(solution)/shard_map/ppermute | solution.py:57
  39.7 4.5 %collective-permute-start.7 = (f32[512,128]{0,1:T(8,128)S(1)}, f32[512,128]{0,1:T(8,128)S(1)}, u32[]{:S(2)}, u32[]{:S(2)}) collective-permute-start(f32[512,128]{0,1:T(8,128)S(1)} %fusion.1), channel_id=1, source_target_pairs={{0,2},{1,3},{2,0},{3,1},{4,6},{5,7},{6,4},{7,5},{8,10},{9,11},{10,... | collective-permute-start | bytes 786440 | tf_op jit(solution)/shard_map/ppermute | solution.py:68
  44.3 0.6 fusion.27
  45.6 5.7 %collective-permute-start.9 = (f32[512,128]{0,1:T(8,128)S(1)}, f32[512,128]{0,1:T(8,128)S(1)}, u32[]{:S(2)}, u32[]{:S(2)}) collective-permute-start(f32[512,128]{0,1:T(8,128)S(1)} %fusion), channel_id=1, source_target_pairs={{0,1},{1,2},{2,3},{3,0},{4,5},{5,6},{6,7},{7,4},{8,9},{9,10},{10,1... | collective-permute-start | bytes 786440 | tf_op jit(solution)/shard_map/ppermute | solution.py:68
  51.3 0.6 fusion.22
  52.4 4.1 %collective-permute-done.9 = f32[512,128]{0,1:T(8,128)S(1)} collective-permute-done((f32[512,128]{0,1:T(8,128)S(1)}, f32[512,128]{0,1:T(8,128)S(1)}, u32[]{:S(2)}, u32[]{:S(2)}) %collective-permute-start.9) | collective-permute-done | bytes 262176 | tf_op jit(solution)/shard_map/ppermute | solution.py:68
  56.7 0.6 copy-done.4
  57.5 0.8 copy.12
  58.2 10.4 %all-to-all-start = ((f32[32,2,512]{2,1,0:T(2,128)}), f32[32,2,512]{2,1,0:T(2,128)S(1)}, u32[]{:S(2)}, u32[]{:S(2)}) async-start(f32[32,2,512]{2,1,0:T(2,128)} %copy.12), calls=%async_computation | async-start | bytes 262144 | tf_op jit(solution)/shard_map/all_to_all | solution.py:75
  68.6 0.8 %copy.15 = f32[512,128]{1,0:T(8,128)} copy(f32[512,128]{0,1:T(8,128)S(1)} %get-tuple-element.13) | data formatting | bytes 524288
  69.4 7.4 %all-to-all-done = f32[32,2,512]{2,1,0:T(2,128)S(1)} async-done(((f32[32,2,512]{2,1,0:T(2,128)}), f32[32,2,512]{2,1,0:T(2,128)S(1)}, u32[]{:S(2)}, u32[]{:S(2)}) %all-to-all-start) | async-done | bytes 131104 | tf_op jit(solution)/shard_map/all_to_all | solution.py:75
  77.0 0.8 %multiply_add_fusion = f32[1,4096]{1,0:T(1,128)} fusion(f32[1,4096]{1,0:T(1,128)S(1)} %bitcast.50, f32[1,4096]{1,0:T(1,128)S(1)} %bitcast.51), kind=kLoop, calls=%fused_computation.29 | loop fusion | flops 32768 | bytes 49152 | tf_op jit(solution)/shard_map/add | solution.py:46
  (38 shorter events, 5.0 us)
Async XLA Ops:
  0.6 21.1 %copy-start = (f32[512,128]{1,0:T(8,128)S(1)}, f32[512,128]{1,0:T(8,128)}, u32[]{:S(2)}) copy-start(f32[512,128]{1,0:T(8,128)} %param.5) | copy-start | bytes 786436
  1.9 13.1 %copy-start.2 = (f32[128,512]{1,0:T(8,128)S(1)}, f32[128,512]{1,0:T(8,128)}, u32[]{:S(2)}) copy-start(f32[128,512]{1,0:T(8,128)} %param.9) | copy-start | bytes 786436
  1.9 11.5 %collective-permute-start = (f32[512,256]{1,0:T(8,128)S(1)}, f32[512,256]{1,0:T(8,128)S(1)}, u32[]{:S(2)}, u32[]{:S(2)}) collective-permute-start(f32[512,256]{1,0:T(8,128)S(1)} %get-tuple-element.15), channel_id=1, source_target_pairs={{8,0},{9,1},{10,2},{11,3}} | collective-permute-start | bytes 1572872 | tf_op jit(solution)/shard_map/ppermute | solution.py:30
  3.3 10.1 %collective-permute-start.1 = (f32[512,256]{1,0:T(8,128)S(1)}, f32[512,256]{1,0:T(8,128)S(1)}, u32[]{:S(2)}, u32[]{:S(2)}) collective-permute-start(f32[512,256]{1,0:T(8,128)S(1)} %get-tuple-element.15), channel_id=1, source_target_pairs={{8,24},{9,25},{10,26},{11,27}} | collective-permute-start | bytes 1572872 | tf_op jit(solution)/shard_map/ppermute | solution.py:30
  4.0 9.4 %collective-permute-start.2 = (f32[512,256]{1,0:T(8,128)S(1)}, f32[512,256]{1,0:T(8,128)S(1)}, u32[]{:S(2)}, u32[]{:S(2)}) collective-permute-start(f32[512,256]{1,0:T(8,128)S(1)} %get-tuple-element.15), channel_id=1, source_target_pairs={{8,16},{9,17},{10,18},{11,19}} | collective-permute-start | bytes 1572872 | tf_op jit(solution)/shard_map/ppermute | solution.py:30
  13.5 8.5 %copy-start.1 = (f32[512,256]{1,0:T(8,128)S(1)}, f32[512,256]{1,0:T(8,128)}, u32[]{:S(2)}) copy-start(f32[512,256]{1,0:T(8,128)} %param.6) | copy-start | bytes 1572868
  13.6 9.3 %collective-permute-start.3 = (f32[512,256]{1,0:T(8,128)S(1)}, f32[512,256]{1,0:T(8,128)S(1)}, u32[]{:S(2)}, u32[]{:S(2)}) collective-permute-start(f32[512,256]{1,0:T(8,128)S(1)} %add_add_fusion), channel_id=1, source_target_pairs={{8,12},{0,4},{24,28},{16,20},{9,13},{1,5},{25,29},{17,21},{10,14},... | collective-permute-start | bytes 1572872 | tf_op jit(solution)/shard_map/ppermute | solution.py:35
  15.0 9.4 %collective-permute-start.4 = (f32[128,512]{1,0:T(8,128)S(1)}, f32[128,512]{1,0:T(8,128)S(1)}, u32[]{:S(2)}, u32[]{:S(2)}) collective-permute-start(f32[128,512]{1,0:T(8,128)S(1)} %copy-done.2), channel_id=1, source_target_pairs={{0,1},{1,2},{2,3},{3,0},{4,5},{5,6},{6,7},{7,4},{8,9},{9,10},{10,1... | collective-permute-start | bytes 786440 | tf_op jit(solution)/shard_map/ppermute | solution.py:57
  17.8 20.6 %collective-permute-start.6 = (f32[128,512]{1,0:T(8,128)S(1)}, f32[128,512]{1,0:T(8,128)S(1)}, u32[]{:S(2)}, u32[]{:S(2)}) collective-permute-start(f32[128,512]{1,0:T(8,128)S(1)} %copy-done.2), channel_id=1, source_target_pairs={{0,2},{1,3},{2,0},{3,1},{4,6},{5,7},{6,4},{7,5},{8,10},{9,11},{10,... | collective-permute-start | bytes 786440 | tf_op jit(solution)/shard_map/ppermute | solution.py:57
  20.4 23.9 %collective-permute-start.8 = (f32[128,512]{1,0:T(8,128)S(1)}, f32[128,512]{1,0:T(8,128)S(1)}, u32[]{:S(2)}, u32[]{:S(2)}) collective-permute-start(f32[128,512]{1,0:T(8,128)S(1)} %copy-done.2), channel_id=1, source_target_pairs={{0,3},{1,0},{2,1},{3,2},{4,7},{5,4},{6,5},{7,6},{8,11},{9,8},{10,9... | collective-permute-start | bytes 786440 | tf_op jit(solution)/shard_map/ppermute | solution.py:57
  21.8 0.8 copy-start.3
  25.7 26.7 %collective-permute-start.5 = (f32[512,128]{0,1:T(8,128)S(1)}, f32[512,128]{0,1:T(8,128)S(1)}, u32[]{:S(2)}, u32[]{:S(2)}) collective-permute-start(f32[512,128]{0,1:T(8,128)S(1)} %fusion.2), channel_id=1, source_target_pairs={{0,3},{1,0},{2,1},{3,2},{4,7},{5,4},{6,5},{7,6},{8,11},{9,8},{10,9... | collective-permute-start | bytes 786440 | tf_op jit(solution)/shard_map/ppermute | solution.py:68
  39.7 12.7 %collective-permute-start.7 = (f32[512,128]{0,1:T(8,128)S(1)}, f32[512,128]{0,1:T(8,128)S(1)}, u32[]{:S(2)}, u32[]{:S(2)}) collective-permute-start(f32[512,128]{0,1:T(8,128)S(1)} %fusion.1), channel_id=1, source_target_pairs={{0,2},{1,3},{2,0},{3,1},{4,6},{5,7},{6,4},{7,5},{8,10},{9,11},{10,... | collective-permute-start | bytes 786440 | tf_op jit(solution)/shard_map/ppermute | solution.py:68
  45.6 10.9 %collective-permute-start.9 = (f32[512,128]{0,1:T(8,128)S(1)}, f32[512,128]{0,1:T(8,128)S(1)}, u32[]{:S(2)}, u32[]{:S(2)}) collective-permute-start(f32[512,128]{0,1:T(8,128)S(1)} %fusion), channel_id=1, source_target_pairs={{0,1},{1,2},{2,3},{3,0},{4,5},{5,6},{6,7},{7,4},{8,9},{9,10},{10,1... | collective-permute-start | bytes 786440 | tf_op jit(solution)/shard_map/ppermute | solution.py:68
  56.5 0.7 copy-start.4
  58.2 18.6 %all-to-all-start = ((f32[32,2,512]{2,1,0:T(2,128)}), f32[32,2,512]{2,1,0:T(2,128)S(1)}, u32[]{:S(2)}, u32[]{:S(2)}) async-start(f32[32,2,512]{2,1,0:T(2,128)} %copy.12), calls=%async_computation | async-start | bytes 262144 | tf_op jit(solution)/shard_map/all_to_all | solution.py:75

commit v2 on v1

--- a/solution.py
+++ b/solution.py
@@ -32,8 +32,7 @@
             held = held + block
         holders = holders + [h ^ f for h in holders for f in flips]
         shift += 2
-    other = lax.ppermute(held, "wide", [(h, h ^ 1) for h in holders])
-    return held + other
+    return held, holders
 
 
 def smooth(uniforms):
@@ -50,33 +49,58 @@
 def per_device(wide, narrow, corr_panel, factor_prev, draws_prev, draws_panel, diag_inverse):
     row_count, depth = factor_prev.shape
     col_share = corr_panel.shape[1]
-    narrow_place = lax.axis_index("narrow")
+    half = diag_inverse.shape[0] // 2
+    wide_place, narrow_place = lax.axis_index("wide"), lax.axis_index("narrow")
+    core = wide_place % 2
+    swap = [(i, i ^ 1) for i in range(wide)]
 
-    pivot = broadcast(factor_prev, wide, depth * narrow // row_count)
-    diag = [diag_inverse] + [
-        lax.ppermute(diag_inverse, "narrow", [(i, (i + k) % narrow) for i in range(narrow)])
-        for k in range(1, narrow)
-    ]
+    def below(value, k):
+        return lax.ppermute(value, "narrow", [(i, (i - k) % narrow) for i in range(narrow)])
 
-    parts = []
-    for rows in diag:
-        mixed = contract(rows, pivot, 1, 0)
-        own_cols = lax.dynamic_slice_in_dim(rows, narrow_place * col_share, col_share, 1)
-        parts.append(contract(corr_panel, own_cols, 1, 1) - contract(factor_prev, mixed, 1, 1))
-    panel_factor = parts[0]
-    for k in range(1, narrow):
-        panel_factor = panel_factor + lax.ppermute(
-            parts[k], "narrow", [(i, (i - k) % narrow) for i in range(narrow)]
-        )
+    def above(value, k):
+        return lax.ppermute(value, "narrow", [(i, (i + k) % narrow) for i in range(narrow)])
+
+    held, holders = broadcast(factor_prev, wide, depth * narrow // row_count)
+    own_half = lax.dynamic_slice_in_dim(diag_inverse, core * half, half, 0)
+    halves = [above(own_half, k) for k in range(1, narrow)]
+    held, *halves = lax.optimization_barrier((held, *halves))
+    pivot = held + lax.ppermute(held, "wide", [(h, h ^ 1) for h in holders])
+    mine = jnp.stack(halves)
+    other = lax.ppermute(mine, "wide", swap)
+    fetched = jnp.where(core == 0, jnp.concatenate([mine, other], 1), jnp.concatenate([other, mine], 1))
+    diag = [diag_inverse] + [fetched[k] for k in range(narrow - 1)]
+
+    def part(k):
+        mixed = contract(diag[k], pivot, 1, 0)
+        own_cols = lax.dynamic_slice_in_dim(diag[k], narrow_place * col_share, col_share, 1)
+        return contract(corr_panel, own_cols, 1, 1) - contract(factor_prev, mixed, 1, 1)
+
+    arrived = [below(part(k), k) for k in range(narrow - 1, 0, -1)]
+    panel_factor = part(0)
+    for block in arrived:
+        panel_factor = panel_factor + block
 
     samples = contract(draws_prev, factor_prev, 0, 1) + contract(draws_panel, panel_factor, 0, 1)
     squares = jnp.sum(factor_prev * factor_prev, axis=1) + jnp.sum(panel_factor * panel_factor, axis=1)
-    outgoing = jnp.stack([samples, jnp.broadcast_to(squares[None, :], samples.shape)], axis=1)
-    incoming = lax.all_to_all(outgoing, ("narrow", "wide"), split_axis=0, concat_axis=0, tiled=True)
-    whole = jnp.sum(incoming.reshape(narrow, wide, 2, row_count), axis=0)
-    scaled = whole[:, 0] * lax.rsqrt(whole[:, 1] + 1e-06)
+    share = samples.shape[0] // narrow
+    blocks = jnp.concatenate(
+        [
+            samples.reshape(narrow, share, row_count),
+            jnp.broadcast_to(squares[None, None, :], (narrow, 1, row_count)),
+        ],
+        axis=1,
+    )
+
+    def block_below(k):
+        return lax.dynamic_index_in_dim(blocks, (narrow_place - k) % narrow, 0, keepdims=False)
+
+    summed = block_below(0)
+    for block in [below(block_below(k), k) for k in range(1, narrow)]:
+        summed = summed + block
+    scaled = summed[:share] * lax.rsqrt(summed[share:] + 1e-06)
     uniforms = 0.5 * (1.0 + lax.erf(scaled * HALF_ROOT))
-    return (panel_factor, smooth(uniforms.reshape(1, wide * row_count)))
+    whole = lax.all_to_all(uniforms, "wide", split_axis=0, concat_axis=1, tiled=True)
+    return (panel_factor, smooth(whole))
 
 
 def solution(mesh):

time: 78.2 us -> 73 us (0.934)
  starting transfers between devices: 34.5 us -> 30.9 us
  waiting for transfers between devices: 31.4 us -> 30.4 us
    ppermute x7 -> x11, waiting for transfers between devices: 15.3 us -> 23.6 us  [the longest x6 20.8 us: below(): lax.ppermute(value, 'narrow', [(i, (i - k) % narrow) for i in range(narro...]
    all_to_all x1, starting transfers between devices: 10.4 us -> 3.34 us  [per_device(): lax.all_to_all(uniforms, 'wide', split_axis=0, concat_axis=1, tiled=True)]
    ppermute x3, waiting for transfers between devices: 8.67 us -> 2.96 us  [broadcast(): lax.ppermute(held, 'wide', [(h, h ^ f) for h in holders])]
    all_to_all x1, waiting for transfers between devices: 7.39 us -> 3.85 us  [per_device(): lax.all_to_all(uniforms, 'wide', split_axis=0, concat_axis=1, tiled=True)]
    ppermute x7 -> x11, starting transfers between devices: 21.3 us -> 24.9 us  [the longest x6 12.6 us: below(): lax.ppermute(value, 'narrow', [(i, (i - k) % narrow) for i in range(narro...]
    unnamed x13 -> x11, local copies, waits for them, and re-layouts: 1.95 us -> 1.71 us
  transfers between devices with their start and end apart: 11 -> 15, of which waited for: 5 -> 10; matrix products, arithmetic and copies ran while one was open for 8% -> 6% of each run, Pallas kernels for 0% -> 0%
where the time goes in v2:
time: 73 us; the launch traced here: 72.6 us
  starting transfers between devices  30.9 us (42%)
  waiting for transfers between devices  30.4 us (42%)
  matrix products  5.47 us (7%)
  other arithmetic  2.44 us (3%)
  local copies, waits for them, and re-layouts  2.4 us (3%)
  between operations  1.03 us (1%)
    ppermute x6, waiting for transfers between devices, below(): lax.ppermute(value, 'narrow', [(i, (i - k) % narrow) for i in range(narro...  20.8 us
    ppermute x6, starting transfers between devices, below(): lax.ppermute(value, 'narrow', [(i, (i - k) % narrow) for i in range(narro...  12.6 us
    ppermute x3, starting transfers between devices, above(): lax.ppermute(value, 'narrow', [(i, (i + k) % narrow) for i in range(narro...  10.4 us
    dot_general x14, matrix products, contract(): lax.dot_general(left_side, right_side, (((left_dim,), (right_dim,)), ((),...  5.47 us
    all_to_all x1, waiting for transfers between devices, per_device(): lax.all_to_all(uniforms, 'wide', split_axis=0, concat_axis=1, tiled=True)  3.85 us
    all_to_all x1, starting transfers between devices, per_device(): lax.all_to_all(uniforms, 'wide', split_axis=0, concat_axis=1, tiled=True)  3.34 us
    ppermute x3, waiting for transfers between devices, broadcast(): lax.ppermute(held, 'wide', [(h, h ^ f) for h in holders])  2.96 us
    ppermute x3, starting transfers between devices, broadcast(): lax.ppermute(held, 'wide', [(h, h ^ f) for h in holders])  2.68 us
  transfers between devices with their start and end apart: 15, of which 10 were waited for; matrix products, arithmetic and copies ran while one was open for 6% of the time, Pallas kernels for 0%

profile of v2, /device:TPU:0, one launch (start us, length us, event | category | flops | bytes accessed | tf_op | source)
XLA Modules:
  0.0 72.6 jit_solution(1447794527990545758)
XLA Ops:
  0.7 1.2 %multiply_reduce_fusion = (f32[512]{0:T(512)S(1)}, f32[512,256]{1,0:T(8,128)S(1)}) fusion(f32[512,256]{1,0:T(8,128)} %param.6, pred[]{:T(512)S(6)} %eq.12), kind=kLoop, calls=%fused_computation.15 | loop fusion | flops 392704 | bytes 1050625 | tf_op jit(solution)/shard_map/reduce_sum | solution.py:84
  1.9 1.3 %collective-permute-start = (f32[512,256]{1,0:T(8,128)S(1)}, f32[512,256]{1,0:T(8,128)S(1)}, u32[]{:S(2)}, u32[]{:S(2)}) collective-permute-start(f32[512,256]{1,0:T(8,128)S(1)} %get-tuple-element.18), channel_id=1, source_target_pairs={{8,0},{9,1},{10,2},{11,3}} | collective-permute-start | bytes 1572872 | tf_op jit(solution)/shard_map/ppermute | solution.py:30
  3.2 0.7 collective-permute-start.1
  3.9 0.7 collective-permute-start.2
  4.7 3.1 %collective-permute-start.3 = (f32[64,512]{1,0:T(8,128)S(1)}, f32[64,512]{1,0:T(8,128)S(1)}, u32[]{:S(2)}, u32[]{:S(2)}) collective-permute-start(f32[64,512]{1,0:T(8,128)S(1)} %constant_dynamic-slice_fusion), channel_id=1, source_target_pairs={{0,1},{1,2},{2,3},{3,0},{4,5},{5,6},{6,7},{7,4},{8,9},{9,10},{10,1... | collective-permute-start | bytes 393224 | tf_op jit(solution)/shard_map/ppermute | solution.py:61
  7.7 2.6 %collective-permute-start.4 = (f32[64,512]{1,0:T(8,128)S(1)}, f32[64,512]{1,0:T(8,128)S(1)}, u32[]{:S(2)}, u32[]{:S(2)}) collective-permute-start(f32[64,512]{1,0:T(8,128)S(1)} %constant_dynamic-slice_fusion), channel_id=1, source_target_pairs={{0,2},{1,3},{2,0},{3,1},{4,6},{5,7},{6,4},{7,5},{8,10},{9,11},{10,... | collective-permute-start | bytes 393224 | tf_op jit(solution)/shard_map/ppermute | solution.py:61
  10.3 3.0 %collective-permute-done = f32[512,256]{1,0:T(8,128)S(1)} collective-permute-done((f32[512,256]{1,0:T(8,128)S(1)}, f32[512,256]{1,0:T(8,128)S(1)}, u32[]{:S(2)}, u32[]{:S(2)}) %collective-permute-start) | collective-permute-done | bytes 524320 | tf_op jit(solution)/shard_map/ppermute | solution.py:30
  13.3 4.8 %collective-permute-start.5 = (f32[64,512]{1,0:T(8,128)S(1)}, f32[64,512]{1,0:T(8,128)S(1)}, u32[]{:S(2)}, u32[]{:S(2)}) collective-permute-start(f32[64,512]{1,0:T(8,128)S(1)} %constant_dynamic-slice_fusion), channel_id=1, source_target_pairs={{0,3},{1,0},{2,1},{3,2},{4,7},{5,4},{6,5},{7,6},{8,11},{9,8},{10,9... | collective-permute-start | bytes 393224 | tf_op jit(solution)/shard_map/ppermute | solution.py:61
  18.4 2.2 %collective-permute-done.5 = f32[64,512]{1,0:T(8,128)S(1)} collective-permute-done((f32[64,512]{1,0:T(8,128)S(1)}, f32[64,512]{1,0:T(8,128)S(1)}, u32[]{:S(2)}, u32[]{:S(2)}) %collective-permute-start.5) | collective-permute-done | bytes 131104 | tf_op jit(solution)/shard_map/ppermute | solution.py:61
  20.7 0.6 copy-done.3
  21.7 1.8 %collective-permute-start.6 = (f32[512,256]{1,0:T(8,128)S(1)}, f32[512,256]{1,0:T(8,128)S(1)}, u32[]{:S(2)}, u32[]{:S(2)}) collective-permute-start(f32[512,256]{1,0:T(8,128)S(1)} %add_add_fusion), channel_id=1, source_target_pairs={{8,12},{0,4},{24,28},{16,20},{9,13},{1,5},{25,29},{17,21},{10,14},... | collective-permute-start | bytes 1572872 | tf_op jit(solution)/shard_map/ppermute | solution.py:67
  26.3 1.2 %collective-permute-start.8 = (f32[512,128]{0,1:T(8,128)S(1)}, f32[512,128]{0,1:T(8,128)S(1)}, u32[]{:S(2)}, u32[]{:S(2)}) collective-permute-start(f32[512,128]{0,1:T(8,128)S(1)} %fusion.2), channel_id=1, source_target_pairs={{0,1},{1,2},{2,3},{3,0},{4,5},{5,6},{6,7},{7,4},{8,9},{9,10},{10,1... | collective-permute-start | bytes 786440 | tf_op jit(solution)/shard_map/ppermute | solution.py:58
  27.9 3.8 %collective-permute-start.9 = (f32[512,128]{0,1:T(8,128)S(1)}, f32[512,128]{0,1:T(8,128)S(1)}, u32[]{:S(2)}, u32[]{:S(2)}) collective-permute-start(f32[512,128]{0,1:T(8,128)S(1)} %fusion.1), channel_id=1, source_target_pairs={{0,2},{1,3},{2,0},{3,1},{4,6},{5,7},{6,4},{7,5},{8,10},{9,11},{10,... | collective-permute-start | bytes 786440 | tf_op jit(solution)/shard_map/ppermute | solution.py:58
  31.7 1.1 %fusion = f32[512,128]{0,1:T(8,128)} fusion(f32[128,512]{1,0:T(8,128)S(1)} %fusion.15, f32[128,256]{1,0:T(8,128)S(1)} %fusion.9, f32[512,256]{1,0:T(8,128)S(1)} %copy-done.1), kind=kOutput, calls=%fused_computation.1 | convolution fusion | flops 100728832 | bytes 1179648 | tf_op jit(solution)/shard_map/dot_general | solution.py:14
  33.7 4.2 %collective-permute-done.8 = f32[512,128]{0,1:T(8,128)S(1)} collective-permute-done((f32[512,128]{0,1:T(8,128)S(1)}, f32[512,128]{0,1:T(8,128)S(1)}, u32[]{:S(2)}, u32[]{:S(2)}) %collective-permute-start.8) | collective-permute-done | bytes 262176 | tf_op jit(solution)/shard_map/ppermute | solution.py:58
  37.9 10.9 %collective-permute-done.9 = f32[512,128]{0,1:T(8,128)S(1)} collective-permute-done((f32[512,128]{0,1:T(8,128)S(1)}, f32[512,128]{0,1:T(8,128)S(1)}, u32[]{:S(2)}, u32[]{:S(2)}) %collective-permute-start.9) | collective-permute-done | bytes 262176 | tf_op jit(solution)/shard_map/ppermute | solution.py:58
  49.7 5.4 %collective-permute-start.11 = (f32[9,512]{1,0:T(8,128)S(1)}, f32[9,512]{1,0:T(8,128)S(1)}, u32[]{:S(2)}, u32[]{:S(2)}) collective-permute-start(f32[9,512]{1,0:T(8,128)S(1)} %get-tuple-element.19), channel_id=1, source_target_pairs={{0,3},{1,0},{2,1},{3,2},{4,7},{5,4},{6,5},{7,6},{8,11},{9,8},{10,9... | collective-permute-start | bytes 55304 | tf_op jit(solution)/shard_map/ppermute | solution.py:58
  55.1 2.2 %collective-permute-start.12 = (f32[9,512]{1,0:T(8,128)S(1)}, f32[9,512]{1,0:T(8,128)S(1)}, u32[]{:S(2)}, u32[]{:S(2)}) collective-permute-start(f32[9,512]{1,0:T(8,128)S(1)} %get-tuple-element.20), channel_id=1, source_target_pairs={{0,2},{1,3},{2,0},{3,1},{4,6},{5,7},{6,4},{7,5},{8,10},{9,11},{10,... | collective-permute-start | bytes 55304 | tf_op jit(solution)/shard_map/ppermute | solution.py:58
  57.8 2.2 %collective-permute-done.12 = f32[9,512]{1,0:T(8,128)S(1)} collective-permute-done((f32[9,512]{1,0:T(8,128)S(1)}, f32[9,512]{1,0:T(8,128)S(1)}, u32[]{:S(2)}, u32[]{:S(2)}) %collective-permute-start.12) | collective-permute-done | bytes 18464 | tf_op jit(solution)/shard_map/ppermute | solution.py:58
  60.0 3.1 %collective-permute-done.13 = f32[9,512]{1,0:T(8,128)S(1)} collective-permute-done((f32[9,512]{1,0:T(8,128)S(1)}, f32[9,512]{1,0:T(8,128)S(1)}, u32[]{:S(2)}, u32[]{:S(2)}) %collective-permute-start.13) | collective-permute-done | bytes 18464 | tf_op jit(solution)/shard_map/ppermute | solution.py:58
  63.8 3.3 %all-to-all-start = ((f32[8,1,512]{2,1,0:T(1,128)}), f32[8,1,512]{2,1,0:T(1,128)S(1)}, u32[]{:S(2)}, u32[]{:S(2)}) async-start(f32[8,1,512]{2,1,0:T(1,128)} %all_to_all.12), calls=%async_computation | async-start | bytes 32768 | tf_op jit(solution)/shard_map/all_to_all | solution.py:102
  67.1 0.8 %copy.8 = f32[512,128]{1,0:T(8,128)} copy(f32[512,128]{0,1:T(8,128)S(1)} %get-tuple-element.23) | data formatting | bytes 524288
  67.9 3.8 %all-to-all-done = f32[8,1,512]{2,1,0:T(1,128)S(1)} async-done(((f32[8,1,512]{2,1,0:T(1,128)}), f32[8,1,512]{2,1,0:T(1,128)S(1)}, u32[]{:S(2)}, u32[]{:S(2)}) %all-to-all-start) | async-done | bytes 16416 | tf_op jit(solution)/shard_map/all_to_all | solution.py:102
  71.8 0.8 %multiply_add_fusion = f32[1,4096]{1,0:T(1,128)} fusion(f32[1,4096]{1,0:T(1,128)S(1)} %bitcast.86), kind=kLoop, calls=%fused_computation.61 | loop fusion | flops 36864 | bytes 32768 | tf_op jit(solution)/shard_map/add | solution.py:45
  (46 shorter events, 6.8 us)
Async XLA Ops:
  0.6 23.0 %copy-start = (f32[512,128]{1,0:T(8,128)S(1)}, f32[512,128]{1,0:T(8,128)}, u32[]{:S(2)}) copy-start(f32[512,128]{1,0:T(8,128)} %param.5) | copy-start | bytes 786436
  0.7 4.0 %copy-start.2 = (f32[128,512]{1,0:T(8,128)S(1)}, f32[128,512]{1,0:T(8,128)}, u32[]{:S(2)}) copy-start(f32[128,512]{1,0:T(8,128)} %param.9) | copy-start | bytes 786436
  1.9 11.4 %collective-permute-start = (f32[512,256]{1,0:T(8,128)S(1)}, f32[512,256]{1,0:T(8,128)S(1)}, u32[]{:S(2)}, u32[]{:S(2)}) collective-permute-start(f32[512,256]{1,0:T(8,128)S(1)} %get-tuple-element.18), channel_id=1, source_target_pairs={{8,0},{9,1},{10,2},{11,3}} | collective-permute-start | bytes 1572872 | tf_op jit(solution)/shard_map/ppermute | solution.py:30
  3.2 14.8 %collective-permute-start.1 = (f32[512,256]{1,0:T(8,128)S(1)}, f32[512,256]{1,0:T(8,128)S(1)}, u32[]{:S(2)}, u32[]{:S(2)}) collective-permute-start(f32[512,256]{1,0:T(8,128)S(1)} %get-tuple-element.18), channel_id=1, source_target_pairs={{8,24},{9,25},{10,26},{11,27}} | collective-permute-start | bytes 1572872 | tf_op jit(solution)/shard_map/ppermute | solution.py:30
  3.9 14.1 %collective-permute-start.2 = (f32[512,256]{1,0:T(8,128)S(1)}, f32[512,256]{1,0:T(8,128)S(1)}, u32[]{:S(2)}, u32[]{:S(2)}) collective-permute-start(f32[512,256]{1,0:T(8,128)S(1)} %get-tuple-element.18), channel_id=1, source_target_pairs={{8,16},{9,17},{10,18},{11,19}} | collective-permute-start | bytes 1572872 | tf_op jit(solution)/shard_map/ppermute | solution.py:30
  4.7 13.5 %collective-permute-start.3 = (f32[64,512]{1,0:T(8,128)S(1)}, f32[64,512]{1,0:T(8,128)S(1)}, u32[]{:S(2)}, u32[]{:S(2)}) collective-permute-start(f32[64,512]{1,0:T(8,128)S(1)} %constant_dynamic-slice_fusion), channel_id=1, source_target_pairs={{0,1},{1,2},{2,3},{3,0},{4,5},{5,6},{6,7},{7,4},{8,9},{9,10},{10,1... | collective-permute-start | bytes 393224 | tf_op jit(solution)/shard_map/ppermute | solution.py:61
  7.7 10.6 %collective-permute-start.4 = (f32[64,512]{1,0:T(8,128)S(1)}, f32[64,512]{1,0:T(8,128)S(1)}, u32[]{:S(2)}, u32[]{:S(2)}) collective-permute-start(f32[64,512]{1,0:T(8,128)S(1)} %constant_dynamic-slice_fusion), channel_id=1, source_target_pairs={{0,2},{1,3},{2,0},{3,1},{4,6},{5,7},{6,4},{7,5},{8,10},{9,11},{10,... | collective-permute-start | bytes 393224 | tf_op jit(solution)/shard_map/ppermute | solution.py:61
  13.3 7.3 %collective-permute-start.5 = (f32[64,512]{1,0:T(8,128)S(1)}, f32[64,512]{1,0:T(8,128)S(1)}, u32[]{:S(2)}, u32[]{:S(2)}) collective-permute-start(f32[64,512]{1,0:T(8,128)S(1)} %constant_dynamic-slice_fusion), channel_id=1, source_target_pairs={{0,3},{1,0},{2,1},{3,2},{4,7},{5,4},{6,5},{7,6},{8,11},{9,8},{10,9... | collective-permute-start | bytes 393224 | tf_op jit(solution)/shard_map/ppermute | solution.py:61
  18.2 2.5 %copy-start.1 = (f32[512,256]{1,0:T(8,128)S(1)}, f32[512,256]{1,0:T(8,128)}, u32[]{:S(2)}) copy-start(f32[512,256]{1,0:T(8,128)} %param.6) | copy-start | bytes 1572868
  20.6 0.8 %copy-start.3 = (f32[256,32]{0,1:T(8,128)S(1)}, f32[256,32]{0,1:T(8,128)}, u32[]{:S(2)}) copy-start(f32[256,32]{0,1:T(8,128)} %param.7) | copy-start | bytes 98308
  20.6 2.9 %collective-permute-start.7 = (f32[3,64,512]{2,1,0:T(8,128)S(1)}, f32[3,64,512]{2,1,0:T(8,128)S(1)}, u32[]{:S(2)}, u32[]{:S(2)}) collective-permute-start(f32[3,64,512]{2,1,0:T(8,128)S(1)} %pad_maximum_fusion), channel_id=1, source_target_pairs={{0,4},{4,0},{8,12},{12,8},{16,20},{20,16},{24,28},{28,24},{1,5},{5... | collective-permute-start | bytes 1179656 | tf_op jit(solution)/shard_map/ppermute | solution.py:69
  21.7 3.3 %collective-permute-start.6 = (f32[512,256]{1,0:T(8,128)S(1)}, f32[512,256]{1,0:T(8,128)S(1)}, u32[]{:S(2)}, u32[]{:S(2)}) collective-permute-start(f32[512,256]{1,0:T(8,128)S(1)} %add_add_fusion), channel_id=1, source_target_pairs={{8,12},{0,4},{24,28},{16,20},{9,13},{1,5},{25,29},{17,21},{10,14},... | collective-permute-start | bytes 1572872 | tf_op jit(solution)/shard_map/ppermute | solution.py:67
  26.3 11.6 %collective-permute-start.8 = (f32[512,128]{0,1:T(8,128)S(1)}, f32[512,128]{0,1:T(8,128)S(1)}, u32[]{:S(2)}, u32[]{:S(2)}) collective-permute-start(f32[512,128]{0,1:T(8,128)S(1)} %fusion.2), channel_id=1, source_target_pairs={{0,1},{1,2},{2,3},{3,0},{4,5},{5,6},{6,7},{7,4},{8,9},{9,10},{10,1... | collective-permute-start | bytes 786440 | tf_op jit(solution)/shard_map/ppermute | solution.py:58
  27.9 20.9 %collective-permute-start.9 = (f32[512,128]{0,1:T(8,128)S(1)}, f32[512,128]{0,1:T(8,128)S(1)}, u32[]{:S(2)}, u32[]{:S(2)}) collective-permute-start(f32[512,128]{0,1:T(8,128)S(1)} %fusion.1), channel_id=1, source_target_pairs={{0,2},{1,3},{2,0},{3,1},{4,6},{5,7},{6,4},{7,5},{8,10},{9,11},{10,... | collective-permute-start | bytes 786440 | tf_op jit(solution)/shard_map/ppermute | solution.py:58
  32.8 16.0 %collective-permute-start.10 = (f32[512,128]{0,1:T(8,128)}, f32[512,128]{0,1:T(8,128)S(1)}, u32[]{:S(2)}, u32[]{:S(2)}) collective-permute-start(f32[512,128]{0,1:T(8,128)} %fusion), channel_id=1, source_target_pairs={{0,3},{1,0},{2,1},{3,2},{4,7},{5,4},{6,5},{7,6},{8,11},{9,8},{10,9... | collective-permute-start | bytes 786440 | tf_op jit(solution)/shard_map/ppermute | solution.py:58
  48.8 0.7 copy-start.4
  49.7 8.1 %collective-permute-start.11 = (f32[9,512]{1,0:T(8,128)S(1)}, f32[9,512]{1,0:T(8,128)S(1)}, u32[]{:S(2)}, u32[]{:S(2)}) collective-permute-start(f32[9,512]{1,0:T(8,128)S(1)} %get-tuple-element.19), channel_id=1, source_target_pairs={{0,3},{1,0},{2,1},{3,2},{4,7},{5,4},{6,5},{7,6},{8,11},{9,8},{10,9... | collective-permute-start | bytes 55304 | tf_op jit(solution)/shard_map/ppermute | solution.py:58
  55.1 4.8 %collective-permute-start.12 = (f32[9,512]{1,0:T(8,128)S(1)}, f32[9,512]{1,0:T(8,128)S(1)}, u32[]{:S(2)}, u32[]{:S(2)}) collective-permute-start(f32[9,512]{1,0:T(8,128)S(1)} %get-tuple-element.20), channel_id=1, source_target_pairs={{0,2},{1,3},{2,0},{3,1},{4,6},{5,7},{6,4},{7,5},{8,10},{9,11},{10,... | collective-permute-start | bytes 55304 | tf_op jit(solution)/shard_map/ppermute | solution.py:58
  57.4 5.7 %collective-permute-start.13 = (f32[9,512]{1,0:T(8,128)S(1)}, f32[9,512]{1,0:T(8,128)S(1)}, u32[]{:S(2)}, u32[]{:S(2)}) collective-permute-start(f32[9,512]{1,0:T(8,128)S(1)} %get-tuple-element.21), channel_id=1, source_target_pairs={{0,1},{1,2},{2,3},{3,0},{4,5},{5,6},{6,7},{7,4},{8,9},{9,10},{10,1... | collective-permute-start | bytes 55304 | tf_op jit(solution)/shard_map/ppermute | solution.py:58
  63.8 8.0 %all-to-all-start = ((f32[8,1,512]{2,1,0:T(1,128)}), f32[8,1,512]{2,1,0:T(1,128)S(1)}, u32[]{:S(2)}, u32[]{:S(2)}) async-start(f32[8,1,512]{2,1,0:T(1,128)} %all_to_all.12), calls=%async_computation | async-start | bytes 32768 | tf_op jit(solution)/shard_map/all_to_all | solution.py:102

commit v3 on v1

v3 whole, which is shorter than its diff:
```python
import math

import jax
import jax.numpy as jnp
from jax import lax
from jax.sharding import PartitionSpec as P

WIN = 5
PRECISE = lax.Precision.HIGH
HALF_ROOT = 1.0 / math.sqrt(2.0)


def contract(left_side, right_side, left_dim, right_dim):
    return lax.dot_general(
        left_side,
        right_side,
        (((left_dim,), (right_dim,)), ((), ())),
        precision=PRECISE,
        preferred_element_type=jnp.float32,
    )


def pack(block, width):
    groups = width // block.shape[1]
    return jnp.concatenate(jnp.split(block, groups, 0), 1)


def unpack(packed, depth):
    return jnp.concatenate(jnp.split(packed, packed.shape[1] // depth, 1), 0)


def broadcast(block, source, wide, narrow, riders):
    place = lax.axis_index("wide")
    on_core = place % 2 == source % 2
    riders, carried = list(riders), []
    half = block.shape[0] // 2
    top = jnp.where(place == source, pack(block[:half], wide_of(riders)), 0.0)
    bottom = jnp.where(place == source, pack(block[half:], wide_of(riders)), 0.0)
    holders = [source]

    def pairs(flips):
        return [
            ((h ^ fro) * narrow + i, (h ^ to) * narrow + i)
            for h in holders
            for fro, to in flips
            for i in range(narrow)
        ]

    def send(*loads):
        values, routes = [], []
        for value, flips in loads:
            route = pairs(flips)
            if riders:
                rider, more = riders.pop(0)
                value, route = jnp.where(on_core, value, rider), route + more
            values.append(value)
            routes.append(route)
        values = lax.optimization_barrier(tuple(values))
        return [lax.ppermute(v, ("wide", "narrow"), r) for v, r in zip(values, routes)]

    shift = 1
    while (1 << shift) < wide:
        low, high = 1 << shift, 2 << shift
        if high < wide:
            both = low | high
            more = len(riders) > 0
            to_low, to_high = send((top, [(0, low)]), (bottom, [(0, high)]))
            carried += [to_low, to_high] if more else []
            top, bottom = top + to_low, bottom + to_high
            more = len(riders) > 0
            (to_high,) = send((top, [(0, high), (low, both)]))
            carried += [to_high] if more else []
            (to_low,) = send((bottom, [(0, low), (high, both)]))
            top, bottom = top + to_high, bottom + to_low
            holders = [h ^ f for h in holders for f in (0, low, high, both)]
        else:
            to_low = send((top, [(0, low)]), (bottom, [(0, low)]))
            top, bottom = top + to_low[0], bottom + to_low[1]
            holders = [h ^ f for h in holders for f in (0, low)]
        shift += 2
    return top, bottom, carried


def wide_of(riders):
    return riders[0][0].shape[1]


def smooth(uniforms):
    half_span = (WIN - 1) // 2
    feature_count = uniforms.shape[1]
    padded = jnp.pad(uniforms, ((0, 0), (half_span, half_span)))
    summed = jnp.zeros_like(uniforms)
    for offset in range(WIN):
        weight_tap = math.comb(WIN - 1, offset) / 2.0 ** (WIN - 1)
        summed = summed + weight_tap * padded[:, offset : offset + feature_count]
    return summed


def per_device(wide, narrow, corr_panel, factor_prev, draws_prev, draws_panel, diag_inverse):
    row_count, depth = factor_prev.shape
    col_share, panel = diag_inverse.shape
    narrow_place = lax.axis_index("narrow")
    source = depth * narrow // row_count
    on_core = lax.axis_index("wide") % 2 == source % 2
    fetchers = [c for c in range(wide) if c % 2 != source % 2]

    def shifted(k):
        return [(c * narrow + i, c * narrow + (i + k) % narrow) for c in fetchers for i in range(narrow)]

    order = sorted(range(1, narrow), key=lambda k: (abs(2 * k - narrow), -k))
    top, bottom, rows = broadcast(
        factor_prev, source, wide, narrow, [(diag_inverse, shifted(k)) for k in range(narrow - 1, 0, -1)]
    )
    rows = [rows[narrow - 1 - k] for k in order]
    own_pivot, own_rows = jnp.concatenate([top, bottom]), jnp.concatenate(rows)
    spare = own_rows.shape[0] - own_pivot.shape[0]
    pieces = jnp.where(on_core, jnp.pad(own_pivot, ((0, spare), (0, 0))), own_rows)
    swapped = lax.ppermute(pieces, "wide", [(i, i ^ 1) for i in range(wide)])
    own_pivot, swapped_pivot = pieces[: own_pivot.shape[0]], swapped[: own_pivot.shape[0]]
    pivot = jnp.where(on_core, own_pivot, swapped_pivot)
    pivot = jnp.concatenate([unpack(half, depth) for half in jnp.split(pivot, 2)])

    def part(diag):
        mixed = contract(diag, pivot, 1, 0)
        own_cols = lax.dynamic_slice_in_dim(diag, narrow_place * col_share, col_share, 1)
        return contract(corr_panel, own_cols, 1, 1) - contract(factor_prev, mixed, 1, 1)

    def deliver(value, k):
        return lax.ppermute(value, "narrow", [(i, (i - k) % narrow) for i in range(narrow)])

    arrived = []
    for at, k in enumerate(order):
        at = slice(at * col_share, (at + 1) * col_share)
        arrived.append(deliver(part(jnp.where(on_core, swapped[at], pieces[at])), k))
    panel_factor = part(diag_inverse)
    for block in arrived:
        panel_factor = panel_factor + block

    samples = contract(draws_prev, factor_prev, 0, 1) + contract(draws_panel, panel_factor, 0, 1)
    squares = jnp.sum(factor_prev * factor_prev, axis=1) + jnp.sum(panel_factor * panel_factor, axis=1)
    outgoing = jnp.concatenate([samples, jnp.broadcast_to(squares[None, :], samples.shape)], axis=1)
    incoming = lax.all_to_all(outgoing, ("narrow", "wide"), split_axis=0, concat_axis=0, tiled=True)
    whole = jnp.sum(incoming.reshape(narrow, wide, 2 * row_count), axis=0)
    scaled = whole[:, :row_count] * lax.rsqrt(whole[:, row_count:] + 1e-06)
    uniforms = 0.5 * (1.0 + lax.erf(scaled * HALF_ROOT))
    return (panel_factor, smooth(uniforms.reshape(1, wide * row_count)))


def solution(mesh):
    wide, narrow = mesh.shape["wide"], mesh.shape["narrow"]
    in_specs = (
        P("wide", "narrow"),
        P("wide", "narrow"),
        P("narrow", None),
        P("narrow", None),
        P("narrow", None),
    )
    out_specs = (P("wide", "narrow"), P(("narrow", "wide"), None))

    def body(*blocks):
        return per_device(wide, narrow, *blocks)

    return jax.shard_map(body, mesh=mesh, in_specs=in_specs, out_specs=out_specs, check_vma=False)
```

time: 78.2 us -> 66.8 us (0.85)
  starting transfers between devices: 34.5 us -> 18.8 us
  waiting for transfers between devices: 31.4 us -> 36.1 us
  local copies, waits for them, and re-layouts: 2.74 us -> 4.07 us
  matrix products: 5.81 us -> 4.75 us
    ppermute x10 -> x8, starting transfers between devices: 24.2 us -> 12.7 us  [the longest x3 6.92 us: deliver(): lax.ppermute(value, 'narrow', [(i, (i - k) % narrow) for i in range(narro...]
    ppermute x10 -> x8, waiting for transfers between devices: 24 us -> 28.7 us  [the longest x3 14.6 us: deliver(): lax.ppermute(value, 'narrow', [(i, (i - k) % narrow) for i in range(narro...]
    all_to_all x1, starting transfers between devices: 10.4 us -> 6.09 us  [per_device(): lax.all_to_all(outgoing, ('narrow', 'wide'), split_axis=0, concat_axis=0,...]
    split x0 -> x2, local copies, waits for them, and re-layouts: none -> 1.22 us  [the longest x1 1.18 us: pack(): return jnp.concatenate(jnp.split(block, groups, 0), 1)]
    reduce_sum x1, other arithmetic: 1.23 us -> 0.15 us  [per_device(): jnp.sum(factor_prev * factor_prev, axis=1)]
    dot_general x14, matrix products: 5.81 us -> 4.75 us  [contract(): lax.dot_general(left_side, right_side, (((left_dim,), (right_dim,)), ((),...]
    unnamed x13 -> x12, local copies, waits for them, and re-layouts: 1.95 us -> 2.07 us
  transfers between devices with their start and end apart: 11 -> 9, of which waited for: 5 -> 7; matrix products, arithmetic and copies ran while one was open for 8% -> 7% of each run, Pallas kernels for 0% -> 0%
where the time goes in v3:
time: 66.8 us; the launch traced here: 66.4 us
  waiting for transfers between devices  36.1 us (54%)
  starting transfers between devices  18.8 us (28%)
  matrix products  4.75 us (7%)
  local copies, waits for them, and re-layouts  4.07 us (6%)
  other arithmetic  1.73 us (3%)
  between operations  0.95 us (1%)
    ppermute x3, waiting for transfers between devices, deliver(): lax.ppermute(value, 'narrow', [(i, (i - k) % narrow) for i in range(narro...  14.6 us
    ppermute x4, waiting for transfers between devices, send(): lax.ppermute(v, ('wide', 'narrow'), r)  13.5 us
    all_to_all x1, waiting for transfers between devices, per_device(): lax.all_to_all(outgoing, ('narrow', 'wide'), split_axis=0, concat_axis=0,...  7.39 us
    ppermute x3, starting transfers between devices, deliver(): lax.ppermute(value, 'narrow', [(i, (i - k) % narrow) for i in range(narro...  6.92 us
    all_to_all x1, starting transfers between devices, per_device(): lax.all_to_all(outgoing, ('narrow', 'wide'), split_axis=0, concat_axis=0,...  6.09 us
    dot_general x14, matrix products, contract(): lax.dot_general(left_side, right_side, (((left_dim,), (right_dim,)), ((),...  4.75 us
    ppermute x4, starting transfers between devices, send(): lax.ppermute(v, ('wide', 'narrow'), r)  4.57 us
    unnamed x12, local copies, waits for them, and re-layouts  2.07 us
  transfers between devices with their start and end apart: 9, of which 7 were waited for; matrix products, arithmetic and copies ran while one was open for 7% of the time, Pallas kernels for 0%

profile of v3, /device:TPU:0, one launch (start us, length us, event | category | flops | bytes accessed | tf_op | source)
XLA Modules:
  0.0 66.4 jit_solution(1849545671179671784)
XLA Ops:
  0.7 1.2 %fusion.30 = (f32[128,256]{1,0:T(8,128)S(1)}, f32[128,256]{1,0:T(8,128)S(1)}, f32[128,256]{1,0:T(8,128)S(1)}, f32[128,256]{1,0:T(8,128)S(1)}) fusion(f32[512,256]{1,0:T(8,128)} %param.6), kind=kLoop, calls=%fused_computation.54 | loop fusion | bytes 1048576 | tf_op jit(solution)/shard_map/split | solution.py:25
  2.0 1.3 %collective-permute-start = (f32[128,512]{1,0:T(8,128)S(1)}, f32[128,512]{1,0:T(8,128)S(1)}, u32[]{:S(2)}, u32[]{:S(2)}) collective-permute-start(f32[128,512]{1,0:T(8,128)S(1)} %get-tuple-element.4), channel_id=1, source_target_pairs={{8,0},{9,1},{10,2},{11,3},{4,7},{5,4},{6,5},{7,6},{12,15},{13,12},... | collective-permute-start | bytes 786440 | tf_op jit(solution)/shard_map/ppermute | solution.py:59
  3.3 0.7 %collective-permute-start.2 = (f32[128,512]{1,0:T(8,128)S(1)}, f32[128,512]{1,0:T(8,128)S(1)}, u32[]{:S(2)}, u32[]{:S(2)}) collective-permute-start(f32[128,512]{1,0:T(8,128)S(1)} %get-tuple-element.5), channel_id=1, source_target_pairs={{8,24},{9,25},{10,26},{11,27},{4,6},{5,7},{6,4},{7,5},{12,14},{13,... | collective-permute-start | bytes 786440 | tf_op jit(solution)/shard_map/ppermute | solution.py:59
  4.0 6.6 %collective-permute-done = f32[128,512]{1,0:T(8,128)S(1)} collective-permute-done((f32[128,512]{1,0:T(8,128)S(1)}, f32[128,512]{1,0:T(8,128)S(1)}, u32[]{:S(2)}, u32[]{:S(2)}) %collective-permute-start) | collective-permute-done | bytes 262176 | tf_op jit(solution)/shard_map/ppermute | solution.py:59
  10.6 1.3 %collective-permute-start.1 = (f32[128,512]{1,0:T(8,128)S(1)}, f32[128,512]{1,0:T(8,128)S(1)}, u32[]{:S(2)}, u32[]{:S(2)}) collective-permute-start(f32[128,512]{1,0:T(8,128)S(1)} %broadcast_select_fusion), channel_id=1, source_target_pairs={{8,24},{9,25},{10,26},{11,27},{0,16},{1,17},{2,18},{3,19},{4,5},{5... | collective-permute-start | bytes 786440 | tf_op jit(solution)/shard_map/ppermute | solution.py:59
  12.0 1.3 %collective-permute-start.3 = (f32[128,512]{1,0:T(8,128)S(1)}, f32[128,512]{1,0:T(8,128)S(1)}, u32[]{:S(2)}, u32[]{:S(2)}) collective-permute-start(f32[128,512]{1,0:T(8,128)S(1)} %fusion.6), channel_id=1, source_target_pairs={{8,0},{9,1},{10,2},{11,3},{24,16},{25,17},{26,18},{27,19}} | collective-permute-start | bytes 786440 | tf_op jit(solution)/shard_map/ppermute | solution.py:59
  13.3 2.5 %collective-permute-done.1 = f32[128,512]{1,0:T(8,128)S(1)} collective-permute-done((f32[128,512]{1,0:T(8,128)S(1)}, f32[128,512]{1,0:T(8,128)S(1)}, u32[]{:S(2)}, u32[]{:S(2)}) %collective-permute-start.1) | collective-permute-done | bytes 262176 | tf_op jit(solution)/shard_map/ppermute | solution.py:59
  15.8 4.4 %collective-permute-done.3 = f32[128,512]{1,0:T(8,128)S(1)} collective-permute-done((f32[128,512]{1,0:T(8,128)S(1)}, f32[128,512]{1,0:T(8,128)S(1)}, u32[]{:S(2)}, u32[]{:S(2)}) %collective-permute-start.3) | collective-permute-done | bytes 262176 | tf_op jit(solution)/shard_map/ppermute | solution.py:59
  20.4 1.2 %collective-permute-start.4 = (f32[384,512]{1,0:T(8,128)S(1)}, f32[384,512]{1,0:T(8,128)S(1)}, u32[]{:S(2)}, u32[]{:S(2)}) collective-permute-start(f32[384,512]{1,0:T(8,128)S(1)} %fusion.5), channel_id=1, source_target_pairs={{0,4},{4,0},{8,12},{12,8},{16,20},{20,16},{24,28},{28,24},{1,5},{5... | collective-permute-start | bytes 2359304 | tf_op jit(solution)/shard_map/ppermute | solution.py:118
  22.1 0.5 copy-done.3
  22.9 0.6 collective-permute-done.4
  24.8 3.0 %collective-permute-start.5 = (f32[512,128]{0,1:T(8,128)S(1)}, f32[512,128]{0,1:T(8,128)S(1)}, u32[]{:S(2)}, u32[]{:S(2)}) collective-permute-start(f32[512,128]{0,1:T(8,128)S(1)} %fusion.2), channel_id=1, source_target_pairs={{0,2},{1,3},{2,0},{3,1},{4,6},{5,7},{6,4},{7,5},{8,10},{9,11},{10,... | collective-permute-start | bytes 786440 | tf_op jit(solution)/shard_map/ppermute | solution.py:129
  28.8 1.6 %collective-permute-start.6 = (f32[512,128]{0,1:T(8,128)S(1)}, f32[512,128]{0,1:T(8,128)S(1)}, u32[]{:S(2)}, u32[]{:S(2)}) collective-permute-start(f32[512,128]{0,1:T(8,128)S(1)} %fusion.1), channel_id=1, source_target_pairs={{0,1},{1,2},{2,3},{3,0},{4,5},{5,6},{6,7},{7,4},{8,9},{9,10},{10,1... | collective-permute-start | bytes 786440 | tf_op jit(solution)/shard_map/ppermute | solution.py:129
  31.4 2.3 %collective-permute-start.7 = (f32[512,128]{0,1:T(8,128)S(1)}, f32[512,128]{0,1:T(8,128)S(1)}, u32[]{:S(2)}, u32[]{:S(2)}) collective-permute-start(f32[512,128]{0,1:T(8,128)S(1)} %fusion), channel_id=1, source_target_pairs={{0,3},{1,0},{2,1},{3,2},{4,7},{5,4},{6,5},{7,6},{8,11},{9,8},{10,9... | collective-permute-start | bytes 786440 | tf_op jit(solution)/shard_map/ppermute | solution.py:129
  33.7 0.6 fusion.28
  34.3 0.4 fusion.3
  34.8 11.4 %collective-permute-done.5 = f32[512,128]{0,1:T(8,128)S(1)} collective-permute-done((f32[512,128]{0,1:T(8,128)S(1)}, f32[512,128]{0,1:T(8,128)S(1)}, u32[]{:S(2)}, u32[]{:S(2)}) %collective-permute-start.5) | collective-permute-done | bytes 262176 | tf_op jit(solution)/shard_map/ppermute | solution.py:129
  46.2 3.2 %collective-permute-done.7 = f32[512,128]{0,1:T(8,128)S(1)} collective-permute-done((f32[512,128]{0,1:T(8,128)S(1)}, f32[512,128]{0,1:T(8,128)S(1)}, u32[]{:S(2)}, u32[]{:S(2)}) %collective-permute-start.7) | collective-permute-done | bytes 262176 | tf_op jit(solution)/shard_map/ppermute | solution.py:129
  49.5 0.7 %copy-done.4 = f32[128,32]{0,1:T(8,128)S(1)} copy-done((f32[128,32]{0,1:T(8,128)S(1)}, f32[128,32]{0,1:T(8,128)}, u32[]{:S(2)}) %copy-start.4) | copy-done | bytes 16408
  50.4 0.8 %copy.8 = f32[32,1,1024]{2,1,0:T(1,128)} copy(f32[32,1,1024]{2,0,1:T(8,128)S(1)} %maximum_bitcast_fusion) | data formatting | bytes 262144 | tf_op jit(solution)/shard_map/all_to_all | solution.py:142
  51.2 6.1 %all-to-all-start = ((f32[32,1,1024]{2,1,0:T(1,128)}), f32[32,1,1024]{2,1,0:T(1,128)S(1)}, u32[]{:S(2)}, u32[]{:S(2)}) async-start(f32[32,1,1024]{2,1,0:T(1,128)} %copy.8), calls=%async_computation | async-start | bytes 262144 | tf_op jit(solution)/shard_map/all_to_all | solution.py:142
  57.3 0.8 %copy.9 = f32[512,128]{1,0:T(8,128)} copy(f32[512,128]{0,1:T(8,128)S(1)} %get-tuple-element.11) | data formatting | bytes 524288
  58.1 7.4 %all-to-all-done = f32[32,1,1024]{2,1,0:T(1,128)S(1)} async-done(((f32[32,1,1024]{2,1,0:T(1,128)}), f32[32,1,1024]{2,1,0:T(1,128)S(1)}, u32[]{:S(2)}, u32[]{:S(2)}) %all-to-all-start) | async-done | bytes 131104 | tf_op jit(solution)/shard_map/all_to_all | solution.py:142
  65.6 0.8 %multiply_add_fusion = f32[1,4096]{1,0:T(1,128)} fusion(f32[1,4096]{1,0:T(1,128)S(1)} %bitcast.40), kind=kLoop, calls=%fused_computation.41 | loop fusion | flops 36864 | bytes 32768 | tf_op jit(solution)/shard_map/add | solution.py:95
  (39 shorter events, 4.8 us)
Async XLA Ops:
  0.6 21.2 %copy-start = (f32[512,128]{1,0:T(8,128)S(1)}, f32[512,128]{1,0:T(8,128)}, u32[]{:S(2)}) copy-start(f32[512,128]{1,0:T(8,128)} %param.5) | copy-start | bytes 786436
  0.7 1.2 %copy-start.2 = (f32[128,512]{1,0:T(8,128)S(1)}, f32[128,512]{1,0:T(8,128)}, u32[]{:S(2)}) copy-start(f32[128,512]{1,0:T(8,128)} %param.9) | copy-start | bytes 786436
  2.0 8.6 %collective-permute-start = (f32[128,512]{1,0:T(8,128)S(1)}, f32[128,512]{1,0:T(8,128)S(1)}, u32[]{:S(2)}, u32[]{:S(2)}) collective-permute-start(f32[128,512]{1,0:T(8,128)S(1)} %get-tuple-element.4), channel_id=1, source_target_pairs={{8,0},{9,1},{10,2},{11,3},{4,7},{5,4},{6,5},{7,6},{12,15},{13,12},... | collective-permute-start | bytes 786440 | tf_op jit(solution)/shard_map/ppermute | solution.py:59
  3.3 8.6 %collective-permute-start.2 = (f32[128,512]{1,0:T(8,128)S(1)}, f32[128,512]{1,0:T(8,128)S(1)}, u32[]{:S(2)}, u32[]{:S(2)}) collective-permute-start(f32[128,512]{1,0:T(8,128)S(1)} %get-tuple-element.5), channel_id=1, source_target_pairs={{8,24},{9,25},{10,26},{11,27},{4,6},{5,7},{6,4},{7,5},{12,14},{13,... | collective-permute-start | bytes 786440 | tf_op jit(solution)/shard_map/ppermute | solution.py:59
  10.6 5.2 %collective-permute-start.1 = (f32[128,512]{1,0:T(8,128)S(1)}, f32[128,512]{1,0:T(8,128)S(1)}, u32[]{:S(2)}, u32[]{:S(2)}) collective-permute-start(f32[128,512]{1,0:T(8,128)S(1)} %broadcast_select_fusion), channel_id=1, source_target_pairs={{8,24},{9,25},{10,26},{11,27},{0,16},{1,17},{2,18},{3,19},{4,5},{5... | collective-permute-start | bytes 786440 | tf_op jit(solution)/shard_map/ppermute | solution.py:59
  12.0 8.3 %collective-permute-start.3 = (f32[128,512]{1,0:T(8,128)S(1)}, f32[128,512]{1,0:T(8,128)S(1)}, u32[]{:S(2)}, u32[]{:S(2)}) collective-permute-start(f32[128,512]{1,0:T(8,128)S(1)} %fusion.6), channel_id=1, source_target_pairs={{8,0},{9,1},{10,2},{11,3},{24,16},{25,17},{26,18},{27,19}} | collective-permute-start | bytes 786440 | tf_op jit(solution)/shard_map/ppermute | solution.py:59
  20.3 1.4 %copy-start.1 = (f32[512,256]{1,0:T(8,128)S(1)}, f32[512,256]{1,0:T(8,128)}, u32[]{:S(2)}) copy-start(f32[512,256]{1,0:T(8,128)} %param.6) | copy-start | bytes 1572868
  20.4 3.1 %collective-permute-start.4 = (f32[384,512]{1,0:T(8,128)S(1)}, f32[384,512]{1,0:T(8,128)S(1)}, u32[]{:S(2)}, u32[]{:S(2)}) collective-permute-start(f32[384,512]{1,0:T(8,128)S(1)} %fusion.5), channel_id=1, source_target_pairs={{0,4},{4,0},{8,12},{12,8},{16,20},{20,16},{24,28},{28,24},{1,5},{5... | collective-permute-start | bytes 2359304 | tf_op jit(solution)/shard_map/ppermute | solution.py:118
  21.8 0.8 %copy-start.3 = (f32[256,32]{0,1:T(8,128)S(1)}, f32[256,32]{0,1:T(8,128)}, u32[]{:S(2)}) copy-start(f32[256,32]{0,1:T(8,128)} %param.7) | copy-start | bytes 98308
  24.8 21.4 %collective-permute-start.5 = (f32[512,128]{0,1:T(8,128)S(1)}, f32[512,128]{0,1:T(8,128)S(1)}, u32[]{:S(2)}, u32[]{:S(2)}) collective-permute-start(f32[512,128]{0,1:T(8,128)S(1)} %fusion.2), channel_id=1, source_target_pairs={{0,2},{1,3},{2,0},{3,1},{4,6},{5,7},{6,4},{7,5},{8,10},{9,11},{10,... | collective-permute-start | bytes 786440 | tf_op jit(solution)/shard_map/ppermute | solution.py:129
  28.8 17.4 %collective-permute-start.6 = (f32[512,128]{0,1:T(8,128)S(1)}, f32[512,128]{0,1:T(8,128)S(1)}, u32[]{:S(2)}, u32[]{:S(2)}) collective-permute-start(f32[512,128]{0,1:T(8,128)S(1)} %fusion.1), channel_id=1, source_target_pairs={{0,1},{1,2},{2,3},{3,0},{4,5},{5,6},{6,7},{7,4},{8,9},{9,10},{10,1... | collective-permute-start | bytes 786440 | tf_op jit(solution)/shard_map/ppermute | solution.py:129
  31.4 17.9 %collective-permute-start.7 = (f32[512,128]{0,1:T(8,128)S(1)}, f32[512,128]{0,1:T(8,128)S(1)}, u32[]{:S(2)}, u32[]{:S(2)}) collective-permute-start(f32[512,128]{0,1:T(8,128)S(1)} %fusion), channel_id=1, source_target_pairs={{0,3},{1,0},{2,1},{3,2},{4,7},{5,4},{6,5},{7,6},{8,11},{9,8},{10,9... | collective-permute-start | bytes 786440 | tf_op jit(solution)/shard_map/ppermute | solution.py:129
  49.5 0.7 %copy-start.4 = (f32[128,32]{0,1:T(8,128)S(1)}, f32[128,32]{0,1:T(8,128)}, u32[]{:S(2)}) copy-start(f32[128,32]{0,1:T(8,128)} %param.8) | copy-start | bytes 49156
  51.2 14.3 %all-to-all-start = ((f32[32,1,1024]{2,1,0:T(1,128)}), f32[32,1,1024]{2,1,0:T(1,128)S(1)}, u32[]{:S(2)}, u32[]{:S(2)}) async-start(f32[32,1,1024]{2,1,0:T(1,128)} %copy.8), calls=%async_computation | async-start | bytes 262144 | tf_op jit(solution)/shard_map/all_to_all | solution.py:142

commit v4 on v1

v4 whole, which is shorter than its diff:
```python
import math

import jax
import jax.numpy as jnp
from jax import lax
from jax.sharding import PartitionSpec as P

WIN = 5
PRECISE = lax.Precision.HIGH
HALF_ROOT = 1.0 / math.sqrt(2.0)


def contract(left_side, right_side, left_dim, right_dim):
    return lax.dot_general(
        left_side,
        right_side,
        (((left_dim,), (right_dim,)), ((), ())),
        precision=PRECISE,
        preferred_element_type=jnp.float32,
    )


def pack(block, width):
    groups = width // block.shape[1]
    return jnp.concatenate(jnp.split(block, groups, 0), 1)


def unpack(packed, depth):
    return jnp.concatenate(jnp.split(packed, packed.shape[1] // depth, 1), 0)


def broadcast(block, source, wide, narrow, riders):
    place = lax.axis_index("wide")
    on_core = place % 2 == source % 2
    riders, carried = list(riders), []
    packed = pack(block, riders[0][0].shape[1])
    half = packed.shape[0] // 2
    held = jnp.where(place == source, packed, 0.0)
    holders = [source]

    def send(value, to):
        pairs = [(h * narrow + i, (h ^ to) * narrow + i) for h in holders for i in range(narrow)]
        if not riders or value.shape != riders[0][0].shape:
            return lax.ppermute(value, ("wide", "narrow"), pairs)
        rider, more = riders.pop(0)
        carried.append(lax.ppermute(jnp.where(on_core, value, rider), ("wide", "narrow"), pairs + more))
        return carried[-1]

    shift = 1
    while (1 << shift) < wide:
        low, high, both = 1 << shift, 2 << shift, 3 << shift
        top, bottom = packed[:half], packed[half:]
        tops, bottoms = [send(top, low)], [send(bottom, low)]
        if high < wide:
            for flip in (both, high):
                tops.append(send(top, flip))
                bottoms.append(send(bottom, flip))
        held = held + jnp.concatenate([sum(tops), sum(bottoms)])
        holders = [h ^ f for h in holders for f in (0, low, high, both)[: 1 + len(tops)]]
        packed = held
        shift += 2
    return held, carried


def smooth(uniforms):
    half_span = (WIN - 1) // 2
    feature_count = uniforms.shape[1]
    padded = jnp.pad(uniforms, ((0, 0), (half_span, half_span)))
    summed = jnp.zeros_like(uniforms)
    for offset in range(WIN):
        weight_tap = math.comb(WIN - 1, offset) / 2.0 ** (WIN - 1)
        summed = summed + weight_tap * padded[:, offset : offset + feature_count]
    return summed


def per_device(wide, narrow, corr_panel, factor_prev, draws_prev, draws_panel, diag_inverse):
    row_count, depth = factor_prev.shape
    col_share, panel = diag_inverse.shape
    narrow_place = lax.axis_index("narrow")
    source = depth * narrow // row_count
    on_core = lax.axis_index("wide") % 2 == source % 2
    fetchers = [c for c in range(wide) if c % 2 != source % 2]

    def shifted(k):
        return [(c * narrow + i, c * narrow + (i + k) % narrow) for c in fetchers for i in range(narrow)]

    far = list(range(narrow - 1, 0, -1))
    own_pivot, rows = broadcast(
        factor_prev, source, wide, narrow, [(diag_inverse, shifted(k)) for k in far]
    )
    rows = dict(zip(far, lax.optimization_barrier(tuple(rows))))

    even = narrow_place % 2 == 0
    own_rows = jnp.concatenate(
        [rows[2], jnp.where(even, rows[1], rows[3]), jnp.where(even, rows[3], rows[1])]
    )
    spare = own_rows.shape[0] - own_pivot.shape[0]
    pieces = jnp.where(on_core, jnp.pad(own_pivot, ((0, spare), (0, 0))), own_rows)
    swapped = lax.ppermute(pieces, "wide", [(i, i ^ 1) for i in range(wide)])
    own_pivot, swapped_pivot = pieces[: own_pivot.shape[0]], swapped[: own_pivot.shape[0]]
    pivot = unpack(jnp.where(on_core, own_pivot, swapped_pivot), depth)

    def part(diag, pivot):
        mixed = contract(diag, pivot, 1, 0)
        own_cols = lax.dynamic_slice_in_dim(diag, narrow_place * col_share, col_share, 1)
        return contract(corr_panel, own_cols, 1, 1) - contract(factor_prev, mixed, 1, 1)

    def turn_part(t, pivot):
        at = slice(t * col_share, (t + 1) * col_share)
        return lax.optimization_barrier((part(jnp.where(on_core, swapped[at], pieces[at]), pivot), pivot))

    end = (narrow_place == 0) | (narrow_place == narrow - 1)
    two_on, pivot = turn_part(0, pivot)
    two_on = lax.ppermute(two_on, "narrow", [(0, 1), (1, 3), (2, 0), (3, 2)])
    across, pivot = turn_part(1, pivot)
    outer = lax.ppermute(across, "narrow", [(0, 3), (3, 0)])
    beside, pivot = turn_part(2, pivot)
    beside = lax.ppermute(beside, "narrow", [(0, 1), (1, 0), (2, 3), (3, 2)])
    inner = lax.ppermute(across + two_on, "narrow", [(1, 2), (2, 1)])
    panel_factor = part(diag_inverse, pivot) + beside + outer + inner + jnp.where(end, two_on, 0.0)

    samples = contract(draws_prev, factor_prev, 0, 1) + contract(draws_panel, panel_factor, 0, 1)
    squares = jnp.sum(factor_prev * factor_prev, axis=1) + jnp.sum(panel_factor * panel_factor, axis=1)
    outgoing = jnp.concatenate([samples, jnp.broadcast_to(squares[None, :], samples.shape)], axis=1)
    incoming = lax.all_to_all(outgoing, ("narrow", "wide"), split_axis=0, concat_axis=0, tiled=True)
    whole = jnp.sum(incoming.reshape(narrow, wide, 2 * row_count), axis=0)
    scaled = whole[:, :row_count] * lax.rsqrt(whole[:, row_count:] + 1e-06)
    uniforms = 0.5 * (1.0 + lax.erf(scaled * HALF_ROOT))
    return (panel_factor, smooth(uniforms.reshape(1, wide * row_count)))


def solution(mesh):
    wide, narrow = mesh.shape["wide"], mesh.shape["narrow"]
    in_specs = (
        P("wide", "narrow"),
        P("wide", "narrow"),
        P("narrow", None),
        P("narrow", None),
        P("narrow", None),
    )
    out_specs = (P("wide", "narrow"), P(("narrow", "wide"), None))

    def body(*blocks):
        return per_device(wide, narrow, *blocks)

    return jax.shard_map(body, mesh=mesh, in_specs=in_specs, out_specs=out_specs, check_vma=False)
```

time: 78.2 us -> 63.1 us (0.81)
  starting transfers between devices: 34.5 us -> 24.4 us
  waiting for transfers between devices: 31.4 us -> 25.6 us
  local copies, waits for them, and re-layouts: 2.74 us -> 4 us
    all_to_all x1, starting transfers between devices: 10.4 us -> 4.16 us  [per_device(): lax.all_to_all(outgoing, ('narrow', 'wide'), split_axis=0, concat_axis=0,...]
    ppermute x10 -> x11, waiting for transfers between devices: 24 us -> 18.2 us  [the longest x3 6.03 us: send(): lax.ppermute(jnp.where(on_core, value, rider), ('wide', 'narrow'), pairs...]
    ppermute x10 -> x11, starting transfers between devices: 24.2 us -> 20.2 us  [the longest x1 7.54 us: per_device(): swapped = lax.ppermute(pieces, 'wide', [(i, i ^ 1) for i in range(wide)])]
    split x0 -> x2, local copies, waits for them, and re-layouts: none -> 1.15 us  [the longest x1 1.12 us: pack(): return jnp.concatenate(jnp.split(block, groups, 0), 1)]
    reduce_sum x1, other arithmetic: 1.23 us -> 0.15 us  [per_device(): jnp.sum(factor_prev * factor_prev, axis=1)]
    all_to_all x0 -> x1, local copies, waits for them, and re-layouts: none -> 0.79 us  [per_device(): lax.all_to_all(outgoing, ('narrow', 'wide'), split_axis=0, concat_axis=0,...]
    unnamed x13 -> x12, local copies, waits for them, and re-layouts: 1.95 us -> 2.04 us
  transfers between devices with their start and end apart: 11 -> 12, of which waited for: 5 -> 7; matrix products, arithmetic and copies ran while one was open for 8% -> 7% of each run, Pallas kernels for 0% -> 0%
where the time goes in v4:
time: 63.1 us; the launch traced here: 62.6 us
  waiting for transfers between devices  25.6 us (41%)
  starting transfers between devices  24.4 us (39%)
  matrix products  5.83 us (9%)
  local copies, waits for them, and re-layouts  4 us (6%)
  other arithmetic  1.78 us (3%)
  between operations  1.04 us (2%)
    ppermute x1, starting transfers between devices, per_device(): swapped = lax.ppermute(pieces, 'wide', [(i, i ^ 1) for i in range(wide)])  7.54 us
    all_to_all x1, waiting for transfers between devices, per_device(): lax.all_to_all(outgoing, ('narrow', 'wide'), split_axis=0, concat_axis=0,...  7.39 us
    ppermute x3, waiting for transfers between devices, send(): lax.ppermute(jnp.where(on_core, value, rider), ('wide', 'narrow'), pairs...  6.03 us
    dot_general x14, matrix products, contract(): lax.dot_general(left_side, right_side, (((left_dim,), (right_dim,)), ((),...  5.83 us
    ppermute x1, waiting for transfers between devices, per_device(): outer = lax.ppermute(across, 'narrow', [(0, 3), (3, 0)])  5.16 us
    ppermute x1, starting transfers between devices, per_device(): outer = lax.ppermute(across, 'narrow', [(0, 3), (3, 0)])  4.99 us
    ppermute x1, waiting for transfers between devices, per_device(): beside = lax.ppermute(beside, 'narrow', [(0, 1), (1, 0), (2, 3), (3, 2)])  4.71 us
    all_to_all x1, starting transfers between devices, per_device(): lax.all_to_all(outgoing, ('narrow', 'wide'), split_axis=0, concat_axis=0,...  4.16 us
  transfers between devices with their start and end apart: 12, of which 7 were waited for; matrix products, arithmetic and copies ran while one was open for 7% of the time, Pallas kernels for 0%

profile of v4, /device:TPU:0, one launch (start us, length us, event | category | flops | bytes accessed | tf_op | source)
XLA Modules:
  0.0 62.6 jit_solution(8783443645766723988)
XLA Ops:
  0.7 1.1 %fusion.31 = (f32[256,256]{1,0:T(8,128)S(1)}, f32[256,256]{1,0:T(8,128)S(1)}) fusion(f32[512,256]{1,0:T(8,128)} %param.6), kind=kLoop, calls=%fused_computation.59 | loop fusion | bytes 1048576 | tf_op jit(solution)/shard_map/split | solution.py:25
  1.9 1.3 %collective-permute-start = (f32[128,512]{1,0:T(8,128)S(1)}, f32[128,512]{1,0:T(8,128)S(1)}, u32[]{:S(2)}, u32[]{:S(2)}) collective-permute-start(f32[128,512]{1,0:T(8,128)S(1)} %get-tuple-element.31), channel_id=1, source_target_pairs={{8,0},{9,1},{10,2},{11,3},{4,7},{5,4},{6,5},{7,6},{12,15},{13,12},... | collective-permute-start | bytes 786440 | tf_op jit(solution)/shard_map/ppermute | solution.py:46
  3.2 1.3 %collective-permute-start.3 = (f32[128,512]{1,0:T(8,128)S(1)}, f32[128,512]{1,0:T(8,128)S(1)}, u32[]{:S(2)}, u32[]{:S(2)}) collective-permute-start(f32[128,512]{1,0:T(8,128)S(1)} %get-tuple-element.24), channel_id=1, source_target_pairs={{8,0},{9,1},{10,2},{11,3},{4,6},{5,7},{6,4},{7,5},{12,14},{13,15},... | collective-permute-start | bytes 786440 | tf_op jit(solution)/shard_map/ppermute | solution.py:46
  4.5 0.7 %collective-permute-start.1 = (f32[128,512]{1,0:T(8,128)S(1)}, f32[128,512]{1,0:T(8,128)S(1)}, u32[]{:S(2)}, u32[]{:S(2)}) collective-permute-start(f32[128,512]{1,0:T(8,128)S(1)} %get-tuple-element.31), channel_id=1, source_target_pairs={{8,16},{9,17},{10,18},{11,19},{4,5},{5,6},{6,7},{7,4},{12,13},{13,... | collective-permute-start | bytes 786440 | tf_op jit(solution)/shard_map/ppermute | solution.py:46
  5.2 0.7 %collective-permute-start.2 = (f32[128,512]{1,0:T(8,128)S(1)}, f32[128,512]{1,0:T(8,128)S(1)}, u32[]{:S(2)}, u32[]{:S(2)}) collective-permute-start(f32[128,512]{1,0:T(8,128)S(1)} %get-tuple-element.32), channel_id=1, source_target_pairs={{8,24},{9,25},{10,26},{11,27}} | collective-permute-start | bytes 786440 | tf_op jit(solution)/shard_map/ppermute | solution.py:44
  5.9 0.7 %collective-permute-start.5 = (f32[128,512]{1,0:T(8,128)S(1)}, f32[128,512]{1,0:T(8,128)S(1)}, u32[]{:S(2)}, u32[]{:S(2)}) collective-permute-start(f32[128,512]{1,0:T(8,128)S(1)} %get-tuple-element.25), channel_id=1, source_target_pairs={{8,24},{9,25},{10,26},{11,27}} | collective-permute-start | bytes 786440 | tf_op jit(solution)/shard_map/ppermute | solution.py:44
  6.6 3.9 %collective-permute-done = f32[128,512]{1,0:T(8,128)S(1)} collective-permute-done((f32[128,512]{1,0:T(8,128)S(1)}, f32[128,512]{1,0:T(8,128)S(1)}, u32[]{:S(2)}, u32[]{:S(2)}) %collective-permute-start) | collective-permute-done | bytes 262176 | tf_op jit(solution)/shard_map/ppermute | solution.py:46
  10.5 0.7 %collective-permute-start.4 = (f32[128,512]{1,0:T(8,128)S(1)}, f32[128,512]{1,0:T(8,128)S(1)}, u32[]{:S(2)}, u32[]{:S(2)}) collective-permute-start(f32[128,512]{1,0:T(8,128)S(1)} %get-tuple-element.25), channel_id=1, source_target_pairs={{8,16},{9,17},{10,18},{11,19}} | collective-permute-start | bytes 786440 | tf_op jit(solution)/shard_map/ppermute | solution.py:44
  11.2 2.1 %collective-permute-done.3 = f32[128,512]{1,0:T(8,128)S(1)} collective-permute-done((f32[128,512]{1,0:T(8,128)S(1)}, f32[128,512]{1,0:T(8,128)S(1)}, u32[]{:S(2)}, u32[]{:S(2)}) %collective-permute-start.3) | collective-permute-done | bytes 262176 | tf_op jit(solution)/shard_map/ppermute | solution.py:46
  13.7 7.5 %collective-permute-start.6 = (f32[384,512]{1,0:T(8,128)S(1)}, f32[384,512]{1,0:T(8,128)S(1)}, u32[]{:S(2)}, u32[]{:S(2)}) collective-permute-start(f32[384,512]{1,0:T(8,128)S(1)} %maximum_select_fusion), channel_id=1, source_target_pairs={{0,4},{4,0},{8,12},{12,8},{16,20},{20,16},{24,28},{28,24},{1,5},{5... | collective-permute-start | bytes 2359304 | tf_op jit(solution)/shard_map/ppermute | solution.py:99
  22.4 0.8 %collective-permute-done.6 = f32[384,512]{1,0:T(8,128)S(1)} collective-permute-done((f32[384,512]{1,0:T(8,128)S(1)}, f32[384,512]{1,0:T(8,128)S(1)}, u32[]{:S(2)}, u32[]{:S(2)}) %collective-permute-start.6) | collective-permute-done | bytes 786464 | tf_op jit(solution)/shard_map/ppermute | solution.py:99
  24.5 1.0 %collective-permute-start.9 = (f32[512,128]{0,1:T(8,128)S(1)}, f32[512,128]{0,1:T(8,128)S(1)}, u32[]{:S(2)}, u32[]{:S(2)}) collective-permute-start(f32[512,128]{0,1:T(8,128)S(1)} %fusion.1), channel_id=1, source_target_pairs={{0,1},{1,3},{2,0},{3,2},{4,5},{5,7},{6,4},{7,6},{8,9},{9,11},{10,8... | collective-permute-start | bytes 786440 | tf_op jit(solution)/shard_map/ppermute | solution.py:114
  26.5 5.0 %collective-permute-start.8 = (f32[512,128]{0,1:T(8,128)S(1)}, f32[512,128]{0,1:T(8,128)S(1)}, u32[]{:S(2)}, u32[]{:S(2)}) collective-permute-start(f32[512,128]{0,1:T(8,128)S(1)} %fusion.2), channel_id=1, source_target_pairs={{0,3},{3,0},{4,7},{7,4},{8,11},{11,8},{12,15},{15,12},{16,19},{19,... | collective-permute-start | bytes 786440 | tf_op jit(solution)/shard_map/ppermute | solution.py:116
  32.5 1.5 %collective-permute-done.9 = f32[512,128]{0,1:T(8,128)S(1)} collective-permute-done((f32[512,128]{0,1:T(8,128)S(1)}, f32[512,128]{0,1:T(8,128)S(1)}, u32[]{:S(2)}, u32[]{:S(2)}) %collective-permute-start.9) | collective-permute-done | bytes 262176 | tf_op jit(solution)/shard_map/ppermute | solution.py:114
  34.1 1.4 %collective-permute-start.10 = (f32[512,128]{0,1:T(8,128)S(1)}, f32[512,128]{0,1:T(8,128)}, u32[]{:S(2)}, u32[]{:S(2)}) collective-permute-start(f32[512,128]{0,1:T(8,128)S(1)} %add.92), channel_id=1, source_target_pairs={{1,2},{2,1},{5,6},{6,5},{9,10},{10,9},{13,14},{14,13},{17,18},{18,... | collective-permute-start | bytes 786440 | tf_op jit(solution)/shard_map/ppermute | solution.py:119
  36.2 5.2 %collective-permute-done.8 = f32[512,128]{0,1:T(8,128)S(1)} collective-permute-done((f32[512,128]{0,1:T(8,128)S(1)}, f32[512,128]{0,1:T(8,128)S(1)}, u32[]{:S(2)}, u32[]{:S(2)}) %collective-permute-start.8) | collective-permute-done | bytes 262176 | tf_op jit(solution)/shard_map/ppermute | solution.py:116
  41.4 4.7 %collective-permute-done.7 = f32[512,128]{0,1:T(8,128)} collective-permute-done((f32[512,128]{0,1:T(8,128)S(1)}, f32[512,128]{0,1:T(8,128)}, u32[]{:S(2)}, u32[]{:S(2)}) %collective-permute-start.7) | collective-permute-done | bytes 262176 | tf_op jit(solution)/shard_map/ppermute | solution.py:118
  46.1 1.5 %multiply_reduce_fusion.1 = (f32[512]{0:T(512)S(1)}, f32[512,128]{0,1:T(8,128)S(1)}) fusion(f32[512,128]{0,1:T(8,128)S(1)} %collective-permute-done.9, pred[]{:T(512)S(6)} %or.3, f32[512,128]{0,1:T(8,128)} %collective-permute-done.10, f32[512,128]{0,1:T(8,128)S(1)} %collective-permute-done.8, f32[512,128]{0,1:T(8,128)} %collective-permute-done.7, ...), kind=kOutput, calls=%fused_computation.30 | convolution fusion | flops 101187072 | bytes 2230273 | tf_op jit(solution)/shard_map/dot_general | solution.py:14
  47.6 0.7 %copy-done.4 = f32[128,32]{0,1:T(8,128)S(1)} copy-done((f32[128,32]{0,1:T(8,128)S(1)}, f32[128,32]{0,1:T(8,128)}, u32[]{:S(2)}) %copy-start.4) | copy-done | bytes 16408
  48.5 0.8 %copy.8 = f32[32,1,1024]{2,1,0:T(1,128)} copy(f32[32,1,1024]{2,0,1:T(8,128)S(1)} %maximum_bitcast_fusion) | data formatting | bytes 262144 | tf_op jit(solution)/shard_map/all_to_all | solution.py:125
  49.3 4.2 %all-to-all-start = ((f32[32,1,1024]{2,1,0:T(1,128)}), f32[32,1,1024]{2,1,0:T(1,128)S(1)}, u32[]{:S(2)}, u32[]{:S(2)}) async-start(f32[32,1,1024]{2,1,0:T(1,128)} %copy.8), calls=%async_computation | async-start | bytes 262144 | tf_op jit(solution)/shard_map/all_to_all | solution.py:125
  53.5 0.8 %copy.9 = f32[512,128]{1,0:T(8,128)} copy(f32[512,128]{0,1:T(8,128)S(1)} %get-tuple-element.40) | data formatting | bytes 524288
  54.3 7.4 %all-to-all-done = f32[32,1,1024]{2,1,0:T(1,128)S(1)} async-done(((f32[32,1,1024]{2,1,0:T(1,128)}), f32[32,1,1024]{2,1,0:T(1,128)S(1)}, u32[]{:S(2)}, u32[]{:S(2)}) %all-to-all-start) | async-done | bytes 131104 | tf_op jit(solution)/shard_map/all_to_all | solution.py:125
  61.8 0.8 %multiply_add_fusion = f32[1,4096]{1,0:T(1,128)} fusion(f32[1,4096]{1,0:T(1,128)S(1)} %bitcast.51), kind=kLoop, calls=%fused_computation.49 | loop fusion | flops 36864 | bytes 32768 | tf_op jit(solution)/shard_map/add | solution.py:72
  (46 shorter events, 5.9 us)
Async XLA Ops:
  0.6 20.7 %copy-start = (f32[512,128]{1,0:T(8,128)S(1)}, f32[512,128]{1,0:T(8,128)}, u32[]{:S(2)}) copy-start(f32[512,128]{1,0:T(8,128)} %param.5) | copy-start | bytes 786436
  0.7 1.1 %copy-start.2 = (f32[128,512]{1,0:T(8,128)S(1)}, f32[128,512]{1,0:T(8,128)}, u32[]{:S(2)}) copy-start(f32[128,512]{1,0:T(8,128)} %param.9) | copy-start | bytes 786436
  1.9 8.6 %collective-permute-start = (f32[128,512]{1,0:T(8,128)S(1)}, f32[128,512]{1,0:T(8,128)S(1)}, u32[]{:S(2)}, u32[]{:S(2)}) collective-permute-start(f32[128,512]{1,0:T(8,128)S(1)} %get-tuple-element.31), channel_id=1, source_target_pairs={{8,0},{9,1},{10,2},{11,3},{4,7},{5,4},{6,5},{7,6},{12,15},{13,12},... | collective-permute-start | bytes 786440 | tf_op jit(solution)/shard_map/ppermute | solution.py:46
  3.2 10.1 %collective-permute-start.3 = (f32[128,512]{1,0:T(8,128)S(1)}, f32[128,512]{1,0:T(8,128)S(1)}, u32[]{:S(2)}, u32[]{:S(2)}) collective-permute-start(f32[128,512]{1,0:T(8,128)S(1)} %get-tuple-element.24), channel_id=1, source_target_pairs={{8,0},{9,1},{10,2},{11,3},{4,6},{5,7},{6,4},{7,5},{12,14},{13,15},... | collective-permute-start | bytes 786440 | tf_op jit(solution)/shard_map/ppermute | solution.py:46
  4.5 8.8 %collective-permute-start.1 = (f32[128,512]{1,0:T(8,128)S(1)}, f32[128,512]{1,0:T(8,128)S(1)}, u32[]{:S(2)}, u32[]{:S(2)}) collective-permute-start(f32[128,512]{1,0:T(8,128)S(1)} %get-tuple-element.31), channel_id=1, source_target_pairs={{8,16},{9,17},{10,18},{11,19},{4,5},{5,6},{6,7},{7,4},{12,13},{13,... | collective-permute-start | bytes 786440 | tf_op jit(solution)/shard_map/ppermute | solution.py:46
  5.2 8.1 %collective-permute-start.2 = (f32[128,512]{1,0:T(8,128)S(1)}, f32[128,512]{1,0:T(8,128)S(1)}, u32[]{:S(2)}, u32[]{:S(2)}) collective-permute-start(f32[128,512]{1,0:T(8,128)S(1)} %get-tuple-element.32), channel_id=1, source_target_pairs={{8,24},{9,25},{10,26},{11,27}} | collective-permute-start | bytes 786440 | tf_op jit(solution)/shard_map/ppermute | solution.py:44
  5.9 7.5 %collective-permute-start.5 = (f32[128,512]{1,0:T(8,128)S(1)}, f32[128,512]{1,0:T(8,128)S(1)}, u32[]{:S(2)}, u32[]{:S(2)}) collective-permute-start(f32[128,512]{1,0:T(8,128)S(1)} %get-tuple-element.25), channel_id=1, source_target_pairs={{8,24},{9,25},{10,26},{11,27}} | collective-permute-start | bytes 786440 | tf_op jit(solution)/shard_map/ppermute | solution.py:44
  10.5 3.0 %collective-permute-start.4 = (f32[128,512]{1,0:T(8,128)S(1)}, f32[128,512]{1,0:T(8,128)S(1)}, u32[]{:S(2)}, u32[]{:S(2)}) collective-permute-start(f32[128,512]{1,0:T(8,128)S(1)} %get-tuple-element.25), channel_id=1, source_target_pairs={{8,16},{9,17},{10,18},{11,19}} | collective-permute-start | bytes 786440 | tf_op jit(solution)/shard_map/ppermute | solution.py:44
  13.7 7.8 %copy-start.1 = (f32[512,256]{1,0:T(8,128)S(1)}, f32[512,256]{1,0:T(8,128)}, u32[]{:S(2)}) copy-start(f32[512,256]{1,0:T(8,128)} %param.6) | copy-start | bytes 1572868
  13.7 9.5 %collective-permute-start.6 = (f32[384,512]{1,0:T(8,128)S(1)}, f32[384,512]{1,0:T(8,128)S(1)}, u32[]{:S(2)}, u32[]{:S(2)}) collective-permute-start(f32[384,512]{1,0:T(8,128)S(1)} %maximum_select_fusion), channel_id=1, source_target_pairs={{0,4},{4,0},{8,12},{12,8},{16,20},{20,16},{24,28},{28,24},{1,5},{5... | collective-permute-start | bytes 2359304 | tf_op jit(solution)/shard_map/ppermute | solution.py:99
  21.3 0.8 %copy-start.3 = (f32[256,32]{0,1:T(8,128)S(1)}, f32[256,32]{0,1:T(8,128)}, u32[]{:S(2)}) copy-start(f32[256,32]{0,1:T(8,128)} %param.7) | copy-start | bytes 98308
  24.5 9.5 %collective-permute-start.9 = (f32[512,128]{0,1:T(8,128)S(1)}, f32[512,128]{0,1:T(8,128)S(1)}, u32[]{:S(2)}, u32[]{:S(2)}) collective-permute-start(f32[512,128]{0,1:T(8,128)S(1)} %fusion.1), channel_id=1, source_target_pairs={{0,1},{1,3},{2,0},{3,2},{4,5},{5,7},{6,4},{7,6},{8,9},{9,11},{10,8... | collective-permute-start | bytes 786440 | tf_op jit(solution)/shard_map/ppermute | solution.py:114
  26.5 14.9 %collective-permute-start.8 = (f32[512,128]{0,1:T(8,128)S(1)}, f32[512,128]{0,1:T(8,128)S(1)}, u32[]{:S(2)}, u32[]{:S(2)}) collective-permute-start(f32[512,128]{0,1:T(8,128)S(1)} %fusion.2), channel_id=1, source_target_pairs={{0,3},{3,0},{4,7},{7,4},{8,11},{11,8},{12,15},{15,12},{16,19},{19,... | collective-permute-start | bytes 786440 | tf_op jit(solution)/shard_map/ppermute | solution.py:116
  32.5 13.6 %collective-permute-start.7 = (f32[512,128]{0,1:T(8,128)S(1)}, f32[512,128]{0,1:T(8,128)}, u32[]{:S(2)}, u32[]{:S(2)}) collective-permute-start(f32[512,128]{0,1:T(8,128)S(1)} %fusion.3), channel_id=1, source_target_pairs={{0,1},{1,0},{2,3},{3,2},{4,5},{5,4},{6,7},{7,6},{8,9},{9,8},{10,11... | collective-permute-start | bytes 786440 | tf_op jit(solution)/shard_map/ppermute | solution.py:118
  34.1 12.0 %collective-permute-start.10 = (f32[512,128]{0,1:T(8,128)S(1)}, f32[512,128]{0,1:T(8,128)}, u32[]{:S(2)}, u32[]{:S(2)}) collective-permute-start(f32[512,128]{0,1:T(8,128)S(1)} %add.92), channel_id=1, source_target_pairs={{1,2},{2,1},{5,6},{6,5},{9,10},{10,9},{13,14},{14,13},{17,18},{18,... | collective-permute-start | bytes 786440 | tf_op jit(solution)/shard_map/ppermute | solution.py:119
  47.6 0.7 %copy-start.4 = (f32[128,32]{0,1:T(8,128)S(1)}, f32[128,32]{0,1:T(8,128)}, u32[]{:S(2)}) copy-start(f32[128,32]{0,1:T(8,128)} %param.8) | copy-start | bytes 49156
  49.3 12.4 %all-to-all-start = ((f32[32,1,1024]{2,1,0:T(1,128)}), f32[32,1,1024]{2,1,0:T(1,128)S(1)}, u32[]{:S(2)}, u32[]{:S(2)}) async-start(f32[32,1,1024]{2,1,0:T(1,128)} %copy.8), calls=%async_computation | async-start | bytes 262144 | tf_op jit(solution)/shard_map/all_to_all | solution.py:125

commit v5 on v4

--- a/solution.py
+++ b/solution.py
@@ -90,6 +90,9 @@
     )
     rows = dict(zip(far, lax.optimization_barrier(tuple(rows))))
 
+    draws = lax.optimization_barrier(jnp.concatenate([draws_prev, draws_panel]))
+    samples_prev = contract(draws[:depth], factor_prev, 0, 1)
+
     even = narrow_place % 2 == 0
     own_rows = jnp.concatenate(
         [rows[2], jnp.where(even, rows[1], rows[3]), jnp.where(even, rows[3], rows[1])]
@@ -113,13 +116,17 @@
     two_on, pivot = turn_part(0, pivot)
     two_on = lax.ppermute(two_on, "narrow", [(0, 1), (1, 3), (2, 0), (3, 2)])
     across, pivot = turn_part(1, pivot)
+    beside, pivot = turn_part(2, pivot)
+    across, beside = lax.optimization_barrier((across, beside))
     outer = lax.ppermute(across, "narrow", [(0, 3), (3, 0)])
-    beside, pivot = turn_part(2, pivot)
     beside = lax.ppermute(beside, "narrow", [(0, 1), (1, 0), (2, 3), (3, 2)])
-    inner = lax.ppermute(across + two_on, "narrow", [(1, 2), (2, 1)])
-    panel_factor = part(diag_inverse, pivot) + beside + outer + inner + jnp.where(end, two_on, 0.0)
+    inner = across + two_on
+    inner, two_on, pivot = lax.optimization_barrier((inner, two_on, pivot))
+    inner = lax.ppermute(inner, "narrow", [(1, 2), (2, 1)])
+    parts = part(diag_inverse, pivot) + jnp.where(end, two_on, 0.0) + beside + outer
+    panel_factor = lax.optimization_barrier(parts) + inner
 
-    samples = contract(draws_prev, factor_prev, 0, 1) + contract(draws_panel, panel_factor, 0, 1)
+    samples = samples_prev + contract(draws[depth:], panel_factor, 0, 1)
     squares = jnp.sum(factor_prev * factor_prev, axis=1) + jnp.sum(panel_factor * panel_factor, axis=1)
     outgoing = jnp.concatenate([samples, jnp.broadcast_to(squares[None, :], samples.shape)], axis=1)
     incoming = lax.all_to_all(outgoing, ("narrow", "wide"), split_axis=0, concat_axis=0, tiled=True)

time: 63.1 us -> 61.9 us (0.981)
  local copies, waits for them, and re-layouts: 4 us -> 2.86 us
  matrix products: 5.83 us -> 4.76 us
  waiting for transfers between devices: 25.6 us -> 26.5 us
    unnamed x12, local copies, waits for them, and re-layouts: 2.04 us -> 0.9 us
    dot_general x14, matrix products: 5.83 us -> 4.76 us  [contract(): lax.dot_general(left_side, right_side, (((left_dim,), (right_dim,)), ((),...]
    ppermute x1, waiting for transfers between devices: 1.51 us -> 2.52 us  [per_device(): two_on = lax.ppermute(two_on, 'narrow', [(0, 1), (1, 3), (2, 0), (3, 2)])]
    all_to_all x1, starting transfers between devices: 4.16 us -> 4.99 us  [per_device(): lax.all_to_all(outgoing, ('narrow', 'wide'), split_axis=0, concat_axis=0,...]
    ppermute x1, waiting for transfers between devices: 4.71 us -> 3.95 us  [per_device(): beside = lax.ppermute(beside, 'narrow', [(0, 1), (1, 0), (2, 3), (3, 2)])]
    ppermute x1, starting transfers between devices: 1.37 us -> 0.68 us  [per_device(): inner = lax.ppermute(inner, 'narrow', [(1, 2), (2, 1)])]
  transfers between devices with their start and end apart: 12 -> 12, of which waited for: 7 -> 7; matrix products, arithmetic and copies ran while one was open for 7% -> 6% of each run, Pallas kernels for 0% -> 0%
where the time goes in v5:
time: 61.9 us; the launch traced here: 61.6 us
  waiting for transfers between devices  26.5 us (43%)
  starting transfers between devices  24.5 us (40%)
  matrix products  4.76 us (8%)
  local copies, waits for them, and re-layouts  2.86 us (5%)
  other arithmetic  1.94 us (3%)
  between operations  1.08 us (2%)
    ppermute x1, starting transfers between devices, per_device(): swapped = lax.ppermute(pieces, 'wide', [(i, i ^ 1) for i in range(wide)])  7.54 us
    all_to_all x1, waiting for transfers between devices, per_device(): lax.all_to_all(outgoing, ('narrow', 'wide'), split_axis=0, concat_axis=0,...  7.39 us
    ppermute x3, waiting for transfers between devices, send(): lax.ppermute(jnp.where(on_core, value, rider), ('wide', 'narrow'), pairs...  6.03 us
    ppermute x1, waiting for transfers between devices, per_device(): outer = lax.ppermute(across, 'narrow', [(0, 3), (3, 0)])  5.49 us
    ppermute x1, starting transfers between devices, per_device(): outer = lax.ppermute(across, 'narrow', [(0, 3), (3, 0)])  5 us
    all_to_all x1, starting transfers between devices, per_device(): lax.all_to_all(outgoing, ('narrow', 'wide'), split_axis=0, concat_axis=0,...  4.99 us
    dot_general x14, matrix products, contract(): lax.dot_general(left_side, right_side, (((left_dim,), (right_dim,)), ((),...  4.76 us
    ppermute x1, waiting for transfers between devices, per_device(): beside = lax.ppermute(beside, 'narrow', [(0, 1), (1, 0), (2, 3), (3, 2)])  3.95 us
  transfers between devices with their start and end apart: 12, of which 7 were waited for; matrix products, arithmetic and copies ran while one was open for 6% of the time, Pallas kernels for 0%

profile of v5, /device:TPU:0, one launch (start us, length us, event | category | flops | bytes accessed | tf_op | source)
XLA Modules:
  0.0 61.6 jit_solution(13780500627456528658)
XLA Ops:
  0.7 1.1 %fusion.29 = (f32[256,256]{1,0:T(8,128)S(1)}, f32[256,256]{1,0:T(8,128)S(1)}) fusion(f32[512,256]{1,0:T(8,128)} %param.6), kind=kLoop, calls=%fused_computation.59 | loop fusion | bytes 1048576 | tf_op jit(solution)/shard_map/split | solution.py:25
  1.9 1.3 %collective-permute-start = (f32[128,512]{1,0:T(8,128)S(1)}, f32[128,512]{1,0:T(8,128)S(1)}, u32[]{:S(2)}, u32[]{:S(2)}) collective-permute-start(f32[128,512]{1,0:T(8,128)S(1)} %get-tuple-element.43), channel_id=1, source_target_pairs={{8,0},{9,1},{10,2},{11,3},{4,7},{5,4},{6,5},{7,6},{12,15},{13,12},... | collective-permute-start | bytes 786440 | tf_op jit(solution)/shard_map/ppermute | solution.py:46
  3.2 1.3 %collective-permute-start.3 = (f32[128,512]{1,0:T(8,128)S(1)}, f32[128,512]{1,0:T(8,128)S(1)}, u32[]{:S(2)}, u32[]{:S(2)}) collective-permute-start(f32[128,512]{1,0:T(8,128)S(1)} %get-tuple-element.36), channel_id=1, source_target_pairs={{8,0},{9,1},{10,2},{11,3},{4,6},{5,7},{6,4},{7,5},{12,14},{13,15},... | collective-permute-start | bytes 786440 | tf_op jit(solution)/shard_map/ppermute | solution.py:46
  4.5 0.7 %collective-permute-start.1 = (f32[128,512]{1,0:T(8,128)S(1)}, f32[128,512]{1,0:T(8,128)S(1)}, u32[]{:S(2)}, u32[]{:S(2)}) collective-permute-start(f32[128,512]{1,0:T(8,128)S(1)} %get-tuple-element.43), channel_id=1, source_target_pairs={{8,16},{9,17},{10,18},{11,19},{4,5},{5,6},{6,7},{7,4},{12,13},{13,... | collective-permute-start | bytes 786440 | tf_op jit(solution)/shard_map/ppermute | solution.py:46
  5.2 0.7 %collective-permute-start.2 = (f32[128,512]{1,0:T(8,128)S(1)}, f32[128,512]{1,0:T(8,128)S(1)}, u32[]{:S(2)}, u32[]{:S(2)}) collective-permute-start(f32[128,512]{1,0:T(8,128)S(1)} %get-tuple-element.44), channel_id=1, source_target_pairs={{8,24},{9,25},{10,26},{11,27}} | collective-permute-start | bytes 786440 | tf_op jit(solution)/shard_map/ppermute | solution.py:44
  5.9 0.7 %collective-permute-start.5 = (f32[128,512]{1,0:T(8,128)S(1)}, f32[128,512]{1,0:T(8,128)S(1)}, u32[]{:S(2)}, u32[]{:S(2)}) collective-permute-start(f32[128,512]{1,0:T(8,128)S(1)} %get-tuple-element.37), channel_id=1, source_target_pairs={{8,24},{9,25},{10,26},{11,27}} | collective-permute-start | bytes 786440 | tf_op jit(solution)/shard_map/ppermute | solution.py:44
  6.6 3.9 %collective-permute-done = f32[128,512]{1,0:T(8,128)S(1)} collective-permute-done((f32[128,512]{1,0:T(8,128)S(1)}, f32[128,512]{1,0:T(8,128)S(1)}, u32[]{:S(2)}, u32[]{:S(2)}) %collective-permute-start) | collective-permute-done | bytes 262176 | tf_op jit(solution)/shard_map/ppermute | solution.py:46
  10.5 0.7 %collective-permute-start.4 = (f32[128,512]{1,0:T(8,128)S(1)}, f32[128,512]{1,0:T(8,128)S(1)}, u32[]{:S(2)}, u32[]{:S(2)}) collective-permute-start(f32[128,512]{1,0:T(8,128)S(1)} %get-tuple-element.37), channel_id=1, source_target_pairs={{8,16},{9,17},{10,18},{11,19}} | collective-permute-start | bytes 786440 | tf_op jit(solution)/shard_map/ppermute | solution.py:44
  11.2 2.1 %collective-permute-done.3 = f32[128,512]{1,0:T(8,128)S(1)} collective-permute-done((f32[128,512]{1,0:T(8,128)S(1)}, f32[128,512]{1,0:T(8,128)S(1)}, u32[]{:S(2)}, u32[]{:S(2)}) %collective-permute-start.3) | collective-permute-done | bytes 262176 | tf_op jit(solution)/shard_map/ppermute | solution.py:46
  13.8 7.5 %collective-permute-start.6 = (f32[384,512]{1,0:T(8,128)S(1)}, f32[384,512]{1,0:T(8,128)S(1)}, u32[]{:S(2)}, u32[]{:S(2)}) collective-permute-start(f32[384,512]{1,0:T(8,128)S(1)} %maximum_select_fusion), channel_id=1, source_target_pairs={{0,4},{4,0},{8,12},{12,8},{16,20},{20,16},{24,28},{28,24},{1,5},{5... | collective-permute-start | bytes 2359304 | tf_op jit(solution)/shard_map/ppermute | solution.py:102
  22.1 1.1 %collective-permute-done.6 = f32[384,512]{1,0:T(8,128)S(1)} collective-permute-done((f32[384,512]{1,0:T(8,128)S(1)}, f32[384,512]{1,0:T(8,128)S(1)}, u32[]{:S(2)}, u32[]{:S(2)}) %collective-permute-start.6) | collective-permute-done | bytes 786464 | tf_op jit(solution)/shard_map/ppermute | solution.py:102
  25.5 0.9 %collective-permute-start.7 = (f32[512,128]{0,1:T(8,128)S(1)}, f32[512,128]{0,1:T(8,128)S(1)}, u32[]{:S(2)}, u32[]{:S(2)}) collective-permute-start(f32[512,128]{0,1:T(8,128)S(1)} %fusion.2), channel_id=1, source_target_pairs={{0,1},{1,3},{2,0},{3,2},{4,5},{5,7},{6,4},{7,6},{8,9},{9,11},{10,8... | collective-permute-start | bytes 786440 | tf_op jit(solution)/shard_map/ppermute | solution.py:117
  27.5 5.0 %collective-permute-start.9 = (f32[512,128]{0,1:T(8,128)S(1)}, f32[512,128]{0,1:T(8,128)S(1)}, u32[]{:S(2)}, u32[]{:S(2)}) collective-permute-start(f32[512,128]{0,1:T(8,128)S(1)} %fusion.3), channel_id=1, source_target_pairs={{0,3},{3,0},{4,7},{7,4},{8,11},{11,8},{12,15},{15,12},{16,19},{19,... | collective-permute-start | bytes 786440 | tf_op jit(solution)/shard_map/ppermute | solution.py:121
  32.6 2.5 %collective-permute-done.7 = f32[512,128]{0,1:T(8,128)S(1)} collective-permute-done((f32[512,128]{0,1:T(8,128)S(1)}, f32[512,128]{0,1:T(8,128)S(1)}, u32[]{:S(2)}, u32[]{:S(2)}) %collective-permute-start.7) | collective-permute-done | bytes 262176 | tf_op jit(solution)/shard_map/ppermute | solution.py:117
  35.1 0.6 fusion.35
  35.7 0.7 %collective-permute-start.10 = (f32[512,128]{0,1:T(8,128)S(1)}, f32[512,128]{0,1:T(8,128)S(1)}, u32[]{:S(2)}, u32[]{:S(2)}) collective-permute-start(f32[512,128]{0,1:T(8,128)S(1)} %add.90), channel_id=1, source_target_pairs={{1,2},{2,1},{5,6},{6,5},{9,10},{10,9},{13,14},{14,13},{17,18},{18,... | collective-permute-start | bytes 786440 | tf_op jit(solution)/shard_map/ppermute | solution.py:125
  36.4 0.4 fusion
  36.9 5.5 %collective-permute-done.9 = f32[512,128]{0,1:T(8,128)S(1)} collective-permute-done((f32[512,128]{0,1:T(8,128)S(1)}, f32[512,128]{0,1:T(8,128)S(1)}, u32[]{:S(2)}, u32[]{:S(2)}) %collective-permute-start.9) | collective-permute-done | bytes 262176 | tf_op jit(solution)/shard_map/ppermute | solution.py:121
  42.4 3.9 %collective-permute-done.8 = f32[512,128]{0,1:T(8,128)S(1)} collective-permute-done((f32[512,128]{0,1:T(8,128)S(1)}, f32[512,128]{0,1:T(8,128)S(1)}, u32[]{:S(2)}, u32[]{:S(2)}) %collective-permute-start.8) | collective-permute-done | bytes 262176 | tf_op jit(solution)/shard_map/ppermute | solution.py:122
  46.7 0.8 %copy.8 = f32[32,1,1024]{2,1,0:T(1,128)} copy(f32[32,1,1024]{2,0,1:T(8,128)S(1)} %maximum_bitcast_fusion) | data formatting | bytes 262144 | tf_op jit(solution)/shard_map/all_to_all | solution.py:132
  47.5 5.0 %all-to-all-start = ((f32[32,1,1024]{2,1,0:T(1,128)}), f32[32,1,1024]{2,1,0:T(1,128)S(1)}, u32[]{:S(2)}, u32[]{:S(2)}) async-start(f32[32,1,1024]{2,1,0:T(1,128)} %copy.8), calls=%async_computation | async-start | bytes 262144 | tf_op jit(solution)/shard_map/all_to_all | solution.py:132
  52.5 0.8 %copy.9 = f32[512,128]{1,0:T(8,128)} copy(f32[512,128]{0,1:T(8,128)S(1)} %get-tuple-element.35) | data formatting | bytes 524288
  53.3 7.4 %all-to-all-done = f32[32,1,1024]{2,1,0:T(1,128)S(1)} async-done(((f32[32,1,1024]{2,1,0:T(1,128)}), f32[32,1,1024]{2,1,0:T(1,128)S(1)}, u32[]{:S(2)}, u32[]{:S(2)}) %all-to-all-start) | async-done | bytes 131104 | tf_op jit(solution)/shard_map/all_to_all | solution.py:132
  60.8 0.8 %multiply_add_fusion = f32[1,4096]{1,0:T(1,128)} fusion(f32[1,4096]{1,0:T(1,128)S(1)} %bitcast.37), kind=kLoop, calls=%fused_computation.49 | loop fusion | flops 36864 | bytes 32768 | tf_op jit(solution)/shard_map/add | solution.py:72
  (49 shorter events, 5.0 us)
Async XLA Ops:
  0.6 20.9 %copy-start = (f32[512,128]{1,0:T(8,128)S(1)}, f32[512,128]{1,0:T(8,128)}, u32[]{:S(2)}) copy-start(f32[512,128]{1,0:T(8,128)} %param.5) | copy-start | bytes 786436
  0.7 1.1 %copy-start.2 = (f32[128,512]{1,0:T(8,128)S(1)}, f32[128,512]{1,0:T(8,128)}, u32[]{:S(2)}) copy-start(f32[128,512]{1,0:T(8,128)} %param.9) | copy-start | bytes 786436
  1.9 8.6 %collective-permute-start = (f32[128,512]{1,0:T(8,128)S(1)}, f32[128,512]{1,0:T(8,128)S(1)}, u32[]{:S(2)}, u32[]{:S(2)}) collective-permute-start(f32[128,512]{1,0:T(8,128)S(1)} %get-tuple-element.43), channel_id=1, source_target_pairs={{8,0},{9,1},{10,2},{11,3},{4,7},{5,4},{6,5},{7,6},{12,15},{13,12},... | collective-permute-start | bytes 786440 | tf_op jit(solution)/shard_map/ppermute | solution.py:46
  3.2 10.1 %collective-permute-start.3 = (f32[128,512]{1,0:T(8,128)S(1)}, f32[128,512]{1,0:T(8,128)S(1)}, u32[]{:S(2)}, u32[]{:S(2)}) collective-permute-start(f32[128,512]{1,0:T(8,128)S(1)} %get-tuple-element.36), channel_id=1, source_target_pairs={{8,0},{9,1},{10,2},{11,3},{4,6},{5,7},{6,4},{7,5},{12,14},{13,15},... | collective-permute-start | bytes 786440 | tf_op jit(solution)/shard_map/ppermute | solution.py:46
  4.5 8.8 %collective-permute-start.1 = (f32[128,512]{1,0:T(8,128)S(1)}, f32[128,512]{1,0:T(8,128)S(1)}, u32[]{:S(2)}, u32[]{:S(2)}) collective-permute-start(f32[128,512]{1,0:T(8,128)S(1)} %get-tuple-element.43), channel_id=1, source_target_pairs={{8,16},{9,17},{10,18},{11,19},{4,5},{5,6},{6,7},{7,4},{12,13},{13,... | collective-permute-start | bytes 786440 | tf_op jit(solution)/shard_map/ppermute | solution.py:46
  5.2 8.1 %collective-permute-start.2 = (f32[128,512]{1,0:T(8,128)S(1)}, f32[128,512]{1,0:T(8,128)S(1)}, u32[]{:S(2)}, u32[]{:S(2)}) collective-permute-start(f32[128,512]{1,0:T(8,128)S(1)} %get-tuple-element.44), channel_id=1, source_target_pairs={{8,24},{9,25},{10,26},{11,27}} | collective-permute-start | bytes 786440 | tf_op jit(solution)/shard_map/ppermute | solution.py:44
  5.9 7.5 %collective-permute-start.5 = (f32[128,512]{1,0:T(8,128)S(1)}, f32[128,512]{1,0:T(8,128)S(1)}, u32[]{:S(2)}, u32[]{:S(2)}) collective-permute-start(f32[128,512]{1,0:T(8,128)S(1)} %get-tuple-element.37), channel_id=1, source_target_pairs={{8,24},{9,25},{10,26},{11,27}} | collective-permute-start | bytes 786440 | tf_op jit(solution)/shard_map/ppermute | solution.py:44
  10.5 3.0 %collective-permute-start.4 = (f32[128,512]{1,0:T(8,128)S(1)}, f32[128,512]{1,0:T(8,128)S(1)}, u32[]{:S(2)}, u32[]{:S(2)}) collective-permute-start(f32[128,512]{1,0:T(8,128)S(1)} %get-tuple-element.37), channel_id=1, source_target_pairs={{8,16},{9,17},{10,18},{11,19}} | collective-permute-start | bytes 786440 | tf_op jit(solution)/shard_map/ppermute | solution.py:44
  13.6 7.7 %copy-start.3 = (f32[256,32]{0,1:T(8,128)S(1)}, f32[256,32]{0,1:T(8,128)}, u32[]{:S(2)}) copy-start(f32[256,32]{0,1:T(8,128)} %param.7) | copy-start | bytes 98308
  13.6 7.7 %copy-start.4 = (f32[128,32]{0,1:T(8,128)S(1)}, f32[128,32]{0,1:T(8,128)}, u32[]{:S(2)}) copy-start(f32[128,32]{0,1:T(8,128)} %param.8) | copy-start | bytes 49156
  13.6 7.7 %copy-start.1 = (f32[512,256]{1,0:T(8,128)S(1)}, f32[512,256]{1,0:T(8,128)}, u32[]{:S(2)}) copy-start(f32[512,256]{1,0:T(8,128)} %param.6) | copy-start | bytes 1572868
  13.8 9.5 %collective-permute-start.6 = (f32[384,512]{1,0:T(8,128)S(1)}, f32[384,512]{1,0:T(8,128)S(1)}, u32[]{:S(2)}, u32[]{:S(2)}) collective-permute-start(f32[384,512]{1,0:T(8,128)S(1)} %maximum_select_fusion), channel_id=1, source_target_pairs={{0,4},{4,0},{8,12},{12,8},{16,20},{20,16},{24,28},{28,24},{1,5},{5... | collective-permute-start | bytes 2359304 | tf_op jit(solution)/shard_map/ppermute | solution.py:102
  25.5 9.5 %collective-permute-start.7 = (f32[512,128]{0,1:T(8,128)S(1)}, f32[512,128]{0,1:T(8,128)S(1)}, u32[]{:S(2)}, u32[]{:S(2)}) collective-permute-start(f32[512,128]{0,1:T(8,128)S(1)} %fusion.2), channel_id=1, source_target_pairs={{0,1},{1,3},{2,0},{3,2},{4,5},{5,7},{6,4},{7,6},{8,9},{9,11},{10,8... | collective-permute-start | bytes 786440 | tf_op jit(solution)/shard_map/ppermute | solution.py:117
  27.5 14.9 %collective-permute-start.9 = (f32[512,128]{0,1:T(8,128)S(1)}, f32[512,128]{0,1:T(8,128)S(1)}, u32[]{:S(2)}, u32[]{:S(2)}) collective-permute-start(f32[512,128]{0,1:T(8,128)S(1)} %fusion.3), channel_id=1, source_target_pairs={{0,3},{3,0},{4,7},{7,4},{8,11},{11,8},{12,15},{15,12},{16,19},{19,... | collective-permute-start | bytes 786440 | tf_op jit(solution)/shard_map/ppermute | solution.py:121
  32.5 13.8 %collective-permute-start.8 = (f32[512,128]{0,1:T(8,128)S(1)}, f32[512,128]{0,1:T(8,128)S(1)}, u32[]{:S(2)}, u32[]{:S(2)}) collective-permute-start(f32[512,128]{0,1:T(8,128)S(1)} %fusion.1), channel_id=1, source_target_pairs={{0,1},{1,0},{2,3},{3,2},{4,5},{5,4},{6,7},{7,6},{8,9},{9,8},{10,11... | collective-permute-start | bytes 786440 | tf_op jit(solution)/shard_map/ppermute | solution.py:122
  35.7 10.7 %collective-permute-start.10 = (f32[512,128]{0,1:T(8,128)S(1)}, f32[512,128]{0,1:T(8,128)S(1)}, u32[]{:S(2)}, u32[]{:S(2)}) collective-permute-start(f32[512,128]{0,1:T(8,128)S(1)} %add.90), channel_id=1, source_target_pairs={{1,2},{2,1},{5,6},{6,5},{9,10},{10,9},{13,14},{14,13},{17,18},{18,... | collective-permute-start | bytes 786440 | tf_op jit(solution)/shard_map/ppermute | solution.py:125
  47.5 13.2 %all-to-all-start = ((f32[32,1,1024]{2,1,0:T(1,128)}), f32[32,1,1024]{2,1,0:T(1,128)S(1)}, u32[]{:S(2)}, u32[]{:S(2)}) async-start(f32[32,1,1024]{2,1,0:T(1,128)} %copy.8), calls=%async_computation | async-start | bytes 262144 | tf_op jit(solution)/shard_map/all_to_all | solution.py:132

commit v6 on v5

--- a/solution.py
+++ b/solution.py
@@ -50,11 +50,17 @@
     while (1 << shift) < wide:
         low, high, both = 1 << shift, 2 << shift, 3 << shift
         top, bottom = packed[:half], packed[half:]
-        tops, bottoms = [send(top, low)], [send(bottom, low)]
+        got = {}
         if high < wide:
-            for flip in (both, high):
-                tops.append(send(top, flip))
-                bottoms.append(send(bottom, flip))
+            got['TL'] = send(top, low)
+            got['TD'] = send(top, both)
+            got['TH'] = send(top, high)
+            got['BD'] = send(bottom, both)
+            got['BL'] = send(bottom, low)
+            got['BH'] = send(bottom, high)
+            tops, bottoms = [got['TD'], got['TL'], got['TH']], [got['BD'], got['BL'], got['BH']]
+        else:
+            tops, bottoms = [send(top, low)], [send(bottom, low)]
         held = held + jnp.concatenate([sum(tops), sum(bottoms)])
         holders = [h ^ f for h in holders for f in (0, low, high, both)[: 1 + len(tops)]]
         packed = held

time: 61.9 us -> 61 us (0.985)
  starting transfers between devices: 24.5 us -> 17.1 us
  waiting for transfers between devices: 26.5 us -> 33 us
    ppermute x3, waiting for transfers between devices: 0.01 us -> 8.1 us  [send(): return lax.ppermute(value, ('wide', 'narrow'), pairs)]
    ppermute x1, starting transfers between devices: 7.54 us -> 0.96 us  [per_device(): swapped = lax.ppermute(pieces, 'wide', [(i, i ^ 1) for i in range(wide)])]
    ppermute x3, waiting for transfers between devices: 6.03 us -> 4.51 us  [send(): lax.ppermute(jnp.where(on_core, value, rider), ('wide', 'narrow'), pairs...]
    all_to_all x1, starting transfers between devices: 4.99 us -> 4.14 us  [per_device(): lax.all_to_all(outgoing, ('narrow', 'wide'), split_axis=0, concat_axis=0,...]
where the time goes in v6:
time: 61 us; the launch traced here: 60.7 us
  waiting for transfers between devices  33 us (54%)
  starting transfers between devices  17.1 us (28%)
  matrix products  4.75 us (8%)
  local copies, waits for them, and re-layouts  2.85 us (5%)
  other arithmetic  1.87 us (3%)
  between operations  1.1 us (2%)
    ppermute x3, waiting for transfers between devices, send(): return lax.ppermute(value, ('wide', 'narrow'), pairs)  8.1 us
    all_to_all x1, waiting for transfers between devices, per_device(): lax.all_to_all(outgoing, ('narrow', 'wide'), split_axis=0, concat_axis=0,...  7.39 us
    ppermute x1, waiting for transfers between devices, per_device(): outer = lax.ppermute(across, 'narrow', [(0, 3), (3, 0)])  5.49 us
    ppermute x1, starting transfers between devices, per_device(): outer = lax.ppermute(across, 'narrow', [(0, 3), (3, 0)])  4.82 us
    dot_general x14, matrix products, contract(): lax.dot_general(left_side, right_side, (((left_dim,), (right_dim,)), ((),...  4.75 us
    ppermute x3, waiting for transfers between devices, send(): lax.ppermute(jnp.where(on_core, value, rider), ('wide', 'narrow'), pairs...  4.51 us
    all_to_all x1, starting transfers between devices, per_device(): lax.all_to_all(outgoing, ('narrow', 'wide'), split_axis=0, concat_axis=0,...  4.14 us
    ppermute x1, waiting for transfers between devices, per_device(): beside = lax.ppermute(beside, 'narrow', [(0, 1), (1, 0), (2, 3), (3, 2)])  3.95 us
  transfers between devices with their start and end apart: 12, of which 7 were waited for; matrix products, arithmetic and copies ran while one was open for 6% of the time, Pallas kernels for 0%

profile of v6, /device:TPU:0, one launch (start us, length us, event | category | flops | bytes accessed | tf_op | source)
XLA Modules:
  0.0 60.7 jit_solution(7128621623221422329)
XLA Ops:
  0.7 1.1 %fusion.28 = (f32[256,256]{1,0:T(8,128)S(1)}, f32[256,256]{1,0:T(8,128)S(1)}) fusion(f32[512,256]{1,0:T(8,128)} %param.6), kind=kLoop, calls=%fused_computation.58 | loop fusion | bytes 1048576 | tf_op jit(solution)/shard_map/split | solution.py:25
  1.9 1.3 %collective-permute-start.1 = (f32[128,512]{1,0:T(8,128)S(1)}, f32[128,512]{1,0:T(8,128)S(1)}, u32[]{:S(2)}, u32[]{:S(2)}) collective-permute-start(f32[128,512]{1,0:T(8,128)S(1)} %get-tuple-element.42), channel_id=1, source_target_pairs={{8,0},{9,1},{10,2},{11,3},{4,7},{5,4},{6,5},{7,6},{12,15},{13,12},... | collective-permute-start | bytes 786440 | tf_op jit(solution)/shard_map/ppermute | solution.py:46
  3.2 0.7 %collective-permute-start = (f32[128,512]{1,0:T(8,128)S(1)}, f32[128,512]{1,0:T(8,128)S(1)}, u32[]{:S(2)}, u32[]{:S(2)}) collective-permute-start(f32[128,512]{1,0:T(8,128)S(1)} %get-tuple-element.42), channel_id=1, source_target_pairs={{8,16},{9,17},{10,18},{11,19},{4,6},{5,7},{6,4},{7,5},{12,14},{13,... | collective-permute-start | bytes 786440 | tf_op jit(solution)/shard_map/ppermute | solution.py:46
  3.9 0.7 %collective-permute-start.2 = (f32[128,512]{1,0:T(8,128)S(1)}, f32[128,512]{1,0:T(8,128)S(1)}, u32[]{:S(2)}, u32[]{:S(2)}) collective-permute-start(f32[128,512]{1,0:T(8,128)S(1)} %get-tuple-element.42), channel_id=1, source_target_pairs={{8,24},{9,25},{10,26},{11,27},{4,5},{5,6},{6,7},{7,4},{12,13},{13,... | collective-permute-start | bytes 786440 | tf_op jit(solution)/shard_map/ppermute | solution.py:46
  4.5 0.7 %collective-permute-start.5 = (f32[128,512]{1,0:T(8,128)S(1)}, f32[128,512]{1,0:T(8,128)S(1)}, u32[]{:S(2)}, u32[]{:S(2)}) collective-permute-start(f32[128,512]{1,0:T(8,128)S(1)} %get-tuple-element.41), channel_id=1, source_target_pairs={{8,24},{9,25},{10,26},{11,27}} | collective-permute-start | bytes 786440 | tf_op jit(solution)/shard_map/ppermute | solution.py:44
  5.2 0.7 %collective-permute-start.3 = (f32[128,512]{1,0:T(8,128)S(1)}, f32[128,512]{1,0:T(8,128)S(1)}, u32[]{:S(2)}, u32[]{:S(2)}) collective-permute-start(f32[128,512]{1,0:T(8,128)S(1)} %get-tuple-element.41), channel_id=1, source_target_pairs={{8,16},{9,17},{10,18},{11,19}} | collective-permute-start | bytes 786440 | tf_op jit(solution)/shard_map/ppermute | solution.py:44
  5.9 4.5 %collective-permute-done.1 = f32[128,512]{1,0:T(8,128)S(1)} collective-permute-done((f32[128,512]{1,0:T(8,128)S(1)}, f32[128,512]{1,0:T(8,128)S(1)}, u32[]{:S(2)}, u32[]{:S(2)}) %collective-permute-start.1) | collective-permute-done | bytes 262176 | tf_op jit(solution)/shard_map/ppermute | solution.py:46
  10.4 1.3 %collective-permute-start.4 = (f32[128,512]{1,0:T(8,128)S(1)}, f32[128,512]{1,0:T(8,128)S(1)}, u32[]{:S(2)}, u32[]{:S(2)}) collective-permute-start(f32[128,512]{1,0:T(8,128)S(1)} %get-tuple-element.41), channel_id=1, source_target_pairs={{8,0},{9,1},{10,2},{11,3}} | collective-permute-start | bytes 786440 | tf_op jit(solution)/shard_map/ppermute | solution.py:44
  11.9 8.1 %collective-permute-done.4 = f32[128,512]{1,0:T(8,128)S(1)} collective-permute-done((f32[128,512]{1,0:T(8,128)S(1)}, f32[128,512]{1,0:T(8,128)S(1)}, u32[]{:S(2)}, u32[]{:S(2)}) %collective-permute-start.4) | collective-permute-done | bytes 262176 | tf_op jit(solution)/shard_map/ppermute | solution.py:44
  20.3 1.0 %collective-permute-start.6 = (f32[384,512]{1,0:T(8,128)S(1)}, f32[384,512]{1,0:T(8,128)S(1)}, u32[]{:S(2)}, u32[]{:S(2)}) collective-permute-start(f32[384,512]{1,0:T(8,128)S(1)} %maximum_select_fusion), channel_id=1, source_target_pairs={{0,4},{4,0},{8,12},{12,8},{16,20},{20,16},{24,28},{28,24},{1,5},{5... | collective-permute-start | bytes 2359304 | tf_op jit(solution)/shard_map/ppermute | solution.py:108
  22.1 1.1 %collective-permute-done.6 = f32[384,512]{1,0:T(8,128)S(1)} collective-permute-done((f32[384,512]{1,0:T(8,128)S(1)}, f32[384,512]{1,0:T(8,128)S(1)}, u32[]{:S(2)}, u32[]{:S(2)}) %collective-permute-start.6) | collective-permute-done | bytes 786464 | tf_op jit(solution)/shard_map/ppermute | solution.py:108
  25.5 1.1 %collective-permute-start.7 = (f32[512,128]{0,1:T(8,128)S(1)}, f32[512,128]{0,1:T(8,128)S(1)}, u32[]{:S(2)}, u32[]{:S(2)}) collective-permute-start(f32[512,128]{0,1:T(8,128)S(1)} %fusion.2), channel_id=1, source_target_pairs={{0,1},{1,3},{2,0},{3,2},{4,5},{5,7},{6,4},{7,6},{8,9},{9,11},{10,8... | collective-permute-start | bytes 786440 | tf_op jit(solution)/shard_map/ppermute | solution.py:123
  27.6 4.8 %collective-permute-start.9 = (f32[512,128]{0,1:T(8,128)S(1)}, f32[512,128]{0,1:T(8,128)S(1)}, u32[]{:S(2)}, u32[]{:S(2)}) collective-permute-start(f32[512,128]{0,1:T(8,128)S(1)} %fusion.3), channel_id=1, source_target_pairs={{0,3},{3,0},{4,7},{7,4},{8,11},{11,8},{12,15},{15,12},{16,19},{19,... | collective-permute-start | bytes 786440 | tf_op jit(solution)/shard_map/ppermute | solution.py:127
  32.5 2.5 %collective-permute-done.7 = f32[512,128]{0,1:T(8,128)S(1)} collective-permute-done((f32[512,128]{0,1:T(8,128)S(1)}, f32[512,128]{0,1:T(8,128)S(1)}, u32[]{:S(2)}, u32[]{:S(2)}) %collective-permute-start.7) | collective-permute-done | bytes 262176 | tf_op jit(solution)/shard_map/ppermute | solution.py:123
  35.0 0.6 fusion.34
  35.6 0.7 %collective-permute-start.10 = (f32[512,128]{0,1:T(8,128)S(1)}, f32[512,128]{0,1:T(8,128)S(1)}, u32[]{:S(2)}, u32[]{:S(2)}) collective-permute-start(f32[512,128]{0,1:T(8,128)S(1)} %add.90), channel_id=1, source_target_pairs={{1,2},{2,1},{5,6},{6,5},{9,10},{10,9},{13,14},{14,13},{17,18},{18,... | collective-permute-start | bytes 786440 | tf_op jit(solution)/shard_map/ppermute | solution.py:131
  36.3 0.4 fusion
  36.8 5.5 %collective-permute-done.9 = f32[512,128]{0,1:T(8,128)S(1)} collective-permute-done((f32[512,128]{0,1:T(8,128)S(1)}, f32[512,128]{0,1:T(8,128)S(1)}, u32[]{:S(2)}, u32[]{:S(2)}) %collective-permute-start.9) | collective-permute-done | bytes 262176 | tf_op jit(solution)/shard_map/ppermute | solution.py:127
  42.3 4.0 %collective-permute-done.8 = f32[512,128]{0,1:T(8,128)S(1)} collective-permute-done((f32[512,128]{0,1:T(8,128)S(1)}, f32[512,128]{0,1:T(8,128)S(1)}, u32[]{:S(2)}, u32[]{:S(2)}) %collective-permute-start.8) | collective-permute-done | bytes 262176 | tf_op jit(solution)/shard_map/ppermute | solution.py:128
  46.6 0.8 %copy.8 = f32[32,1,1024]{2,1,0:T(1,128)} copy(f32[32,1,1024]{2,0,1:T(8,128)S(1)} %maximum_bitcast_fusion) | data formatting | bytes 262144 | tf_op jit(solution)/shard_map/all_to_all | solution.py:138
  47.4 4.1 %all-to-all-start = ((f32[32,1,1024]{2,1,0:T(1,128)}), f32[32,1,1024]{2,1,0:T(1,128)S(1)}, u32[]{:S(2)}, u32[]{:S(2)}) async-start(f32[32,1,1024]{2,1,0:T(1,128)} %copy.8), calls=%async_computation | async-start | bytes 262144 | tf_op jit(solution)/shard_map/all_to_all | solution.py:138
  51.6 0.8 %copy.9 = f32[512,128]{1,0:T(8,128)} copy(f32[512,128]{0,1:T(8,128)S(1)} %get-tuple-element.35) | data formatting | bytes 524288
  52.4 7.4 %all-to-all-done = f32[32,1,1024]{2,1,0:T(1,128)S(1)} async-done(((f32[32,1,1024]{2,1,0:T(1,128)}), f32[32,1,1024]{2,1,0:T(1,128)S(1)}, u32[]{:S(2)}, u32[]{:S(2)}) %all-to-all-start) | async-done | bytes 131104 | tf_op jit(solution)/shard_map/all_to_all | solution.py:138
  59.9 0.8 %multiply_add_fusion = f32[1,4096]{1,0:T(1,128)} fusion(f32[1,4096]{1,0:T(1,128)S(1)} %bitcast.37), kind=kLoop, calls=%fused_computation.48 | loop fusion | flops 36864 | bytes 32768 | tf_op jit(solution)/shard_map/add | solution.py:78
  (49 shorter events, 4.9 us)
Async XLA Ops:
  0.6 20.8 %copy-start = (f32[512,128]{1,0:T(8,128)S(1)}, f32[512,128]{1,0:T(8,128)}, u32[]{:S(2)}) copy-start(f32[512,128]{1,0:T(8,128)} %param.5) | copy-start | bytes 786436
  0.7 1.1 %copy-start.2 = (f32[128,512]{1,0:T(8,128)S(1)}, f32[128,512]{1,0:T(8,128)}, u32[]{:S(2)}) copy-start(f32[128,512]{1,0:T(8,128)} %param.9) | copy-start | bytes 786436
  1.9 8.6 %collective-permute-start.1 = (f32[128,512]{1,0:T(8,128)S(1)}, f32[128,512]{1,0:T(8,128)S(1)}, u32[]{:S(2)}, u32[]{:S(2)}) collective-permute-start(f32[128,512]{1,0:T(8,128)S(1)} %get-tuple-element.42), channel_id=1, source_target_pairs={{8,0},{9,1},{10,2},{11,3},{4,7},{5,4},{6,5},{7,6},{12,15},{13,12},... | collective-permute-start | bytes 786440 | tf_op jit(solution)/shard_map/ppermute | solution.py:46
  3.2 8.6 %collective-permute-start = (f32[128,512]{1,0:T(8,128)S(1)}, f32[128,512]{1,0:T(8,128)S(1)}, u32[]{:S(2)}, u32[]{:S(2)}) collective-permute-start(f32[128,512]{1,0:T(8,128)S(1)} %get-tuple-element.42), channel_id=1, source_target_pairs={{8,16},{9,17},{10,18},{11,19},{4,6},{5,7},{6,4},{7,5},{12,14},{13,... | collective-permute-start | bytes 786440 | tf_op jit(solution)/shard_map/ppermute | solution.py:46
  3.9 7.9 %collective-permute-start.2 = (f32[128,512]{1,0:T(8,128)S(1)}, f32[128,512]{1,0:T(8,128)S(1)}, u32[]{:S(2)}, u32[]{:S(2)}) collective-permute-start(f32[128,512]{1,0:T(8,128)S(1)} %get-tuple-element.42), channel_id=1, source_target_pairs={{8,24},{9,25},{10,26},{11,27},{4,5},{5,6},{6,7},{7,4},{12,13},{13,... | collective-permute-start | bytes 786440 | tf_op jit(solution)/shard_map/ppermute | solution.py:46
  4.5 7.3 %collective-permute-start.5 = (f32[128,512]{1,0:T(8,128)S(1)}, f32[128,512]{1,0:T(8,128)S(1)}, u32[]{:S(2)}, u32[]{:S(2)}) collective-permute-start(f32[128,512]{1,0:T(8,128)S(1)} %get-tuple-element.41), channel_id=1, source_target_pairs={{8,24},{9,25},{10,26},{11,27}} | collective-permute-start | bytes 786440 | tf_op jit(solution)/shard_map/ppermute | solution.py:44
  5.2 6.6 %collective-permute-start.3 = (f32[128,512]{1,0:T(8,128)S(1)}, f32[128,512]{1,0:T(8,128)S(1)}, u32[]{:S(2)}, u32[]{:S(2)}) collective-permute-start(f32[128,512]{1,0:T(8,128)S(1)} %get-tuple-element.41), channel_id=1, source_target_pairs={{8,16},{9,17},{10,18},{11,19}} | collective-permute-start | bytes 786440 | tf_op jit(solution)/shard_map/ppermute | solution.py:44
  10.4 9.5 %collective-permute-start.4 = (f32[128,512]{1,0:T(8,128)S(1)}, f32[128,512]{1,0:T(8,128)S(1)}, u32[]{:S(2)}, u32[]{:S(2)}) collective-permute-start(f32[128,512]{1,0:T(8,128)S(1)} %get-tuple-element.41), channel_id=1, source_target_pairs={{8,0},{9,1},{10,2},{11,3}} | collective-permute-start | bytes 786440 | tf_op jit(solution)/shard_map/ppermute | solution.py:44
  20.1 1.1 %copy-start.3 = (f32[256,32]{0,1:T(8,128)S(1)}, f32[256,32]{0,1:T(8,128)}, u32[]{:S(2)}) copy-start(f32[256,32]{0,1:T(8,128)} %param.7) | copy-start | bytes 98308
  20.1 1.1 %copy-start.4 = (f32[128,32]{0,1:T(8,128)S(1)}, f32[128,32]{0,1:T(8,128)}, u32[]{:S(2)}) copy-start(f32[128,32]{0,1:T(8,128)} %param.8) | copy-start | bytes 49156
  20.1 1.1 %copy-start.1 = (f32[512,256]{1,0:T(8,128)S(1)}, f32[512,256]{1,0:T(8,128)}, u32[]{:S(2)}) copy-start(f32[512,256]{1,0:T(8,128)} %param.6) | copy-start | bytes 1572868
  20.3 2.9 %collective-permute-start.6 = (f32[384,512]{1,0:T(8,128)S(1)}, f32[384,512]{1,0:T(8,128)S(1)}, u32[]{:S(2)}, u32[]{:S(2)}) collective-permute-start(f32[384,512]{1,0:T(8,128)S(1)} %maximum_select_fusion), channel_id=1, source_target_pairs={{0,4},{4,0},{8,12},{12,8},{16,20},{20,16},{24,28},{28,24},{1,5},{5... | collective-permute-start | bytes 2359304 | tf_op jit(solution)/shard_map/ppermute | solution.py:108
  25.5 9.5 %collective-permute-start.7 = (f32[512,128]{0,1:T(8,128)S(1)}, f32[512,128]{0,1:T(8,128)S(1)}, u32[]{:S(2)}, u32[]{:S(2)}) collective-permute-start(f32[512,128]{0,1:T(8,128)S(1)} %fusion.2), channel_id=1, source_target_pairs={{0,1},{1,3},{2,0},{3,2},{4,5},{5,7},{6,4},{7,6},{8,9},{9,11},{10,8... | collective-permute-start | bytes 786440 | tf_op jit(solution)/shard_map/ppermute | solution.py:123
  27.6 14.7 %collective-permute-start.9 = (f32[512,128]{0,1:T(8,128)S(1)}, f32[512,128]{0,1:T(8,128)S(1)}, u32[]{:S(2)}, u32[]{:S(2)}) collective-permute-start(f32[512,128]{0,1:T(8,128)S(1)} %fusion.3), channel_id=1, source_target_pairs={{0,3},{3,0},{4,7},{7,4},{8,11},{11,8},{12,15},{15,12},{16,19},{19,... | collective-permute-start | bytes 786440 | tf_op jit(solution)/shard_map/ppermute | solution.py:127
  32.4 13.8 %collective-permute-start.8 = (f32[512,128]{0,1:T(8,128)S(1)}, f32[512,128]{0,1:T(8,128)S(1)}, u32[]{:S(2)}, u32[]{:S(2)}) collective-permute-start(f32[512,128]{0,1:T(8,128)S(1)} %fusion.1), channel_id=1, source_target_pairs={{0,1},{1,0},{2,3},{3,2},{4,5},{5,4},{6,7},{7,6},{8,9},{9,8},{10,11... | collective-permute-start | bytes 786440 | tf_op jit(solution)/shard_map/ppermute | solution.py:128
  35.6 10.7 %collective-permute-start.10 = (f32[512,128]{0,1:T(8,128)S(1)}, f32[512,128]{0,1:T(8,128)S(1)}, u32[]{:S(2)}, u32[]{:S(2)}) collective-permute-start(f32[512,128]{0,1:T(8,128)S(1)} %add.90), channel_id=1, source_target_pairs={{1,2},{2,1},{5,6},{6,5},{9,10},{10,9},{13,14},{14,13},{17,18},{18,... | collective-permute-start | bytes 786440 | tf_op jit(solution)/shard_map/ppermute | solution.py:131
  47.4 12.4 %all-to-all-start = ((f32[32,1,1024]{2,1,0:T(1,128)}), f32[32,1,1024]{2,1,0:T(1,128)S(1)}, u32[]{:S(2)}, u32[]{:S(2)}) async-start(f32[32,1,1024]{2,1,0:T(1,128)} %copy.8), calls=%async_computation | async-start | bytes 262144 | tf_op jit(solution)/shard_map/all_to_all | solution.py:138

commit v7 on v6

--- a/solution.py
+++ b/solution.py
@@ -121,8 +121,8 @@
     end = (narrow_place == 0) | (narrow_place == narrow - 1)
     two_on, pivot = turn_part(0, pivot)
     two_on = lax.ppermute(two_on, "narrow", [(0, 1), (1, 3), (2, 0), (3, 2)])
+    beside, pivot = turn_part(2, pivot)
     across, pivot = turn_part(1, pivot)
-    beside, pivot = turn_part(2, pivot)
     across, beside = lax.optimization_barrier((across, beside))
     outer = lax.ppermute(across, "narrow", [(0, 3), (3, 0)])
     beside = lax.ppermute(beside, "narrow", [(0, 1), (1, 0), (2, 3), (3, 2)])
@@ -134,10 +134,18 @@
 
     samples = samples_prev + contract(draws[depth:], panel_factor, 0, 1)
     squares = jnp.sum(factor_prev * factor_prev, axis=1) + jnp.sum(panel_factor * panel_factor, axis=1)
-    outgoing = jnp.concatenate([samples, jnp.broadcast_to(squares[None, :], samples.shape)], axis=1)
+    count, lanes = samples.shape[0], 128
+    groups = row_count // lanes
+    outgoing = jnp.concatenate(
+        [
+            samples.reshape(count, groups, lanes),
+            jnp.broadcast_to(squares.reshape(1, groups, lanes), (count, groups, lanes)),
+        ],
+        axis=1,
+    )
     incoming = lax.all_to_all(outgoing, ("narrow", "wide"), split_axis=0, concat_axis=0, tiled=True)
-    whole = jnp.sum(incoming.reshape(narrow, wide, 2 * row_count), axis=0)
-    scaled = whole[:, :row_count] * lax.rsqrt(whole[:, row_count:] + 1e-06)
+    whole = jnp.sum(incoming.reshape(narrow, wide, 2 * groups, lanes), axis=0)
+    scaled = whole[:, :groups] * lax.rsqrt(whole[:, groups:] + 1e-06)
     uniforms = 0.5 * (1.0 + lax.erf(scaled * HALF_ROOT))
     return (panel_factor, smooth(uniforms.reshape(1, wide * row_count)))
 

time: 61 us -> 60.9 us (level)
  local copies, waits for them, and re-layouts: 2.85 us -> 2.06 us
  other arithmetic: 1.87 us -> 2.54 us
    all_to_all x1 -> x0, local copies, waits for them, and re-layouts: 0.79 us -> none  [per_device(): lax.all_to_all(outgoing, ('narrow', 'wide'), split_axis=0, concat_axis=0,...]
    concatenate x0 -> x1, other arithmetic: none -> 0.69 us  [per_device(): jnp.concatenate([samples.reshape(count, groups, lanes), jnp.broadcast_to(...]
where the time goes in v7:
time: 60.9 us; the launch traced here: 60.6 us
  waiting for transfers between devices  33 us (54%)
  starting transfers between devices  17.1 us (28%)
  matrix products  4.75 us (8%)
  other arithmetic  2.54 us (4%)
  local copies, waits for them, and re-layouts  2.06 us (3%)
  between operations  1.09 us (2%)
    ppermute x3, waiting for transfers between devices, send(): return lax.ppermute(value, ('wide', 'narrow'), pairs)  8.1 us
    all_to_all x1, waiting for transfers between devices, per_device(): lax.all_to_all(outgoing, ('narrow', 'wide'), split_axis=0, concat_axis=0,...  7.39 us
    ppermute x1, waiting for transfers between devices, per_device(): outer = lax.ppermute(across, 'narrow', [(0, 3), (3, 0)])  5.49 us
    ppermute x1, starting transfers between devices, per_device(): outer = lax.ppermute(across, 'narrow', [(0, 3), (3, 0)])  4.82 us
    dot_general x14, matrix products, contract(): lax.dot_general(left_side, right_side, (((left_dim,), (right_dim,)), ((),...  4.75 us
    ppermute x3, waiting for transfers between devices, send(): lax.ppermute(jnp.where(on_core, value, rider), ('wide', 'narrow'), pairs...  4.51 us
    all_to_all x1, starting transfers between devices, per_device(): lax.all_to_all(outgoing, ('narrow', 'wide'), split_axis=0, concat_axis=0,...  4.14 us
    ppermute x1, waiting for transfers between devices, per_device(): beside = lax.ppermute(beside, 'narrow', [(0, 1), (1, 0), (2, 3), (3, 2)])  3.95 us
  transfers between devices with their start and end apart: 12, of which 7 were waited for; matrix products, arithmetic and copies ran while one was open for 6% of the time, Pallas kernels for 0%

profile of v7, /device:TPU:0, one launch (start us, length us, event | category | flops | bytes accessed | tf_op | source)
XLA Modules:
  0.0 60.6 jit_solution(14482324954674991623)
XLA Ops:
  0.7 1.1 %fusion.28 = (f32[256,256]{1,0:T(8,128)S(1)}, f32[256,256]{1,0:T(8,128)S(1)}) fusion(f32[512,256]{1,0:T(8,128)} %param.6), kind=kLoop, calls=%fused_computation.58 | loop fusion | bytes 1048576 | tf_op jit(solution)/shard_map/split | solution.py:25
  1.9 1.3 %collective-permute-start.1 = (f32[128,512]{1,0:T(8,128)S(1)}, f32[128,512]{1,0:T(8,128)S(1)}, u32[]{:S(2)}, u32[]{:S(2)}) collective-permute-start(f32[128,512]{1,0:T(8,128)S(1)} %get-tuple-element.40), channel_id=1, source_target_pairs={{8,0},{9,1},{10,2},{11,3},{4,7},{5,4},{6,5},{7,6},{12,15},{13,12},... | collective-permute-start | bytes 786440 | tf_op jit(solution)/shard_map/ppermute | solution.py:46
  3.2 0.7 %collective-permute-start = (f32[128,512]{1,0:T(8,128)S(1)}, f32[128,512]{1,0:T(8,128)S(1)}, u32[]{:S(2)}, u32[]{:S(2)}) collective-permute-start(f32[128,512]{1,0:T(8,128)S(1)} %get-tuple-element.40), channel_id=1, source_target_pairs={{8,16},{9,17},{10,18},{11,19},{4,6},{5,7},{6,4},{7,5},{12,14},{13,... | collective-permute-start | bytes 786440 | tf_op jit(solution)/shard_map/ppermute | solution.py:46
  3.9 0.7 %collective-permute-start.2 = (f32[128,512]{1,0:T(8,128)S(1)}, f32[128,512]{1,0:T(8,128)S(1)}, u32[]{:S(2)}, u32[]{:S(2)}) collective-permute-start(f32[128,512]{1,0:T(8,128)S(1)} %get-tuple-element.40), channel_id=1, source_target_pairs={{8,24},{9,25},{10,26},{11,27},{4,5},{5,6},{6,7},{7,4},{12,13},{13,... | collective-permute-start | bytes 786440 | tf_op jit(solution)/shard_map/ppermute | solution.py:46
  4.5 0.7 %collective-permute-start.5 = (f32[128,512]{1,0:T(8,128)S(1)}, f32[128,512]{1,0:T(8,128)S(1)}, u32[]{:S(2)}, u32[]{:S(2)}) collective-permute-start(f32[128,512]{1,0:T(8,128)S(1)} %get-tuple-element.39), channel_id=1, source_target_pairs={{8,24},{9,25},{10,26},{11,27}} | collective-permute-start | bytes 786440 | tf_op jit(solution)/shard_map/ppermute | solution.py:44
  5.2 0.7 %collective-permute-start.3 = (f32[128,512]{1,0:T(8,128)S(1)}, f32[128,512]{1,0:T(8,128)S(1)}, u32[]{:S(2)}, u32[]{:S(2)}) collective-permute-start(f32[128,512]{1,0:T(8,128)S(1)} %get-tuple-element.39), channel_id=1, source_target_pairs={{8,16},{9,17},{10,18},{11,19}} | collective-permute-start | bytes 786440 | tf_op jit(solution)/shard_map/ppermute | solution.py:44
  5.9 4.5 %collective-permute-done.1 = f32[128,512]{1,0:T(8,128)S(1)} collective-permute-done((f32[128,512]{1,0:T(8,128)S(1)}, f32[128,512]{1,0:T(8,128)S(1)}, u32[]{:S(2)}, u32[]{:S(2)}) %collective-permute-start.1) | collective-permute-done | bytes 262176 | tf_op jit(solution)/shard_map/ppermute | solution.py:46
  10.4 1.3 %collective-permute-start.4 = (f32[128,512]{1,0:T(8,128)S(1)}, f32[128,512]{1,0:T(8,128)S(1)}, u32[]{:S(2)}, u32[]{:S(2)}) collective-permute-start(f32[128,512]{1,0:T(8,128)S(1)} %get-tuple-element.39), channel_id=1, source_target_pairs={{8,0},{9,1},{10,2},{11,3}} | collective-permute-start | bytes 786440 | tf_op jit(solution)/shard_map/ppermute | solution.py:44
  11.9 8.1 %collective-permute-done.4 = f32[128,512]{1,0:T(8,128)S(1)} collective-permute-done((f32[128,512]{1,0:T(8,128)S(1)}, f32[128,512]{1,0:T(8,128)S(1)}, u32[]{:S(2)}, u32[]{:S(2)}) %collective-permute-start.4) | collective-permute-done | bytes 262176 | tf_op jit(solution)/shard_map/ppermute | solution.py:44
  20.3 1.0 %collective-permute-start.6 = (f32[384,512]{1,0:T(8,128)S(1)}, f32[384,512]{1,0:T(8,128)S(1)}, u32[]{:S(2)}, u32[]{:S(2)}) collective-permute-start(f32[384,512]{1,0:T(8,128)S(1)} %maximum_select_fusion), channel_id=1, source_target_pairs={{0,4},{4,0},{8,12},{12,8},{16,20},{20,16},{24,28},{28,24},{1,5},{5... | collective-permute-start | bytes 2359304 | tf_op jit(solution)/shard_map/ppermute | solution.py:108
  22.1 1.1 %collective-permute-done.6 = f32[384,512]{1,0:T(8,128)S(1)} collective-permute-done((f32[384,512]{1,0:T(8,128)S(1)}, f32[384,512]{1,0:T(8,128)S(1)}, u32[]{:S(2)}, u32[]{:S(2)}) %collective-permute-start.6) | collective-permute-done | bytes 786464 | tf_op jit(solution)/shard_map/ppermute | solution.py:108
  25.5 1.1 %collective-permute-start.7 = (f32[512,128]{0,1:T(8,128)S(1)}, f32[512,128]{0,1:T(8,128)S(1)}, u32[]{:S(2)}, u32[]{:S(2)}) collective-permute-start(f32[512,128]{0,1:T(8,128)S(1)} %fusion.1), channel_id=1, source_target_pairs={{0,1},{1,3},{2,0},{3,2},{4,5},{5,7},{6,4},{7,6},{8,9},{9,11},{10,8... | collective-permute-start | bytes 786440 | tf_op jit(solution)/shard_map/ppermute | solution.py:123
  27.6 4.8 %collective-permute-start.9 = (f32[512,128]{0,1:T(8,128)S(1)}, f32[512,128]{0,1:T(8,128)S(1)}, u32[]{:S(2)}, u32[]{:S(2)}) collective-permute-start(f32[512,128]{0,1:T(8,128)S(1)} %fusion.3), channel_id=1, source_target_pairs={{0,3},{3,0},{4,7},{7,4},{8,11},{11,8},{12,15},{15,12},{16,19},{19,... | collective-permute-start | bytes 786440 | tf_op jit(solution)/shard_map/ppermute | solution.py:127
  32.5 2.5 %collective-permute-done.7 = f32[512,128]{0,1:T(8,128)S(1)} collective-permute-done((f32[512,128]{0,1:T(8,128)S(1)}, f32[512,128]{0,1:T(8,128)S(1)}, u32[]{:S(2)}, u32[]{:S(2)}) %collective-permute-start.7) | collective-permute-done | bytes 262176 | tf_op jit(solution)/shard_map/ppermute | solution.py:123
  35.0 0.6 fusion.34
  35.6 0.7 %collective-permute-start.10 = (f32[512,128]{0,1:T(8,128)S(1)}, f32[512,128]{0,1:T(8,128)S(1)}, u32[]{:S(2)}, u32[]{:S(2)}) collective-permute-start(f32[512,128]{0,1:T(8,128)S(1)} %add.93), channel_id=1, source_target_pairs={{1,2},{2,1},{5,6},{6,5},{9,10},{10,9},{13,14},{14,13},{17,18},{18,... | collective-permute-start | bytes 786440 | tf_op jit(solution)/shard_map/ppermute | solution.py:131
  36.3 0.4 fusion
  36.8 5.5 %collective-permute-done.9 = f32[512,128]{0,1:T(8,128)S(1)} collective-permute-done((f32[512,128]{0,1:T(8,128)S(1)}, f32[512,128]{0,1:T(8,128)S(1)}, u32[]{:S(2)}, u32[]{:S(2)}) %collective-permute-start.9) | collective-permute-done | bytes 262176 | tf_op jit(solution)/shard_map/ppermute | solution.py:127
  42.3 4.0 %collective-permute-done.8 = f32[512,128]{0,1:T(8,128)S(1)} collective-permute-done((f32[512,128]{0,1:T(8,128)S(1)}, f32[512,128]{0,1:T(8,128)S(1)}, u32[]{:S(2)}, u32[]{:S(2)}) %collective-permute-start.8) | collective-permute-done | bytes 262176 | tf_op jit(solution)/shard_map/ppermute | solution.py:128
  46.7 0.7 %pad_maximum_fusion.2 = f32[32,8,128]{2,1,0:T(8,128)} fusion(f32[32,4,128]{2,1,0:T(4,128)S(1)} %broadcast_in_dim.15, f32[32,4,128]{2,1,0:T(4,128)S(1)} %reshape.36), kind=kLoop, calls=%fused_computation.30 | loop fusion | flops 32768 | bytes 262144 | tf_op jit(solution)/shard_map/concatenate | solution.py:139
  47.3 4.1 %all-to-all-start = ((f32[32,8,128]{2,1,0:T(8,128)}), f32[32,8,128]{2,1,0:T(8,128)S(1)}, u32[]{:S(2)}, u32[]{:S(2)}) async-start(f32[32,8,128]{2,1,0:T(8,128)} %pad_maximum_fusion.2), calls=%async_computation | async-start | bytes 262144 | tf_op jit(solution)/shard_map/all_to_all | solution.py:146
  51.5 0.8 %copy.7 = f32[512,128]{1,0:T(8,128)} copy(f32[512,128]{0,1:T(8,128)S(1)} %get-tuple-element.33) | data formatting | bytes 524288
  52.3 7.4 %all-to-all-done = f32[32,8,128]{2,1,0:T(8,128)S(1)} async-done(((f32[32,8,128]{2,1,0:T(8,128)}), f32[32,8,128]{2,1,0:T(8,128)S(1)}, u32[]{:S(2)}, u32[]{:S(2)}) %all-to-all-start) | async-done | bytes 131104 | tf_op jit(solution)/shard_map/all_to_all | solution.py:146
  59.8 0.8 %multiply_add_fusion = f32[1,4096]{1,0:T(1,128)} fusion(f32[1,4096]{1,0:T(1,128)S(1)} %bitcast.34), kind=kLoop, calls=%fused_computation.47 | loop fusion | flops 36864 | bytes 32768 | tf_op jit(solution)/shard_map/add | solution.py:78
  (48 shorter events, 4.9 us)
Async XLA Ops:
  0.6 20.8 %copy-start = (f32[512,128]{1,0:T(8,128)S(1)}, f32[512,128]{1,0:T(8,128)}, u32[]{:S(2)}) copy-start(f32[512,128]{1,0:T(8,128)} %param.5) | copy-start | bytes 786436
  0.7 1.1 %copy-start.2 = (f32[128,512]{1,0:T(8,128)S(1)}, f32[128,512]{1,0:T(8,128)}, u32[]{:S(2)}) copy-start(f32[128,512]{1,0:T(8,128)} %param.9) | copy-start | bytes 786436
  1.9 8.6 %collective-permute-start.1 = (f32[128,512]{1,0:T(8,128)S(1)}, f32[128,512]{1,0:T(8,128)S(1)}, u32[]{:S(2)}, u32[]{:S(2)}) collective-permute-start(f32[128,512]{1,0:T(8,128)S(1)} %get-tuple-element.40), channel_id=1, source_target_pairs={{8,0},{9,1},{10,2},{11,3},{4,7},{5,4},{6,5},{7,6},{12,15},{13,12},... | collective-permute-start | bytes 786440 | tf_op jit(solution)/shard_map/ppermute | solution.py:46
  3.2 8.6 %collective-permute-start = (f32[128,512]{1,0:T(8,128)S(1)}, f32[128,512]{1,0:T(8,128)S(1)}, u32[]{:S(2)}, u32[]{:S(2)}) collective-permute-start(f32[128,512]{1,0:T(8,128)S(1)} %get-tuple-element.40), channel_id=1, source_target_pairs={{8,16},{9,17},{10,18},{11,19},{4,6},{5,7},{6,4},{7,5},{12,14},{13,... | collective-permute-start | bytes 786440 | tf_op jit(solution)/shard_map/ppermute | solution.py:46
  3.9 7.9 %collective-permute-start.2 = (f32[128,512]{1,0:T(8,128)S(1)}, f32[128,512]{1,0:T(8,128)S(1)}, u32[]{:S(2)}, u32[]{:S(2)}) collective-permute-start(f32[128,512]{1,0:T(8,128)S(1)} %get-tuple-element.40), channel_id=1, source_target_pairs={{8,24},{9,25},{10,26},{11,27},{4,5},{5,6},{6,7},{7,4},{12,13},{13,... | collective-permute-start | bytes 786440 | tf_op jit(solution)/shard_map/ppermute | solution.py:46
  4.5 7.3 %collective-permute-start.5 = (f32[128,512]{1,0:T(8,128)S(1)}, f32[128,512]{1,0:T(8,128)S(1)}, u32[]{:S(2)}, u32[]{:S(2)}) collective-permute-start(f32[128,512]{1,0:T(8,128)S(1)} %get-tuple-element.39), channel_id=1, source_target_pairs={{8,24},{9,25},{10,26},{11,27}} | collective-permute-start | bytes 786440 | tf_op jit(solution)/shard_map/ppermute | solution.py:44
  5.2 6.6 %collective-permute-start.3 = (f32[128,512]{1,0:T(8,128)S(1)}, f32[128,512]{1,0:T(8,128)S(1)}, u32[]{:S(2)}, u32[]{:S(2)}) collective-permute-start(f32[128,512]{1,0:T(8,128)S(1)} %get-tuple-element.39), channel_id=1, source_target_pairs={{8,16},{9,17},{10,18},{11,19}} | collective-permute-start | bytes 786440 | tf_op jit(solution)/shard_map/ppermute | solution.py:44
  10.4 9.5 %collective-permute-start.4 = (f32[128,512]{1,0:T(8,128)S(1)}, f32[128,512]{1,0:T(8,128)S(1)}, u32[]{:S(2)}, u32[]{:S(2)}) collective-permute-start(f32[128,512]{1,0:T(8,128)S(1)} %get-tuple-element.39), channel_id=1, source_target_pairs={{8,0},{9,1},{10,2},{11,3}} | collective-permute-start | bytes 786440 | tf_op jit(solution)/shard_map/ppermute | solution.py:44
  20.1 1.1 %copy-start.3 = (f32[256,32]{0,1:T(8,128)S(1)}, f32[256,32]{0,1:T(8,128)}, u32[]{:S(2)}) copy-start(f32[256,32]{0,1:T(8,128)} %param.7) | copy-start | bytes 98308
  20.1 1.1 %copy-start.4 = (f32[128,32]{0,1:T(8,128)S(1)}, f32[128,32]{0,1:T(8,128)}, u32[]{:S(2)}) copy-start(f32[128,32]{0,1:T(8,128)} %param.8) | copy-start | bytes 49156
  20.1 1.1 %copy-start.1 = (f32[512,256]{1,0:T(8,128)S(1)}, f32[512,256]{1,0:T(8,128)}, u32[]{:S(2)}) copy-start(f32[512,256]{1,0:T(8,128)} %param.6) | copy-start | bytes 1572868
  20.3 2.9 %collective-permute-start.6 = (f32[384,512]{1,0:T(8,128)S(1)}, f32[384,512]{1,0:T(8,128)S(1)}, u32[]{:S(2)}, u32[]{:S(2)}) collective-permute-start(f32[384,512]{1,0:T(8,128)S(1)} %maximum_select_fusion), channel_id=1, source_target_pairs={{0,4},{4,0},{8,12},{12,8},{16,20},{20,16},{24,28},{28,24},{1,5},{5... | collective-permute-start | bytes 2359304 | tf_op jit(solution)/shard_map/ppermute | solution.py:108
  25.5 9.5 %collective-permute-start.7 = (f32[512,128]{0,1:T(8,128)S(1)}, f32[512,128]{0,1:T(8,128)S(1)}, u32[]{:S(2)}, u32[]{:S(2)}) collective-permute-start(f32[512,128]{0,1:T(8,128)S(1)} %fusion.1), channel_id=1, source_target_pairs={{0,1},{1,3},{2,0},{3,2},{4,5},{5,7},{6,4},{7,6},{8,9},{9,11},{10,8... | collective-permute-start | bytes 786440 | tf_op jit(solution)/shard_map/ppermute | solution.py:123
  27.6 14.7 %collective-permute-start.9 = (f32[512,128]{0,1:T(8,128)S(1)}, f32[512,128]{0,1:T(8,128)S(1)}, u32[]{:S(2)}, u32[]{:S(2)}) collective-permute-start(f32[512,128]{0,1:T(8,128)S(1)} %fusion.3), channel_id=1, source_target_pairs={{0,3},{3,0},{4,7},{7,4},{8,11},{11,8},{12,15},{15,12},{16,19},{19,... | collective-permute-start | bytes 786440 | tf_op jit(solution)/shard_map/ppermute | solution.py:127
  32.4 13.8 %collective-permute-start.8 = (f32[512,128]{0,1:T(8,128)S(1)}, f32[512,128]{0,1:T(8,128)S(1)}, u32[]{:S(2)}, u32[]{:S(2)}) collective-permute-start(f32[512,128]{0,1:T(8,128)S(1)} %fusion.2), channel_id=1, source_target_pairs={{0,1},{1,0},{2,3},{3,2},{4,5},{5,4},{6,7},{7,6},{8,9},{9,8},{10,11... | collective-permute-start | bytes 786440 | tf_op jit(solution)/shard_map/ppermute | solution.py:128
  35.6 10.7 %collective-permute-start.10 = (f32[512,128]{0,1:T(8,128)S(1)}, f32[512,128]{0,1:T(8,128)S(1)}, u32[]{:S(2)}, u32[]{:S(2)}) collective-permute-start(f32[512,128]{0,1:T(8,128)S(1)} %add.93), channel_id=1, source_target_pairs={{1,2},{2,1},{5,6},{6,5},{9,10},{10,9},{13,14},{14,13},{17,18},{18,... | collective-permute-start | bytes 786440 | tf_op jit(solution)/shard_map/ppermute | solution.py:131
  47.3 12.4 %all-to-all-start = ((f32[32,8,128]{2,1,0:T(8,128)}), f32[32,8,128]{2,1,0:T(8,128)S(1)}, u32[]{:S(2)}, u32[]{:S(2)}) async-start(f32[32,8,128]{2,1,0:T(8,128)} %pad_maximum_fusion.2), calls=%async_computation | async-start | bytes 262144 | tf_op jit(solution)/shard_map/all_to_all | solution.py:146

commit v8 on v7

--- a/solution.py
+++ b/solution.py
@@ -38,9 +38,9 @@
     held = jnp.where(place == source, packed, 0.0)
     holders = [source]
 
-    def send(value, to):
-        pairs = [(h * narrow + i, (h ^ to) * narrow + i) for h in holders for i in range(narrow)]
-        if not riders or value.shape != riders[0][0].shape:
+    def send(value, to, fro=0):
+        pairs = [((h ^ fro) * narrow + i, (h ^ to) * narrow + i) for h in holders for i in range(narrow)]
+        if not riders:
             return lax.ppermute(value, ("wide", "narrow"), pairs)
         rider, more = riders.pop(0)
         carried.append(lax.ppermute(jnp.where(on_core, value, rider), ("wide", "narrow"), pairs + more))
@@ -50,19 +50,18 @@
     while (1 << shift) < wide:
         low, high, both = 1 << shift, 2 << shift, 3 << shift
         top, bottom = packed[:half], packed[half:]
-        got = {}
+        low_top = send(top, low)
         if high < wide:
-            got['TL'] = send(top, low)
-            got['TD'] = send(top, both)
-            got['TH'] = send(top, high)
-            got['BD'] = send(bottom, both)
-            got['BL'] = send(bottom, low)
-            got['BH'] = send(bottom, high)
-            tops, bottoms = [got['TD'], got['TL'], got['TH']], [got['BD'], got['BL'], got['BH']]
-        else:
-            tops, bottoms = [send(top, low)], [send(bottom, low)]
-        held = held + jnp.concatenate([sum(tops), sum(bottoms)])
-        holders = [h ^ f for h in holders for f in (0, low, high, both)[: 1 + len(tops)]]
+            high_bottom = send(bottom, high)
+            high_top = send(top, high)
+            both_bottom = send(bottom, both)
+        low_bottom = send(bottom, low)
+        tops, bottoms = low_top, low_bottom
+        if high < wide:
+            both_top = send(low_top, both, low)
+            tops, bottoms = both_top + low_top + high_top, both_bottom + low_bottom + high_bottom
+        held = held + jnp.concatenate([tops, bottoms])
+        holders = [h ^ f for h in holders for f in ((0, low, high, both) if high < wide else (0, low))]
         packed = held
         shift += 2
     return held, carried
@@ -88,9 +87,9 @@
     fetchers = [c for c in range(wide) if c % 2 != source % 2]
 
     def shifted(k):
-        return [(c * narrow + i, c * narrow + (i + k) % narrow) for c in fetchers for i in range(narrow)]
+        return [(c * narrow + i, c * narrow + (i ^ k)) for c in fetchers for i in range(narrow)]
 
-    far = list(range(narrow - 1, 0, -1))
+    far = [2, 1, 3]
     own_pivot, rows = broadcast(
         factor_prev, source, wide, narrow, [(diag_inverse, shifted(k)) for k in far]
     )
@@ -99,10 +98,7 @@
     draws = lax.optimization_barrier(jnp.concatenate([draws_prev, draws_panel]))
     samples_prev = contract(draws[:depth], factor_prev, 0, 1)
 
-    even = narrow_place % 2 == 0
-    own_rows = jnp.concatenate(
-        [rows[2], jnp.where(even, rows[1], rows[3]), jnp.where(even, rows[3], rows[1])]
-    )
+    own_rows = jnp.concatenate([rows[2], rows[3], rows[1]])
     spare = own_rows.shape[0] - own_pivot.shape[0]
     pieces = jnp.where(on_core, jnp.pad(own_pivot, ((0, spare), (0, 0))), own_rows)
     swapped = lax.ppermute(pieces, "wide", [(i, i ^ 1) for i in range(wide)])

time: 60.9 us -> 59.8 us (0.982)
  waiting for transfers between devices: 33 us -> 31.2 us
  starting transfers between devices: 17.1 us -> 17.9 us
    ppermute x3, waiting for transfers between devices: 8.1 us -> 6.96 us  [send(): return lax.ppermute(value, ('wide', 'narrow'), pairs)]
    ppermute x3, starting transfers between devices: 2.64 us -> 3.26 us  [send(): return lax.ppermute(value, ('wide', 'narrow'), pairs)]
where the time goes in v8:
time: 59.8 us; the launch traced here: 59.5 us
  waiting for transfers between devices  31.2 us (52%)
  starting transfers between devices  17.9 us (30%)
  matrix products  4.76 us (8%)
  other arithmetic  2.52 us (4%)
  local copies, waits for them, and re-layouts  2.07 us (3%)
  between operations  1.06 us (2%)
    all_to_all x1, waiting for transfers between devices, per_device(): lax.all_to_all(outgoing, ('narrow', 'wide'), split_axis=0, concat_axis=0,...  7.39 us
    ppermute x3, waiting for transfers between devices, send(): return lax.ppermute(value, ('wide', 'narrow'), pairs)  6.96 us
    ppermute x1, waiting for transfers between devices, per_device(): outer = lax.ppermute(across, 'narrow', [(0, 3), (3, 0)])  5.59 us
    dot_general x14, matrix products, contract(): lax.dot_general(left_side, right_side, (((left_dim,), (right_dim,)), ((),...  4.76 us
    ppermute x1, starting transfers between devices, per_device(): outer = lax.ppermute(across, 'narrow', [(0, 3), (3, 0)])  4.63 us
    all_to_all x1, starting transfers between devices, per_device(): lax.all_to_all(outgoing, ('narrow', 'wide'), split_axis=0, concat_axis=0,...  4.2 us
    ppermute x3, waiting for transfers between devices, send(): lax.ppermute(jnp.where(on_core, value, rider), ('wide', 'narrow'), pairs...  3.91 us
    ppermute x1, waiting for transfers between devices, per_device(): beside = lax.ppermute(beside, 'narrow', [(0, 1), (1, 0), (2, 3), (3, 2)])  3.87 us
  transfers between devices with their start and end apart: 12, of which 7 were waited for; matrix products, arithmetic and copies ran while one was open for 6% of the time, Pallas kernels for 0%

profile of v8, /device:TPU:0, one launch (start us, length us, event | category | flops | bytes accessed | tf_op | source)
XLA Modules:
  0.0 59.5 jit_solution(264149739040931161)
XLA Ops:
  0.7 1.1 %fusion.29 = (f32[256,256]{1,0:T(8,128)S(1)}, f32[256,256]{1,0:T(8,128)S(1)}) fusion(f32[512,256]{1,0:T(8,128)} %param.6), kind=kLoop, calls=%fused_computation.57 | loop fusion | bytes 1048576 | tf_op jit(solution)/shard_map/split | solution.py:25
  1.9 1.3 %collective-permute-start = (f32[128,512]{1,0:T(8,128)S(1)}, f32[128,512]{1,0:T(8,128)S(1)}, u32[]{:S(2)}, u32[]{:S(2)}) collective-permute-start(f32[128,512]{1,0:T(8,128)S(1)} %get-tuple-element.39), channel_id=1, source_target_pairs={{8,0},{9,1},{10,2},{11,3},{4,6},{5,7},{6,4},{7,5},{12,14},{13,15},... | collective-permute-start | bytes 786440 | tf_op jit(solution)/shard_map/ppermute | solution.py:46
  3.2 0.7 %collective-permute-start.5 = (f32[128,512]{1,0:T(8,128)S(1)}, f32[128,512]{1,0:T(8,128)S(1)}, u32[]{:S(2)}, u32[]{:S(2)}) collective-permute-start(f32[128,512]{1,0:T(8,128)S(1)} %get-tuple-element.34), channel_id=1, source_target_pairs={{8,24},{9,25},{10,26},{11,27},{4,5},{5,4},{6,7},{7,6},{12,13},{13,... | collective-permute-start | bytes 786440 | tf_op jit(solution)/shard_map/ppermute | solution.py:46
  3.9 0.7 %collective-permute-start.2 = (f32[128,512]{1,0:T(8,128)S(1)}, f32[128,512]{1,0:T(8,128)S(1)}, u32[]{:S(2)}, u32[]{:S(2)}) collective-permute-start(f32[128,512]{1,0:T(8,128)S(1)} %get-tuple-element.39), channel_id=1, source_target_pairs={{8,24},{9,25},{10,26},{11,27},{4,7},{5,6},{6,5},{7,4},{12,15},{13,... | collective-permute-start | bytes 786440 | tf_op jit(solution)/shard_map/ppermute | solution.py:46
  4.6 0.7 %collective-permute-start.3 = (f32[128,512]{1,0:T(8,128)S(1)}, f32[128,512]{1,0:T(8,128)S(1)}, u32[]{:S(2)}, u32[]{:S(2)}) collective-permute-start(f32[128,512]{1,0:T(8,128)S(1)} %get-tuple-element.35), channel_id=1, source_target_pairs={{8,16},{9,17},{10,18},{11,19}} | collective-permute-start | bytes 786440 | tf_op jit(solution)/shard_map/ppermute | solution.py:44
  5.3 1.3 %collective-permute-start.4 = (f32[128,512]{1,0:T(8,128)S(1)}, f32[128,512]{1,0:T(8,128)S(1)}, u32[]{:S(2)}, u32[]{:S(2)}) collective-permute-start(f32[128,512]{1,0:T(8,128)S(1)} %get-tuple-element.35), channel_id=1, source_target_pairs={{8,0},{9,1},{10,2},{11,3}} | collective-permute-start | bytes 786440 | tf_op jit(solution)/shard_map/ppermute | solution.py:44
  6.6 3.9 %collective-permute-done = f32[128,512]{1,0:T(8,128)S(1)} collective-permute-done((f32[128,512]{1,0:T(8,128)S(1)}, f32[128,512]{1,0:T(8,128)S(1)}, u32[]{:S(2)}, u32[]{:S(2)}) %collective-permute-start) | collective-permute-done | bytes 262176 | tf_op jit(solution)/shard_map/ppermute | solution.py:46
  10.5 1.3 %collective-permute-start.1 = (f32[128,512]{1,0:T(8,128)S(1)}, f32[128,512]{1,0:T(8,128)S(1)}, u32[]{:S(2)}, u32[]{:S(2)}) collective-permute-start(f32[128,512]{1,0:T(8,128)S(1)} %collective-permute-done), channel_id=1, source_target_pairs={{0,16},{1,17},{2,18},{3,19}} | collective-permute-start | bytes 786440 | tf_op jit(solution)/shard_map/ppermute | solution.py:44
  11.8 7.0 %collective-permute-done.4 = f32[128,512]{1,0:T(8,128)S(1)} collective-permute-done((f32[128,512]{1,0:T(8,128)S(1)}, f32[128,512]{1,0:T(8,128)S(1)}, u32[]{:S(2)}, u32[]{:S(2)}) %collective-permute-start.4) | collective-permute-done | bytes 262176 | tf_op jit(solution)/shard_map/ppermute | solution.py:44
  19.1 1.0 %collective-permute-start.6 = (f32[384,512]{1,0:T(8,128)S(1)}, f32[384,512]{1,0:T(8,128)S(1)}, u32[]{:S(2)}, u32[]{:S(2)}) collective-permute-start(f32[384,512]{1,0:T(8,128)S(1)} %maximum_select_fusion), channel_id=1, source_target_pairs={{0,4},{4,0},{8,12},{12,8},{16,20},{20,16},{24,28},{28,24},{1,5},{5... | collective-permute-start | bytes 2359304 | tf_op jit(solution)/shard_map/ppermute | solution.py:104
  20.9 1.1 %collective-permute-done.6 = f32[384,512]{1,0:T(8,128)S(1)} collective-permute-done((f32[384,512]{1,0:T(8,128)S(1)}, f32[384,512]{1,0:T(8,128)S(1)}, u32[]{:S(2)}, u32[]{:S(2)}) %collective-permute-start.6) | collective-permute-done | bytes 786464 | tf_op jit(solution)/shard_map/ppermute | solution.py:104
  24.3 1.4 %collective-permute-start.7 = (f32[512,128]{0,1:T(8,128)S(1)}, f32[512,128]{0,1:T(8,128)S(1)}, u32[]{:S(2)}, u32[]{:S(2)}) collective-permute-start(f32[512,128]{0,1:T(8,128)S(1)} %fusion.1), channel_id=1, source_target_pairs={{0,1},{1,3},{2,0},{3,2},{4,5},{5,7},{6,4},{7,6},{8,9},{9,11},{10,8... | collective-permute-start | bytes 786440 | tf_op jit(solution)/shard_map/ppermute | solution.py:119
  26.7 4.6 %collective-permute-start.9 = (f32[512,128]{0,1:T(8,128)S(1)}, f32[512,128]{0,1:T(8,128)S(1)}, u32[]{:S(2)}, u32[]{:S(2)}) collective-permute-start(f32[512,128]{0,1:T(8,128)S(1)} %fusion.3), channel_id=1, source_target_pairs={{0,3},{3,0},{4,7},{7,4},{8,11},{11,8},{12,15},{15,12},{16,19},{19,... | collective-permute-start | bytes 786440 | tf_op jit(solution)/shard_map/ppermute | solution.py:123
  31.4 2.4 %collective-permute-done.7 = f32[512,128]{0,1:T(8,128)S(1)} collective-permute-done((f32[512,128]{0,1:T(8,128)S(1)}, f32[512,128]{0,1:T(8,128)S(1)}, u32[]{:S(2)}, u32[]{:S(2)}) %collective-permute-start.7) | collective-permute-done | bytes 262176 | tf_op jit(solution)/shard_map/ppermute | solution.py:119
  33.9 0.6 fusion.35
  34.5 0.7 %collective-permute-start.10 = (f32[512,128]{0,1:T(8,128)S(1)}, f32[512,128]{0,1:T(8,128)S(1)}, u32[]{:S(2)}, u32[]{:S(2)}) collective-permute-start(f32[512,128]{0,1:T(8,128)S(1)} %add.89), channel_id=1, source_target_pairs={{1,2},{2,1},{5,6},{6,5},{9,10},{10,9},{13,14},{14,13},{17,18},{18,... | collective-permute-start | bytes 786440 | tf_op jit(solution)/shard_map/ppermute | solution.py:127
  35.2 0.4 fusion
  35.6 5.6 %collective-permute-done.9 = f32[512,128]{0,1:T(8,128)S(1)} collective-permute-done((f32[512,128]{0,1:T(8,128)S(1)}, f32[512,128]{0,1:T(8,128)S(1)}, u32[]{:S(2)}, u32[]{:S(2)}) %collective-permute-start.9) | collective-permute-done | bytes 262176 | tf_op jit(solution)/shard_map/ppermute | solution.py:123
  41.2 3.9 %collective-permute-done.8 = f32[512,128]{0,1:T(8,128)S(1)} collective-permute-done((f32[512,128]{0,1:T(8,128)S(1)}, f32[512,128]{0,1:T(8,128)S(1)}, u32[]{:S(2)}, u32[]{:S(2)}) %collective-permute-start.8) | collective-permute-done | bytes 262176 | tf_op jit(solution)/shard_map/ppermute | solution.py:124
  45.5 0.7 %pad_maximum_fusion.2 = f32[32,8,128]{2,1,0:T(8,128)} fusion(f32[32,4,128]{2,1,0:T(4,128)S(1)} %broadcast_in_dim.15, f32[32,4,128]{2,1,0:T(4,128)S(1)} %reshape.36), kind=kLoop, calls=%fused_computation.30 | loop fusion | flops 32768 | bytes 262144 | tf_op jit(solution)/shard_map/concatenate | solution.py:135
  46.2 4.2 %all-to-all-start = ((f32[32,8,128]{2,1,0:T(8,128)}), f32[32,8,128]{2,1,0:T(8,128)S(1)}, u32[]{:S(2)}, u32[]{:S(2)}) async-start(f32[32,8,128]{2,1,0:T(8,128)} %pad_maximum_fusion.2), calls=%async_computation | async-start | bytes 262144 | tf_op jit(solution)/shard_map/all_to_all | solution.py:142
  50.4 0.8 %copy.7 = f32[512,128]{1,0:T(8,128)} copy(f32[512,128]{0,1:T(8,128)S(1)} %get-tuple-element.33) | data formatting | bytes 524288
  51.2 7.4 %all-to-all-done = f32[32,8,128]{2,1,0:T(8,128)S(1)} async-done(((f32[32,8,128]{2,1,0:T(8,128)}), f32[32,8,128]{2,1,0:T(8,128)S(1)}, u32[]{:S(2)}, u32[]{:S(2)}) %all-to-all-start) | async-done | bytes 131104 | tf_op jit(solution)/shard_map/all_to_all | solution.py:142
  58.7 0.8 %multiply_add_fusion = f32[1,4096]{1,0:T(1,128)} fusion(f32[1,4096]{1,0:T(1,128)S(1)} %bitcast.34), kind=kLoop, calls=%fused_computation.46 | loop fusion | flops 36864 | bytes 32768 | tf_op jit(solution)/shard_map/add | solution.py:77
  (47 shorter events, 4.9 us)
Async XLA Ops:
  0.6 19.6 %copy-start = (f32[512,128]{1,0:T(8,128)S(1)}, f32[512,128]{1,0:T(8,128)}, u32[]{:S(2)}) copy-start(f32[512,128]{1,0:T(8,128)} %param.5) | copy-start | bytes 786436
  0.7 1.1 %copy-start.2 = (f32[128,512]{1,0:T(8,128)S(1)}, f32[128,512]{1,0:T(8,128)}, u32[]{:S(2)}) copy-start(f32[128,512]{1,0:T(8,128)} %param.9) | copy-start | bytes 786436
  1.9 8.6 %collective-permute-start = (f32[128,512]{1,0:T(8,128)S(1)}, f32[128,512]{1,0:T(8,128)S(1)}, u32[]{:S(2)}, u32[]{:S(2)}) collective-permute-start(f32[128,512]{1,0:T(8,128)S(1)} %get-tuple-element.39), channel_id=1, source_target_pairs={{8,0},{9,1},{10,2},{11,3},{4,6},{5,7},{6,4},{7,5},{12,14},{13,15},... | collective-permute-start | bytes 786440 | tf_op jit(solution)/shard_map/ppermute | solution.py:46
  3.2 8.6 %collective-permute-start.5 = (f32[128,512]{1,0:T(8,128)S(1)}, f32[128,512]{1,0:T(8,128)S(1)}, u32[]{:S(2)}, u32[]{:S(2)}) collective-permute-start(f32[128,512]{1,0:T(8,128)S(1)} %get-tuple-element.34), channel_id=1, source_target_pairs={{8,24},{9,25},{10,26},{11,27},{4,5},{5,4},{6,7},{7,6},{12,13},{13,... | collective-permute-start | bytes 786440 | tf_op jit(solution)/shard_map/ppermute | solution.py:46
  3.9 7.9 %collective-permute-start.2 = (f32[128,512]{1,0:T(8,128)S(1)}, f32[128,512]{1,0:T(8,128)S(1)}, u32[]{:S(2)}, u32[]{:S(2)}) collective-permute-start(f32[128,512]{1,0:T(8,128)S(1)} %get-tuple-element.39), channel_id=1, source_target_pairs={{8,24},{9,25},{10,26},{11,27},{4,7},{5,6},{6,5},{7,4},{12,15},{13,... | collective-permute-start | bytes 786440 | tf_op jit(solution)/shard_map/ppermute | solution.py:46
  4.6 7.2 %collective-permute-start.3 = (f32[128,512]{1,0:T(8,128)S(1)}, f32[128,512]{1,0:T(8,128)S(1)}, u32[]{:S(2)}, u32[]{:S(2)}) collective-permute-start(f32[128,512]{1,0:T(8,128)S(1)} %get-tuple-element.35), channel_id=1, source_target_pairs={{8,16},{9,17},{10,18},{11,19}} | collective-permute-start | bytes 786440 | tf_op jit(solution)/shard_map/ppermute | solution.py:44
  5.3 13.5 %collective-permute-start.4 = (f32[128,512]{1,0:T(8,128)S(1)}, f32[128,512]{1,0:T(8,128)S(1)}, u32[]{:S(2)}, u32[]{:S(2)}) collective-permute-start(f32[128,512]{1,0:T(8,128)S(1)} %get-tuple-element.35), channel_id=1, source_target_pairs={{8,0},{9,1},{10,2},{11,3}} | collective-permute-start | bytes 786440 | tf_op jit(solution)/shard_map/ppermute | solution.py:44
  10.5 8.4 %collective-permute-start.1 = (f32[128,512]{1,0:T(8,128)S(1)}, f32[128,512]{1,0:T(8,128)S(1)}, u32[]{:S(2)}, u32[]{:S(2)}) collective-permute-start(f32[128,512]{1,0:T(8,128)S(1)} %collective-permute-done), channel_id=1, source_target_pairs={{0,16},{1,17},{2,18},{3,19}} | collective-permute-start | bytes 786440 | tf_op jit(solution)/shard_map/ppermute | solution.py:44
  19.0 1.1 %copy-start.3 = (f32[256,32]{0,1:T(8,128)S(1)}, f32[256,32]{0,1:T(8,128)}, u32[]{:S(2)}) copy-start(f32[256,32]{0,1:T(8,128)} %param.7) | copy-start | bytes 98308
  19.0 1.1 %copy-start.4 = (f32[128,32]{0,1:T(8,128)S(1)}, f32[128,32]{0,1:T(8,128)}, u32[]{:S(2)}) copy-start(f32[128,32]{0,1:T(8,128)} %param.8) | copy-start | bytes 49156
  19.0 1.1 %copy-start.1 = (f32[512,256]{1,0:T(8,128)S(1)}, f32[512,256]{1,0:T(8,128)}, u32[]{:S(2)}) copy-start(f32[512,256]{1,0:T(8,128)} %param.6) | copy-start | bytes 1572868
  19.1 2.9 %collective-permute-start.6 = (f32[384,512]{1,0:T(8,128)S(1)}, f32[384,512]{1,0:T(8,128)S(1)}, u32[]{:S(2)}, u32[]{:S(2)}) collective-permute-start(f32[384,512]{1,0:T(8,128)S(1)} %maximum_select_fusion), channel_id=1, source_target_pairs={{0,4},{4,0},{8,12},{12,8},{16,20},{20,16},{24,28},{28,24},{1,5},{5... | collective-permute-start | bytes 2359304 | tf_op jit(solution)/shard_map/ppermute | solution.py:104
  24.3 9.5 %collective-permute-start.7 = (f32[512,128]{0,1:T(8,128)S(1)}, f32[512,128]{0,1:T(8,128)S(1)}, u32[]{:S(2)}, u32[]{:S(2)}) collective-permute-start(f32[512,128]{0,1:T(8,128)S(1)} %fusion.1), channel_id=1, source_target_pairs={{0,1},{1,3},{2,0},{3,2},{4,5},{5,7},{6,4},{7,6},{8,9},{9,11},{10,8... | collective-permute-start | bytes 786440 | tf_op jit(solution)/shard_map/ppermute | solution.py:119
  26.7 14.5 %collective-permute-start.9 = (f32[512,128]{0,1:T(8,128)S(1)}, f32[512,128]{0,1:T(8,128)S(1)}, u32[]{:S(2)}, u32[]{:S(2)}) collective-permute-start(f32[512,128]{0,1:T(8,128)S(1)} %fusion.3), channel_id=1, source_target_pairs={{0,3},{3,0},{4,7},{7,4},{8,11},{11,8},{12,15},{15,12},{16,19},{19,... | collective-permute-start | bytes 786440 | tf_op jit(solution)/shard_map/ppermute | solution.py:123
  31.3 13.7 %collective-permute-start.8 = (f32[512,128]{0,1:T(8,128)S(1)}, f32[512,128]{0,1:T(8,128)S(1)}, u32[]{:S(2)}, u32[]{:S(2)}) collective-permute-start(f32[512,128]{0,1:T(8,128)S(1)} %fusion.2), channel_id=1, source_target_pairs={{0,1},{1,0},{2,3},{3,2},{4,5},{5,4},{6,7},{7,6},{8,9},{9,8},{10,11... | collective-permute-start | bytes 786440 | tf_op jit(solution)/shard_map/ppermute | solution.py:124
  34.5 10.7 %collective-permute-start.10 = (f32[512,128]{0,1:T(8,128)S(1)}, f32[512,128]{0,1:T(8,128)S(1)}, u32[]{:S(2)}, u32[]{:S(2)}) collective-permute-start(f32[512,128]{0,1:T(8,128)S(1)} %add.89), channel_id=1, source_target_pairs={{1,2},{2,1},{5,6},{6,5},{9,10},{10,9},{13,14},{14,13},{17,18},{18,... | collective-permute-start | bytes 786440 | tf_op jit(solution)/shard_map/ppermute | solution.py:127
  46.2 12.4 %all-to-all-start = ((f32[32,8,128]{2,1,0:T(8,128)}), f32[32,8,128]{2,1,0:T(8,128)S(1)}, u32[]{:S(2)}, u32[]{:S(2)}) async-start(f32[32,8,128]{2,1,0:T(8,128)} %pad_maximum_fusion.2), calls=%async_computation | async-start | bytes 262144 | tf_op jit(solution)/shard_map/all_to_all | solution.py:142

commit v9 on v8

--- a/solution.py
+++ b/solution.py
@@ -53,8 +53,8 @@
         low_top = send(top, low)
         if high < wide:
             high_bottom = send(bottom, high)
+            both_bottom = send(bottom, both)
             high_top = send(top, high)
-            both_bottom = send(bottom, both)
         low_bottom = send(bottom, low)
         tops, bottoms = low_top, low_bottom
         if high < wide:
@@ -117,8 +117,8 @@
     end = (narrow_place == 0) | (narrow_place == narrow - 1)
     two_on, pivot = turn_part(0, pivot)
     two_on = lax.ppermute(two_on, "narrow", [(0, 1), (1, 3), (2, 0), (3, 2)])
+    across, pivot = turn_part(1, pivot)
     beside, pivot = turn_part(2, pivot)
-    across, pivot = turn_part(1, pivot)
     across, beside = lax.optimization_barrier((across, beside))
     outer = lax.ppermute(across, "narrow", [(0, 3), (3, 0)])
     beside = lax.ppermute(beside, "narrow", [(0, 1), (1, 0), (2, 3), (3, 2)])

time: 59.8 us -> 59.6 us (level)
  waiting for transfers between devices: 31.2 us -> 29.9 us
  starting transfers between devices: 17.9 us -> 19 us
    ppermute x1, starting transfers between devices: 0.95 us -> 2.3 us  [per_device(): swapped = lax.ppermute(pieces, 'wide', [(i, i ^ 1) for i in range(wide)])]
    ppermute x3, waiting for transfers between devices: 6.96 us -> 5.62 us  [send(): return lax.ppermute(value, ('wide', 'narrow'), pairs)]
where the time goes in v9:
time: 59.6 us; the launch traced here: 59.3 us
  waiting for transfers between devices  29.9 us (50%)
  starting transfers between devices  19 us (32%)
  matrix products  4.76 us (8%)
  other arithmetic  2.55 us (4%)
  local copies, waits for them, and re-layouts  2.07 us (3%)
  between operations  1.06 us (2%)
    all_to_all x1, waiting for transfers between devices, per_device(): lax.all_to_all(outgoing, ('narrow', 'wide'), split_axis=0, concat_axis=0,...  7.39 us
    ppermute x3, waiting for transfers between devices, send(): return lax.ppermute(value, ('wide', 'narrow'), pairs)  5.62 us
    ppermute x1, waiting for transfers between devices, per_device(): outer = lax.ppermute(across, 'narrow', [(0, 3), (3, 0)])  5.6 us
    dot_general x14, matrix products, contract(): lax.dot_general(left_side, right_side, (((left_dim,), (right_dim,)), ((),...  4.76 us
    ppermute x1, starting transfers between devices, per_device(): outer = lax.ppermute(across, 'narrow', [(0, 3), (3, 0)])  4.64 us
    all_to_all x1, starting transfers between devices, per_device(): lax.all_to_all(outgoing, ('narrow', 'wide'), split_axis=0, concat_axis=0,...  4.02 us
    ppermute x3, waiting for transfers between devices, send(): lax.ppermute(jnp.where(on_core, value, rider), ('wide', 'narrow'), pairs...  3.91 us
    ppermute x1, waiting for transfers between devices, per_device(): beside = lax.ppermute(beside, 'narrow', [(0, 1), (1, 0), (2, 3), (3, 2)])  3.85 us
  transfers between devices with their start and end apart: 12, of which 7 were waited for; matrix products, arithmetic and copies ran while one was open for 6% of the time, Pallas kernels for 0%

profile of v9, /device:TPU:0, one launch (start us, length us, event | category | flops | bytes accessed | tf_op | source)
XLA Modules:
  0.0 59.3 jit_solution(4875520883750043385)
XLA Ops:
  0.7 1.1 %fusion.29 = (f32[256,256]{1,0:T(8,128)S(1)}, f32[256,256]{1,0:T(8,128)S(1)}) fusion(f32[512,256]{1,0:T(8,128)} %param.6), kind=kLoop, calls=%fused_computation.57 | loop fusion | bytes 1048576 | tf_op jit(solution)/shard_map/split | solution.py:25
  1.9 1.3 %collective-permute-start = (f32[128,512]{1,0:T(8,128)S(1)}, f32[128,512]{1,0:T(8,128)S(1)}, u32[]{:S(2)}, u32[]{:S(2)}) collective-permute-start(f32[128,512]{1,0:T(8,128)S(1)} %get-tuple-element.41), channel_id=1, source_target_pairs={{8,0},{9,1},{10,2},{11,3},{4,6},{5,7},{6,4},{7,5},{12,14},{13,15},... | collective-permute-start | bytes 786440 | tf_op jit(solution)/shard_map/ppermute | solution.py:46
  3.2 0.7 %collective-permute-start.5 = (f32[128,512]{1,0:T(8,128)S(1)}, f32[128,512]{1,0:T(8,128)S(1)}, u32[]{:S(2)}, u32[]{:S(2)}) collective-permute-start(f32[128,512]{1,0:T(8,128)S(1)} %get-tuple-element.34), channel_id=1, source_target_pairs={{8,24},{9,25},{10,26},{11,27},{4,5},{5,4},{6,7},{7,6},{12,13},{13,... | collective-permute-start | bytes 786440 | tf_op jit(solution)/shard_map/ppermute | solution.py:46
  3.9 0.7 %collective-permute-start.3 = (f32[128,512]{1,0:T(8,128)S(1)}, f32[128,512]{1,0:T(8,128)S(1)}, u32[]{:S(2)}, u32[]{:S(2)}) collective-permute-start(f32[128,512]{1,0:T(8,128)S(1)} %get-tuple-element.34), channel_id=1, source_target_pairs={{8,16},{9,17},{10,18},{11,19},{4,7},{5,6},{6,5},{7,4},{12,15},{13,... | collective-permute-start | bytes 786440 | tf_op jit(solution)/shard_map/ppermute | solution.py:46
  4.6 1.3 %collective-permute-start.4 = (f32[128,512]{1,0:T(8,128)S(1)}, f32[128,512]{1,0:T(8,128)S(1)}, u32[]{:S(2)}, u32[]{:S(2)}) collective-permute-start(f32[128,512]{1,0:T(8,128)S(1)} %get-tuple-element.35), channel_id=1, source_target_pairs={{8,0},{9,1},{10,2},{11,3}} | collective-permute-start | bytes 786440 | tf_op jit(solution)/shard_map/ppermute | solution.py:44
  5.9 0.7 %collective-permute-start.2 = (f32[128,512]{1,0:T(8,128)S(1)}, f32[128,512]{1,0:T(8,128)S(1)}, u32[]{:S(2)}, u32[]{:S(2)}) collective-permute-start(f32[128,512]{1,0:T(8,128)S(1)} %get-tuple-element.42), channel_id=1, source_target_pairs={{8,24},{9,25},{10,26},{11,27}} | collective-permute-start | bytes 786440 | tf_op jit(solution)/shard_map/ppermute | solution.py:44
  6.6 3.9 %collective-permute-done = f32[128,512]{1,0:T(8,128)S(1)} collective-permute-done((f32[128,512]{1,0:T(8,128)S(1)}, f32[128,512]{1,0:T(8,128)S(1)}, u32[]{:S(2)}, u32[]{:S(2)}) %collective-permute-start) | collective-permute-done | bytes 262176 | tf_op jit(solution)/shard_map/ppermute | solution.py:46
  10.5 1.3 %collective-permute-start.1 = (f32[128,512]{1,0:T(8,128)S(1)}, f32[128,512]{1,0:T(8,128)S(1)}, u32[]{:S(2)}, u32[]{:S(2)}) collective-permute-start(f32[128,512]{1,0:T(8,128)S(1)} %collective-permute-done), channel_id=1, source_target_pairs={{0,16},{1,17},{2,18},{3,19}} | collective-permute-start | bytes 786440 | tf_op jit(solution)/shard_map/ppermute | solution.py:44
  11.8 5.6 %collective-permute-done.4 = f32[128,512]{1,0:T(8,128)S(1)} collective-permute-done((f32[128,512]{1,0:T(8,128)S(1)}, f32[128,512]{1,0:T(8,128)S(1)}, u32[]{:S(2)}, u32[]{:S(2)}) %collective-permute-start.4) | collective-permute-done | bytes 262176 | tf_op jit(solution)/shard_map/ppermute | solution.py:44
  17.8 2.3 %collective-permute-start.6 = (f32[384,512]{1,0:T(8,128)S(1)}, f32[384,512]{1,0:T(8,128)S(1)}, u32[]{:S(2)}, u32[]{:S(2)}) collective-permute-start(f32[384,512]{1,0:T(8,128)S(1)} %maximum_select_fusion), channel_id=1, source_target_pairs={{0,4},{4,0},{8,12},{12,8},{16,20},{20,16},{24,28},{28,24},{1,5},{5... | collective-permute-start | bytes 2359304 | tf_op jit(solution)/shard_map/ppermute | solution.py:104
  21.0 1.1 %collective-permute-done.6 = f32[384,512]{1,0:T(8,128)S(1)} collective-permute-done((f32[384,512]{1,0:T(8,128)S(1)}, f32[384,512]{1,0:T(8,128)S(1)}, u32[]{:S(2)}, u32[]{:S(2)}) %collective-permute-start.6) | collective-permute-done | bytes 786464 | tf_op jit(solution)/shard_map/ppermute | solution.py:104
  24.4 1.4 %collective-permute-start.7 = (f32[512,128]{0,1:T(8,128)S(1)}, f32[512,128]{0,1:T(8,128)S(1)}, u32[]{:S(2)}, u32[]{:S(2)}) collective-permute-start(f32[512,128]{0,1:T(8,128)S(1)} %fusion.2), channel_id=1, source_target_pairs={{0,1},{1,3},{2,0},{3,2},{4,5},{5,7},{6,4},{7,6},{8,9},{9,11},{10,8... | collective-permute-start | bytes 786440 | tf_op jit(solution)/shard_map/ppermute | solution.py:119
  26.8 4.6 %collective-permute-start.9 = (f32[512,128]{0,1:T(8,128)S(1)}, f32[512,128]{0,1:T(8,128)S(1)}, u32[]{:S(2)}, u32[]{:S(2)}) collective-permute-start(f32[512,128]{0,1:T(8,128)S(1)} %fusion.3), channel_id=1, source_target_pairs={{0,3},{3,0},{4,7},{7,4},{8,11},{11,8},{12,15},{15,12},{16,19},{19,... | collective-permute-start | bytes 786440 | tf_op jit(solution)/shard_map/ppermute | solution.py:123
  31.5 2.4 %collective-permute-done.7 = f32[512,128]{0,1:T(8,128)S(1)} collective-permute-done((f32[512,128]{0,1:T(8,128)S(1)}, f32[512,128]{0,1:T(8,128)S(1)}, u32[]{:S(2)}, u32[]{:S(2)}) %collective-permute-start.7) | collective-permute-done | bytes 262176 | tf_op jit(solution)/shard_map/ppermute | solution.py:119
  33.9 0.6 fusion.35
  34.5 0.7 %collective-permute-start.10 = (f32[512,128]{0,1:T(8,128)S(1)}, f32[512,128]{0,1:T(8,128)S(1)}, u32[]{:S(2)}, u32[]{:S(2)}) collective-permute-start(f32[512,128]{0,1:T(8,128)S(1)} %add.89), channel_id=1, source_target_pairs={{1,2},{2,1},{5,6},{6,5},{9,10},{10,9},{13,14},{14,13},{17,18},{18,... | collective-permute-start | bytes 786440 | tf_op jit(solution)/shard_map/ppermute | solution.py:127
  35.2 0.4 fusion
  35.7 5.6 %collective-permute-done.9 = f32[512,128]{0,1:T(8,128)S(1)} collective-permute-done((f32[512,128]{0,1:T(8,128)S(1)}, f32[512,128]{0,1:T(8,128)S(1)}, u32[]{:S(2)}, u32[]{:S(2)}) %collective-permute-start.9) | collective-permute-done | bytes 262176 | tf_op jit(solution)/shard_map/ppermute | solution.py:123
  41.3 3.9 %collective-permute-done.8 = f32[512,128]{0,1:T(8,128)S(1)} collective-permute-done((f32[512,128]{0,1:T(8,128)S(1)}, f32[512,128]{0,1:T(8,128)S(1)}, u32[]{:S(2)}, u32[]{:S(2)}) %collective-permute-start.8) | collective-permute-done | bytes 262176 | tf_op jit(solution)/shard_map/ppermute | solution.py:124
  45.5 0.7 %pad_maximum_fusion.2 = f32[32,8,128]{2,1,0:T(8,128)} fusion(f32[32,4,128]{2,1,0:T(4,128)S(1)} %broadcast_in_dim.15, f32[32,4,128]{2,1,0:T(4,128)S(1)} %reshape.36), kind=kLoop, calls=%fused_computation.29 | loop fusion | flops 32768 | bytes 262144 | tf_op jit(solution)/shard_map/concatenate | solution.py:135
  46.2 4.0 %all-to-all-start = ((f32[32,8,128]{2,1,0:T(8,128)}), f32[32,8,128]{2,1,0:T(8,128)S(1)}, u32[]{:S(2)}, u32[]{:S(2)}) async-start(f32[32,8,128]{2,1,0:T(8,128)} %pad_maximum_fusion.2), calls=%async_computation | async-start | bytes 262144 | tf_op jit(solution)/shard_map/all_to_all | solution.py:142
  50.3 0.8 %copy.7 = f32[512,128]{1,0:T(8,128)} copy(f32[512,128]{0,1:T(8,128)S(1)} %get-tuple-element.33) | data formatting | bytes 524288
  51.1 7.4 %all-to-all-done = f32[32,8,128]{2,1,0:T(8,128)S(1)} async-done(((f32[32,8,128]{2,1,0:T(8,128)}), f32[32,8,128]{2,1,0:T(8,128)S(1)}, u32[]{:S(2)}, u32[]{:S(2)}) %all-to-all-start) | async-done | bytes 131104 | tf_op jit(solution)/shard_map/all_to_all | solution.py:142
  58.5 0.8 %multiply_add_fusion = f32[1,4096]{1,0:T(1,128)} fusion(f32[1,4096]{1,0:T(1,128)S(1)} %bitcast.34), kind=kLoop, calls=%fused_computation.46 | loop fusion | flops 36864 | bytes 32768 | tf_op jit(solution)/shard_map/add | solution.py:77
  (47 shorter events, 5.0 us)
Async XLA Ops:
  0.6 19.7 %copy-start = (f32[512,128]{1,0:T(8,128)S(1)}, f32[512,128]{1,0:T(8,128)}, u32[]{:S(2)}) copy-start(f32[512,128]{1,0:T(8,128)} %param.5) | copy-start | bytes 786436
  0.7 1.1 %copy-start.2 = (f32[128,512]{1,0:T(8,128)S(1)}, f32[128,512]{1,0:T(8,128)}, u32[]{:S(2)}) copy-start(f32[128,512]{1,0:T(8,128)} %param.9) | copy-start | bytes 786436
  1.9 8.6 %collective-permute-start = (f32[128,512]{1,0:T(8,128)S(1)}, f32[128,512]{1,0:T(8,128)S(1)}, u32[]{:S(2)}, u32[]{:S(2)}) collective-permute-start(f32[128,512]{1,0:T(8,128)S(1)} %get-tuple-element.41), channel_id=1, source_target_pairs={{8,0},{9,1},{10,2},{11,3},{4,6},{5,7},{6,4},{7,5},{12,14},{13,15},... | collective-permute-start | bytes 786440 | tf_op jit(solution)/shard_map/ppermute | solution.py:46
  3.2 8.6 %collective-permute-start.5 = (f32[128,512]{1,0:T(8,128)S(1)}, f32[128,512]{1,0:T(8,128)S(1)}, u32[]{:S(2)}, u32[]{:S(2)}) collective-permute-start(f32[128,512]{1,0:T(8,128)S(1)} %get-tuple-element.34), channel_id=1, source_target_pairs={{8,24},{9,25},{10,26},{11,27},{4,5},{5,4},{6,7},{7,6},{12,13},{13,... | collective-permute-start | bytes 786440 | tf_op jit(solution)/shard_map/ppermute | solution.py:46
  3.9 7.9 %collective-permute-start.3 = (f32[128,512]{1,0:T(8,128)S(1)}, f32[128,512]{1,0:T(8,128)S(1)}, u32[]{:S(2)}, u32[]{:S(2)}) collective-permute-start(f32[128,512]{1,0:T(8,128)S(1)} %get-tuple-element.34), channel_id=1, source_target_pairs={{8,16},{9,17},{10,18},{11,19},{4,7},{5,6},{6,5},{7,4},{12,15},{13,... | collective-permute-start | bytes 786440 | tf_op jit(solution)/shard_map/ppermute | solution.py:46
  4.6 12.8 %collective-permute-start.4 = (f32[128,512]{1,0:T(8,128)S(1)}, f32[128,512]{1,0:T(8,128)S(1)}, u32[]{:S(2)}, u32[]{:S(2)}) collective-permute-start(f32[128,512]{1,0:T(8,128)S(1)} %get-tuple-element.35), channel_id=1, source_target_pairs={{8,0},{9,1},{10,2},{11,3}} | collective-permute-start | bytes 786440 | tf_op jit(solution)/shard_map/ppermute | solution.py:44
  5.9 11.6 %collective-permute-start.2 = (f32[128,512]{1,0:T(8,128)S(1)}, f32[128,512]{1,0:T(8,128)S(1)}, u32[]{:S(2)}, u32[]{:S(2)}) collective-permute-start(f32[128,512]{1,0:T(8,128)S(1)} %get-tuple-element.42), channel_id=1, source_target_pairs={{8,24},{9,25},{10,26},{11,27}} | collective-permute-start | bytes 786440 | tf_op jit(solution)/shard_map/ppermute | solution.py:44
  10.5 7.0 %collective-permute-start.1 = (f32[128,512]{1,0:T(8,128)S(1)}, f32[128,512]{1,0:T(8,128)S(1)}, u32[]{:S(2)}, u32[]{:S(2)}) collective-permute-start(f32[128,512]{1,0:T(8,128)S(1)} %collective-permute-done), channel_id=1, source_target_pairs={{0,16},{1,17},{2,18},{3,19}} | collective-permute-start | bytes 786440 | tf_op jit(solution)/shard_map/ppermute | solution.py:44
  17.7 2.5 %copy-start.3 = (f32[256,32]{0,1:T(8,128)S(1)}, f32[256,32]{0,1:T(8,128)}, u32[]{:S(2)}) copy-start(f32[256,32]{0,1:T(8,128)} %param.7) | copy-start | bytes 98308
  17.7 2.5 %copy-start.4 = (f32[128,32]{0,1:T(8,128)S(1)}, f32[128,32]{0,1:T(8,128)}, u32[]{:S(2)}) copy-start(f32[128,32]{0,1:T(8,128)} %param.8) | copy-start | bytes 49156
  17.7 2.5 %copy-start.1 = (f32[512,256]{1,0:T(8,128)S(1)}, f32[512,256]{1,0:T(8,128)}, u32[]{:S(2)}) copy-start(f32[512,256]{1,0:T(8,128)} %param.6) | copy-start | bytes 1572868
  17.8 4.2 %collective-permute-start.6 = (f32[384,512]{1,0:T(8,128)S(1)}, f32[384,512]{1,0:T(8,128)S(1)}, u32[]{:S(2)}, u32[]{:S(2)}) collective-permute-start(f32[384,512]{1,0:T(8,128)S(1)} %maximum_select_fusion), channel_id=1, source_target_pairs={{0,4},{4,0},{8,12},{12,8},{16,20},{20,16},{24,28},{28,24},{1,5},{5... | collective-permute-start | bytes 2359304 | tf_op jit(solution)/shard_map/ppermute | solution.py:104
  24.4 9.5 %collective-permute-start.7 = (f32[512,128]{0,1:T(8,128)S(1)}, f32[512,128]{0,1:T(8,128)S(1)}, u32[]{:S(2)}, u32[]{:S(2)}) collective-permute-start(f32[512,128]{0,1:T(8,128)S(1)} %fusion.2), channel_id=1, source_target_pairs={{0,1},{1,3},{2,0},{3,2},{4,5},{5,7},{6,4},{7,6},{8,9},{9,11},{10,8... | collective-permute-start | bytes 786440 | tf_op jit(solution)/shard_map/ppermute | solution.py:119
  26.8 14.5 %collective-permute-start.9 = (f32[512,128]{0,1:T(8,128)S(1)}, f32[512,128]{0,1:T(8,128)S(1)}, u32[]{:S(2)}, u32[]{:S(2)}) collective-permute-start(f32[512,128]{0,1:T(8,128)S(1)} %fusion.3), channel_id=1, source_target_pairs={{0,3},{3,0},{4,7},{7,4},{8,11},{11,8},{12,15},{15,12},{16,19},{19,... | collective-permute-start | bytes 786440 | tf_op jit(solution)/shard_map/ppermute | solution.py:123
  31.4 13.7 %collective-permute-start.8 = (f32[512,128]{0,1:T(8,128)S(1)}, f32[512,128]{0,1:T(8,128)S(1)}, u32[]{:S(2)}, u32[]{:S(2)}) collective-permute-start(f32[512,128]{0,1:T(8,128)S(1)} %fusion.1), channel_id=1, source_target_pairs={{0,1},{1,0},{2,3},{3,2},{4,5},{5,4},{6,7},{7,6},{8,9},{9,8},{10,11... | collective-permute-start | bytes 786440 | tf_op jit(solution)/shard_map/ppermute | solution.py:124
  34.5 10.7 %collective-permute-start.10 = (f32[512,128]{0,1:T(8,128)S(1)}, f32[512,128]{0,1:T(8,128)S(1)}, u32[]{:S(2)}, u32[]{:S(2)}) collective-permute-start(f32[512,128]{0,1:T(8,128)S(1)} %add.89), channel_id=1, source_target_pairs={{1,2},{2,1},{5,6},{6,5},{9,10},{10,9},{13,14},{14,13},{17,18},{18,... | collective-permute-start | bytes 786440 | tf_op jit(solution)/shard_map/ppermute | solution.py:127
  46.2 12.3 %all-to-all-start = ((f32[32,8,128]{2,1,0:T(8,128)}), f32[32,8,128]{2,1,0:T(8,128)S(1)}, u32[]{:S(2)}, u32[]{:S(2)}) async-start(f32[32,8,128]{2,1,0:T(8,128)} %pad_maximum_fusion.2), calls=%async_computation | async-start | bytes 262144 | tf_op jit(solution)/shard_map/all_to_all | solution.py:142

commit v10 on v9

--- a/solution.py
+++ b/solution.py
@@ -93,7 +93,7 @@
     own_pivot, rows = broadcast(
         factor_prev, source, wide, narrow, [(diag_inverse, shifted(k)) for k in far]
     )
-    rows = dict(zip(far, lax.optimization_barrier(tuple(rows))))
+    rows = dict(zip(far, rows))
 
     draws = lax.optimization_barrier(jnp.concatenate([draws_prev, draws_panel]))
     samples_prev = contract(draws[:depth], factor_prev, 0, 1)

time: 59.6 us -> 59.6 us (level)
  no operation moved by 1% of the time
where the time goes in v10:
time: 59.6 us; the launch traced here: 59.3 us
  waiting for transfers between devices  29.9 us (50%)
  starting transfers between devices  19 us (32%)
  matrix products  4.76 us (8%)
  other arithmetic  2.56 us (4%)
  local copies, waits for them, and re-layouts  2.07 us (3%)
  between operations  1.06 us (2%)
    all_to_all x1, waiting for transfers between devices, per_device(): lax.all_to_all(outgoing, ('narrow', 'wide'), split_axis=0, concat_axis=0,...  7.39 us
    ppermute x3, waiting for transfers between devices, send(): return lax.ppermute(value, ('wide', 'narrow'), pairs)  5.62 us
    ppermute x1, waiting for transfers between devices, per_device(): outer = lax.ppermute(across, 'narrow', [(0, 3), (3, 0)])  5.59 us
    dot_general x14, matrix products, contract(): lax.dot_general(left_side, right_side, (((left_dim,), (right_dim,)), ((),...  4.76 us
    ppermute x1, starting transfers between devices, per_device(): outer = lax.ppermute(across, 'narrow', [(0, 3), (3, 0)])  4.64 us
    all_to_all x1, starting transfers between devices, per_device(): lax.all_to_all(outgoing, ('narrow', 'wide'), split_axis=0, concat_axis=0,...  4.01 us
    ppermute x3, waiting for transfers between devices, send(): lax.ppermute(jnp.where(on_core, value, rider), ('wide', 'narrow'), pairs...  3.91 us
    ppermute x1, waiting for transfers between devices, per_device(): beside = lax.ppermute(beside, 'narrow', [(0, 1), (1, 0), (2, 3), (3, 2)])  3.86 us
  transfers between devices with their start and end apart: 12, of which 7 were waited for; matrix products, arithmetic and copies ran while one was open for 6% of the time, Pallas kernels for 0%

profile of v10, /device:TPU:0, one launch (start us, length us, event | category | flops | bytes accessed | tf_op | source)
XLA Modules:
  0.0 59.3 jit_solution(13532274979395339440)
XLA Ops:
  0.7 1.1 %fusion.29 = (f32[256,256]{1,0:T(8,128)S(1)}, f32[256,256]{1,0:T(8,128)S(1)}) fusion(f32[512,256]{1,0:T(8,128)} %param.6), kind=kLoop, calls=%fused_computation.57 | loop fusion | bytes 1048576 | tf_op jit(solution)/shard_map/split | solution.py:25
  1.9 1.3 %collective-permute-start = (f32[128,512]{1,0:T(8,128)S(1)}, f32[128,512]{1,0:T(8,128)S(1)}, u32[]{:S(2)}, u32[]{:S(2)}) collective-permute-start(f32[128,512]{1,0:T(8,128)S(1)} %get-tuple-element.28), channel_id=1, source_target_pairs={{8,0},{9,1},{10,2},{11,3},{4,6},{5,7},{6,4},{7,5},{12,14},{13,15},... | collective-permute-start | bytes 786440 | tf_op jit(solution)/shard_map/ppermute | solution.py:46
  3.2 0.7 %collective-permute-start.5 = (f32[128,512]{1,0:T(8,128)S(1)}, f32[128,512]{1,0:T(8,128)S(1)}, u32[]{:S(2)}, u32[]{:S(2)}) collective-permute-start(f32[128,512]{1,0:T(8,128)S(1)} %get-tuple-element.35), channel_id=1, source_target_pairs={{8,24},{9,25},{10,26},{11,27},{4,5},{5,4},{6,7},{7,6},{12,13},{13,... | collective-permute-start | bytes 786440 | tf_op jit(solution)/shard_map/ppermute | solution.py:46
  3.9 0.7 %collective-permute-start.3 = (f32[128,512]{1,0:T(8,128)S(1)}, f32[128,512]{1,0:T(8,128)S(1)}, u32[]{:S(2)}, u32[]{:S(2)}) collective-permute-start(f32[128,512]{1,0:T(8,128)S(1)} %get-tuple-element.35), channel_id=1, source_target_pairs={{8,16},{9,17},{10,18},{11,19},{4,7},{5,6},{6,5},{7,4},{12,15},{13,... | collective-permute-start | bytes 786440 | tf_op jit(solution)/shard_map/ppermute | solution.py:46
  4.6 1.3 %collective-permute-start.4 = (f32[128,512]{1,0:T(8,128)S(1)}, f32[128,512]{1,0:T(8,128)S(1)}, u32[]{:S(2)}, u32[]{:S(2)}) collective-permute-start(f32[128,512]{1,0:T(8,128)S(1)} %get-tuple-element.36), channel_id=1, source_target_pairs={{8,0},{9,1},{10,2},{11,3}} | collective-permute-start | bytes 786440 | tf_op jit(solution)/shard_map/ppermute | solution.py:44
  5.9 0.7 %collective-permute-start.2 = (f32[128,512]{1,0:T(8,128)S(1)}, f32[128,512]{1,0:T(8,128)S(1)}, u32[]{:S(2)}, u32[]{:S(2)}) collective-permute-start(f32[128,512]{1,0:T(8,128)S(1)} %get-tuple-element.29), channel_id=1, source_target_pairs={{8,24},{9,25},{10,26},{11,27}} | collective-permute-start | bytes 786440 | tf_op jit(solution)/shard_map/ppermute | solution.py:44
  6.6 3.9 %collective-permute-done = f32[128,512]{1,0:T(8,128)S(1)} collective-permute-done((f32[128,512]{1,0:T(8,128)S(1)}, f32[128,512]{1,0:T(8,128)S(1)}, u32[]{:S(2)}, u32[]{:S(2)}) %collective-permute-start) | collective-permute-done | bytes 262176 | tf_op jit(solution)/shard_map/ppermute | solution.py:46
  10.5 1.3 %collective-permute-start.1 = (f32[128,512]{1,0:T(8,128)S(1)}, f32[128,512]{1,0:T(8,128)S(1)}, u32[]{:S(2)}, u32[]{:S(2)}) collective-permute-start(f32[128,512]{1,0:T(8,128)S(1)} %collective-permute-done), channel_id=1, source_target_pairs={{0,16},{1,17},{2,18},{3,19}} | collective-permute-start | bytes 786440 | tf_op jit(solution)/shard_map/ppermute | solution.py:44
  11.8 5.6 %collective-permute-done.4 = f32[128,512]{1,0:T(8,128)S(1)} collective-permute-done((f32[128,512]{1,0:T(8,128)S(1)}, f32[128,512]{1,0:T(8,128)S(1)}, u32[]{:S(2)}, u32[]{:S(2)}) %collective-permute-start.4) | collective-permute-done | bytes 262176 | tf_op jit(solution)/shard_map/ppermute | solution.py:44
  17.8 2.3 %collective-permute-start.6 = (f32[384,512]{1,0:T(8,128)S(1)}, f32[384,512]{1,0:T(8,128)S(1)}, u32[]{:S(2)}, u32[]{:S(2)}) collective-permute-start(f32[384,512]{1,0:T(8,128)S(1)} %maximum_select_fusion), channel_id=1, source_target_pairs={{0,4},{4,0},{8,12},{12,8},{16,20},{20,16},{24,28},{28,24},{1,5},{5... | collective-permute-start | bytes 2359304 | tf_op jit(solution)/shard_map/ppermute | solution.py:104
  21.0 1.1 %collective-permute-done.6 = f32[384,512]{1,0:T(8,128)S(1)} collective-permute-done((f32[384,512]{1,0:T(8,128)S(1)}, f32[384,512]{1,0:T(8,128)S(1)}, u32[]{:S(2)}, u32[]{:S(2)}) %collective-permute-start.6) | collective-permute-done | bytes 786464 | tf_op jit(solution)/shard_map/ppermute | solution.py:104
  24.4 1.4 %collective-permute-start.7 = (f32[512,128]{0,1:T(8,128)S(1)}, f32[512,128]{0,1:T(8,128)S(1)}, u32[]{:S(2)}, u32[]{:S(2)}) collective-permute-start(f32[512,128]{0,1:T(8,128)S(1)} %fusion.2), channel_id=1, source_target_pairs={{0,1},{1,3},{2,0},{3,2},{4,5},{5,7},{6,4},{7,6},{8,9},{9,11},{10,8... | collective-permute-start | bytes 786440 | tf_op jit(solution)/shard_map/ppermute | solution.py:119
  26.8 4.6 %collective-permute-start.9 = (f32[512,128]{0,1:T(8,128)S(1)}, f32[512,128]{0,1:T(8,128)S(1)}, u32[]{:S(2)}, u32[]{:S(2)}) collective-permute-start(f32[512,128]{0,1:T(8,128)S(1)} %fusion.3), channel_id=1, source_target_pairs={{0,3},{3,0},{4,7},{7,4},{8,11},{11,8},{12,15},{15,12},{16,19},{19,... | collective-permute-start | bytes 786440 | tf_op jit(solution)/shard_map/ppermute | solution.py:123
  31.5 2.4 %collective-permute-done.7 = f32[512,128]{0,1:T(8,128)S(1)} collective-permute-done((f32[512,128]{0,1:T(8,128)S(1)}, f32[512,128]{0,1:T(8,128)S(1)}, u32[]{:S(2)}, u32[]{:S(2)}) %collective-permute-start.7) | collective-permute-done | bytes 262176 | tf_op jit(solution)/shard_map/ppermute | solution.py:119
  33.9 0.6 fusion.35
  34.5 0.7 %collective-permute-start.10 = (f32[512,128]{0,1:T(8,128)S(1)}, f32[512,128]{0,1:T(8,128)S(1)}, u32[]{:S(2)}, u32[]{:S(2)}) collective-permute-start(f32[512,128]{0,1:T(8,128)S(1)} %add.89), channel_id=1, source_target_pairs={{1,2},{2,1},{5,6},{6,5},{9,10},{10,9},{13,14},{14,13},{17,18},{18,... | collective-permute-start | bytes 786440 | tf_op jit(solution)/shard_map/ppermute | solution.py:127
  35.2 0.4 fusion
  35.7 5.6 %collective-permute-done.9 = f32[512,128]{0,1:T(8,128)S(1)} collective-permute-done((f32[512,128]{0,1:T(8,128)S(1)}, f32[512,128]{0,1:T(8,128)S(1)}, u32[]{:S(2)}, u32[]{:S(2)}) %collective-permute-start.9) | collective-permute-done | bytes 262176 | tf_op jit(solution)/shard_map/ppermute | solution.py:123
  41.3 3.9 %collective-permute-done.8 = f32[512,128]{0,1:T(8,128)S(1)} collective-permute-done((f32[512,128]{0,1:T(8,128)S(1)}, f32[512,128]{0,1:T(8,128)S(1)}, u32[]{:S(2)}, u32[]{:S(2)}) %collective-permute-start.8) | collective-permute-done | bytes 262176 | tf_op jit(solution)/shard_map/ppermute | solution.py:124
  45.6 0.7 %pad_maximum_fusion.2 = f32[32,8,128]{2,1,0:T(8,128)} fusion(f32[32,4,128]{2,1,0:T(4,128)S(1)} %broadcast_in_dim.15, f32[32,4,128]{2,1,0:T(4,128)S(1)} %reshape.36), kind=kLoop, calls=%fused_computation.29 | loop fusion | flops 32768 | bytes 262144 | tf_op jit(solution)/shard_map/concatenate | solution.py:135
  46.2 4.0 %all-to-all-start = ((f32[32,8,128]{2,1,0:T(8,128)}), f32[32,8,128]{2,1,0:T(8,128)S(1)}, u32[]{:S(2)}, u32[]{:S(2)}) async-start(f32[32,8,128]{2,1,0:T(8,128)} %pad_maximum_fusion.2), calls=%async_computation | async-start | bytes 262144 | tf_op jit(solution)/shard_map/all_to_all | solution.py:142
  50.3 0.8 %copy.7 = f32[512,128]{1,0:T(8,128)} copy(f32[512,128]{0,1:T(8,128)S(1)} %get-tuple-element.27) | data formatting | bytes 524288
  51.1 7.4 %all-to-all-done = f32[32,8,128]{2,1,0:T(8,128)S(1)} async-done(((f32[32,8,128]{2,1,0:T(8,128)}), f32[32,8,128]{2,1,0:T(8,128)S(1)}, u32[]{:S(2)}, u32[]{:S(2)}) %all-to-all-start) | async-done | bytes 131104 | tf_op jit(solution)/shard_map/all_to_all | solution.py:142
  58.5 0.8 %multiply_add_fusion = f32[1,4096]{1,0:T(1,128)} fusion(f32[1,4096]{1,0:T(1,128)S(1)} %bitcast.34), kind=kLoop, calls=%fused_computation.46 | loop fusion | flops 36864 | bytes 32768 | tf_op jit(solution)/shard_map/add | solution.py:77
  (47 shorter events, 5.0 us)
Async XLA Ops:
  0.6 19.7 %copy-start = (f32[512,128]{1,0:T(8,128)S(1)}, f32[512,128]{1,0:T(8,128)}, u32[]{:S(2)}) copy-start(f32[512,128]{1,0:T(8,128)} %param.5) | copy-start | bytes 786436
  0.7 1.1 %copy-start.2 = (f32[128,512]{1,0:T(8,128)S(1)}, f32[128,512]{1,0:T(8,128)}, u32[]{:S(2)}) copy-start(f32[128,512]{1,0:T(8,128)} %param.9) | copy-start | bytes 786436
  1.9 8.6 %collective-permute-start = (f32[128,512]{1,0:T(8,128)S(1)}, f32[128,512]{1,0:T(8,128)S(1)}, u32[]{:S(2)}, u32[]{:S(2)}) collective-permute-start(f32[128,512]{1,0:T(8,128)S(1)} %get-tuple-element.28), channel_id=1, source_target_pairs={{8,0},{9,1},{10,2},{11,3},{4,6},{5,7},{6,4},{7,5},{12,14},{13,15},... | collective-permute-start | bytes 786440 | tf_op jit(solution)/shard_map/ppermute | solution.py:46
  3.2 8.6 %collective-permute-start.5 = (f32[128,512]{1,0:T(8,128)S(1)}, f32[128,512]{1,0:T(8,128)S(1)}, u32[]{:S(2)}, u32[]{:S(2)}) collective-permute-start(f32[128,512]{1,0:T(8,128)S(1)} %get-tuple-element.35), channel_id=1, source_target_pairs={{8,24},{9,25},{10,26},{11,27},{4,5},{5,4},{6,7},{7,6},{12,13},{13,... | collective-permute-start | bytes 786440 | tf_op jit(solution)/shard_map/ppermute | solution.py:46
  3.9 7.9 %collective-permute-start.3 = (f32[128,512]{1,0:T(8,128)S(1)}, f32[128,512]{1,0:T(8,128)S(1)}, u32[]{:S(2)}, u32[]{:S(2)}) collective-permute-start(f32[128,512]{1,0:T(8,128)S(1)} %get-tuple-element.35), channel_id=1, source_target_pairs={{8,16},{9,17},{10,18},{11,19},{4,7},{5,6},{6,5},{7,4},{12,15},{13,... | collective-permute-start | bytes 786440 | tf_op jit(solution)/shard_map/ppermute | solution.py:46
  4.6 12.8 %collective-permute-start.4 = (f32[128,512]{1,0:T(8,128)S(1)}, f32[128,512]{1,0:T(8,128)S(1)}, u32[]{:S(2)}, u32[]{:S(2)}) collective-permute-start(f32[128,512]{1,0:T(8,128)S(1)} %get-tuple-element.36), channel_id=1, source_target_pairs={{8,0},{9,1},{10,2},{11,3}} | collective-permute-start | bytes 786440 | tf_op jit(solution)/shard_map/ppermute | solution.py:44
  5.9 11.6 %collective-permute-start.2 = (f32[128,512]{1,0:T(8,128)S(1)}, f32[128,512]{1,0:T(8,128)S(1)}, u32[]{:S(2)}, u32[]{:S(2)}) collective-permute-start(f32[128,512]{1,0:T(8,128)S(1)} %get-tuple-element.29), channel_id=1, source_target_pairs={{8,24},{9,25},{10,26},{11,27}} | collective-permute-start | bytes 786440 | tf_op jit(solution)/shard_map/ppermute | solution.py:44
  10.5 7.0 %collective-permute-start.1 = (f32[128,512]{1,0:T(8,128)S(1)}, f32[128,512]{1,0:T(8,128)S(1)}, u32[]{:S(2)}, u32[]{:S(2)}) collective-permute-start(f32[128,512]{1,0:T(8,128)S(1)} %collective-permute-done), channel_id=1, source_target_pairs={{0,16},{1,17},{2,18},{3,19}} | collective-permute-start | bytes 786440 | tf_op jit(solution)/shard_map/ppermute | solution.py:44
  17.7 2.5 %copy-start.3 = (f32[256,32]{0,1:T(8,128)S(1)}, f32[256,32]{0,1:T(8,128)}, u32[]{:S(2)}) copy-start(f32[256,32]{0,1:T(8,128)} %param.7) | copy-start | bytes 98308
  17.7 2.5 %copy-start.4 = (f32[128,32]{0,1:T(8,128)S(1)}, f32[128,32]{0,1:T(8,128)}, u32[]{:S(2)}) copy-start(f32[128,32]{0,1:T(8,128)} %param.8) | copy-start | bytes 49156
  17.7 2.5 %copy-start.1 = (f32[512,256]{1,0:T(8,128)S(1)}, f32[512,256]{1,0:T(8,128)}, u32[]{:S(2)}) copy-start(f32[512,256]{1,0:T(8,128)} %param.6) | copy-start | bytes 1572868
  17.8 4.2 %collective-permute-start.6 = (f32[384,512]{1,0:T(8,128)S(1)}, f32[384,512]{1,0:T(8,128)S(1)}, u32[]{:S(2)}, u32[]{:S(2)}) collective-permute-start(f32[384,512]{1,0:T(8,128)S(1)} %maximum_select_fusion), channel_id=1, source_target_pairs={{0,4},{4,0},{8,12},{12,8},{16,20},{20,16},{24,28},{28,24},{1,5},{5... | collective-permute-start | bytes 2359304 | tf_op jit(solution)/shard_map/ppermute | solution.py:104
  24.4 9.5 %collective-permute-start.7 = (f32[512,128]{0,1:T(8,128)S(1)}, f32[512,128]{0,1:T(8,128)S(1)}, u32[]{:S(2)}, u32[]{:S(2)}) collective-permute-start(f32[512,128]{0,1:T(8,128)S(1)} %fusion.2), channel_id=1, source_target_pairs={{0,1},{1,3},{2,0},{3,2},{4,5},{5,7},{6,4},{7,6},{8,9},{9,11},{10,8... | collective-permute-start | bytes 786440 | tf_op jit(solution)/shard_map/ppermute | solution.py:119
  26.8 14.5 %collective-permute-start.9 = (f32[512,128]{0,1:T(8,128)S(1)}, f32[512,128]{0,1:T(8,128)S(1)}, u32[]{:S(2)}, u32[]{:S(2)}) collective-permute-start(f32[512,128]{0,1:T(8,128)S(1)} %fusion.3), channel_id=1, source_target_pairs={{0,3},{3,0},{4,7},{7,4},{8,11},{11,8},{12,15},{15,12},{16,19},{19,... | collective-permute-start | bytes 786440 | tf_op jit(solution)/shard_map/ppermute | solution.py:123
  31.4 13.7 %collective-permute-start.8 = (f32[512,128]{0,1:T(8,128)S(1)}, f32[512,128]{0,1:T(8,128)S(1)}, u32[]{:S(2)}, u32[]{:S(2)}) collective-permute-start(f32[512,128]{0,1:T(8,128)S(1)} %fusion.1), channel_id=1, source_target_pairs={{0,1},{1,0},{2,3},{3,2},{4,5},{5,4},{6,7},{7,6},{8,9},{9,8},{10,11... | collective-permute-start | bytes 786440 | tf_op jit(solution)/shard_map/ppermute | solution.py:124
  34.5 10.7 %collective-permute-start.10 = (f32[512,128]{0,1:T(8,128)S(1)}, f32[512,128]{0,1:T(8,128)S(1)}, u32[]{:S(2)}, u32[]{:S(2)}) collective-permute-start(f32[512,128]{0,1:T(8,128)S(1)} %add.89), channel_id=1, source_target_pairs={{1,2},{2,1},{5,6},{6,5},{9,10},{10,9},{13,14},{14,13},{17,18},{18,... | collective-permute-start | bytes 786440 | tf_op jit(solution)/shard_map/ppermute | solution.py:127
  46.2 12.2 %all-to-all-start = ((f32[32,8,128]{2,1,0:T(8,128)}), f32[32,8,128]{2,1,0:T(8,128)S(1)}, u32[]{:S(2)}, u32[]{:S(2)}) async-start(f32[32,8,128]{2,1,0:T(8,128)} %pad_maximum_fusion.2), calls=%async_computation | async-start | bytes 262144 | tf_op jit(solution)/shard_map/all_to_all | solution.py:142
